TPU v7x, 256 devices: a whole 4x4x8 slice. The times are simulated.
256 devices in a mesh: slab: 32 (over z, x), blk: 8 (over y, core).
Axes of the slice: x: 4, y: 4, z: 8, core: 2. Of those that a mesh axis runs over, the one named last changes fastest.
Arguments:
- columns: float32 [65536, 4096], P('slab', 'blk'), may hold values from -40 to 40
- movers: int32 [2, 8], P(None, 'blk'), may hold values 0 or 1
Outputs:
- rotated: float32 [65536, 4096], P('slab', 'blk')
All inputs are finite; a program needn't handle non-finite values. No bound on the sum of `movers` on one device may be relied on, other than what follows from the above.
Results may differ from a plain program's by a relative error of at most 0.00016.
Values sent between devices are 32-bit elements; how exact they have to be, the bound alone decides.
No kernel may reach another device: no remote copies, remote signals or barrier semaphores. Data moves between devices by JAX's collectives and lax.ppermute only.
A program may use at most 64 MiB of HBM per device.

v0:
```python
import jax
import jax.numpy as jnp
from jax import lax
from jax.sharding import PartitionSpec as P

ROUNDS = 2
NS_STEPS = 12


epsilon = 1e-06


def passed_along(value, axis, steps):
    count = lax.axis_size(axis)
    pairs = [(source, (source + steps) % count) for source in range(count)]
    return lax.ppermute(value, axis, pairs)


def skew_rows(gram_rows, col_norms, half):
    nrows = gram_rows.shape[0]
    width = gram_rows.shape[1]
    row_ids = jnp.arange(nrows, dtype=jnp.int32)
    col_ids = jnp.arange(width, dtype=jnp.int32)
    diff = col_norms[:, None] - col_norms[None, :]
    total = col_norms[:, None] + col_norms[None, :]
    cross = (row_ids[:, None] < half) != (col_ids[None, :] < half)
    value = -gram_rows * diff / (diff * diff + 0.25 * total * total + epsilon)
    return jnp.where(cross, value, jnp.float32(0.0))


def start_rows(skew_part, skew_total):
    nrows, width = skew_part.shape
    row_ids = jnp.arange(nrows, dtype=jnp.int32)
    col_ids = jnp.arange(width, dtype=jnp.int32)
    identity = (row_ids[:, None] == col_ids[None, :]).astype(jnp.float32)
    return (identity + skew_part) / (4.0 * jnp.sqrt(width + skew_total))


def inner_rows(left, right):
    return lax.dot_general(
        left,
        right,
        (((0,), (0,)), ((), ())),
        precision=lax.Precision.HIGHEST,
        preferred_element_type=jnp.float32,
    )


def outer_rows(left, right):
    return lax.dot_general(
        left,
        right,
        (((1,), (1,)), ((), ())),
        precision=lax.Precision.HIGHEST,
        preferred_element_type=jnp.float32,
    )


def matmul_high(left, right):
    return jnp.dot(left, right, precision=lax.Precision.HIGHEST, preferred_element_type=jnp.float32)


def gather_iterate(iterate_rows):
    return lax.all_gather(iterate_rows, "slab", axis=0, tiled=True)


def local(columns, movers):
    pair_width = columns.shape[1]
    half = pair_width // 2
    share = pair_width // lax.axis_size("slab")
    first_row = lax.axis_index("slab") * share
    current = columns
    for round_index in range(ROUNDS):
        full_start = None
        gram_matrix = lax.psum(inner_rows(current, current), "slab")
        col_norms = jnp.diagonal(gram_matrix)
        skew_part = skew_rows(gram_matrix, col_norms, half)
        full_start = start_rows(skew_part, jnp.sum(skew_part * skew_part))
        iterate_rows = lax.dynamic_slice_in_dim(full_start, first_row, share, 0)
        iterate_full = full_start

        def newton_split(step_index, carry):
            rows_now, full_now = carry
            products = outer_rows(rows_now, full_now)
            rows_next = 1.5 * rows_now - 0.5 * matmul_high(products, full_now)
            return (rows_next, gather_iterate(rows_next))

        iterate_rows, iterate_full = lax.fori_loop(
            0, NS_STEPS, newton_split, (iterate_rows, iterate_full)
        )
        rotated_pair = matmul_high(current, iterate_full)
        first = rotated_pair[:, :half]
        second = rotated_pair[:, half:]
        flag = movers[round_index, 0] == 1
        moving = jnp.where(flag, first, second)
        staying = jnp.where(flag, second, first)
        arrived = passed_along(moving, "blk", 1)
        current = jnp.concatenate([staying, arrived], axis=1)
    return current


def solution(mesh):
    placed = (P("slab", "blk"), P(None, "blk"))
    return jax.shard_map(
        local, mesh=mesh, in_specs=placed, out_specs=P("slab", "blk"), check_vma=False
    )
```

profile of v0, /device:TPU:1, one launch (start us, length us, event | category | flops | bytes accessed | tf_op | source)
XLA Modules:
  0.0 2333.4 jit_solution(7255707491854763999)
XLA Ops:
  6.5 11.2 fusion.17
  19.1 147.4 %all-reduce.3.cloned.1.call-done = f32[512,512]{1,0:T(8,128)} async-done(((f32[512,512]{1,0:T(8,128)}), f32[512,512]{1,0:T(8,128)}) %all-reduce.3.cloned.1.call-update) | async-done | bytes 1048592 | tf_op jit(solution)/shard_map/psum | solution.py:75
  166.5 8.8 gather_fusion
  175.3 2.6 multiply_reduce_fusion.1
  181.1 943.9 %while.24 = (s32[]{:T(128)}, f32[16,512]{1,0:T(8,128)}, f32[512,512]{1,0:T(8,128)}, s32[]{:T(128)}) while((s32[]{:T(128)}, f32[16,512]{1,0:T(8,128)}, f32[512,512]{1,0:T(8,128)}, s32[]{:T(128)}) %tuple.36), condition=%wide.region_3.4_spmd, body=%wide.region_2.3_spmd.sunk | while | flops 100687872 | bytes 5505117 | solution.py:88
  183.3 2.5 fusion.48
  185.8 73.9 %all-gather.3.cloned.1.call-done = f32[512,512]{1,0:T(8,128)} async-done(((f32[16,512]{1,0:T(8,128)}), f32[512,512]{1,0:T(8,128)}) %all-gather.3.cloned.1.call-update) | async-done | bytes 1048592 | tf_op jit(solution)/shard_map/while/body/eval_jaxpr/all_gather | solution.py:64
  261.9 2.5 fusion.48
  264.4 74.0 %all-gather.3.cloned.1.call-done = f32[512,512]{1,0:T(8,128)} async-done(((f32[16,512]{1,0:T(8,128)}), f32[512,512]{1,0:T(8,128)}) %all-gather.3.cloned.1.call-update) | async-done | bytes 1048592 | tf_op jit(solution)/shard_map/while/body/eval_jaxpr/all_gather | solution.py:64
  340.5 2.5 fusion.48
  343.0 74.0 %all-gather.3.cloned.1.call-done = f32[512,512]{1,0:T(8,128)} async-done(((f32[16,512]{1,0:T(8,128)}), f32[512,512]{1,0:T(8,128)}) %all-gather.3.cloned.1.call-update) | async-done | bytes 1048592 | tf_op jit(solution)/shard_map/while/body/eval_jaxpr/all_gather | solution.py:64
  419.2 2.5 fusion.48
  421.7 74.0 %all-gather.3.cloned.1.call-done = f32[512,512]{1,0:T(8,128)} async-done(((f32[16,512]{1,0:T(8,128)}), f32[512,512]{1,0:T(8,128)}) %all-gather.3.cloned.1.call-update) | async-done | bytes 1048592 | tf_op jit(solution)/shard_map/while/body/eval_jaxpr/all_gather | solution.py:64
  497.8 2.5 fusion.48
  500.3 74.0 %all-gather.3.cloned.1.call-done = f32[512,512]{1,0:T(8,128)} async-done(((f32[16,512]{1,0:T(8,128)}), f32[512,512]{1,0:T(8,128)}) %all-gather.3.cloned.1.call-update) | async-done | bytes 1048592 | tf_op jit(solution)/shard_map/while/body/eval_jaxpr/all_gather | solution.py:64
  576.5 2.5 fusion.48
  579.0 74.0 %all-gather.3.cloned.1.call-done = f32[512,512]{1,0:T(8,128)} async-done(((f32[16,512]{1,0:T(8,128)}), f32[512,512]{1,0:T(8,128)}) %all-gather.3.cloned.1.call-update) | async-done | bytes 1048592 | tf_op jit(solution)/shard_map/while/body/eval_jaxpr/all_gather | solution.py:64
  655.2 2.5 fusion.48
  657.7 74.0 %all-gather.3.cloned.1.call-done = f32[512,512]{1,0:T(8,128)} async-done(((f32[16,512]{1,0:T(8,128)}), f32[512,512]{1,0:T(8,128)}) %all-gather.3.cloned.1.call-update) | async-done | bytes 1048592 | tf_op jit(solution)/shard_map/while/body/eval_jaxpr/all_gather | solution.py:64
  736.3 74.0 %all-gather.3.cloned.1.call-done = f32[512,512]{1,0:T(8,128)} async-done(((f32[16,512]{1,0:T(8,128)}), f32[512,512]{1,0:T(8,128)}) %all-gather.3.cloned.1.call-update) | async-done | bytes 1048592 | tf_op jit(solution)/shard_map/while/body/eval_jaxpr/all_gather | solution.py:64
  815.0 74.0 %all-gather.3.cloned.1.call-done = f32[512,512]{1,0:T(8,128)} async-done(((f32[16,512]{1,0:T(8,128)}), f32[512,512]{1,0:T(8,128)}) %all-gather.3.cloned.1.call-update) | async-done | bytes 1048592 | tf_op jit(solution)/shard_map/while/body/eval_jaxpr/all_gather | solution.py:64
  893.6 74.0 %all-gather.3.cloned.1.call-done = f32[512,512]{1,0:T(8,128)} async-done(((f32[16,512]{1,0:T(8,128)}), f32[512,512]{1,0:T(8,128)}) %all-gather.3.cloned.1.call-update) | async-done | bytes 1048592 | tf_op jit(solution)/shard_map/while/body/eval_jaxpr/all_gather | solution.py:64
  972.3 74.0 %all-gather.3.cloned.1.call-done = f32[512,512]{1,0:T(8,128)} async-done(((f32[16,512]{1,0:T(8,128)}), f32[512,512]{1,0:T(8,128)}) %all-gather.3.cloned.1.call-update) | async-done | bytes 1048592 | tf_op jit(solution)/shard_map/while/body/eval_jaxpr/all_gather | solution.py:64
  1051.0 74.0 %all-gather.3.cloned.1.call-done = f32[512,512]{1,0:T(8,128)} async-done(((f32[16,512]{1,0:T(8,128)}), f32[512,512]{1,0:T(8,128)}) %all-gather.3.cloned.1.call-update) | async-done | bytes 1048592 | tf_op jit(solution)/shard_map/while/body/eval_jaxpr/all_gather | solution.py:64
  1124.9 15.5 convolution_bitcast_fusion
  1141.0 6.1 collective-permute-start
  1147.1 23.0 collective-permute-done
  1171.4 8.0 fusion.3
  1180.0 142.6 %all-reduce.5.cloned.1.call-done = f32[512,512]{1,0:T(8,128)} async-done(((f32[512,512]{1,0:T(8,128)}), f32[512,512]{1,0:T(8,128)}) %all-reduce.5.cloned.1.call-update) | async-done | bytes 1048592 | tf_op jit(solution)/shard_map/psum | solution.py:75
  1322.7 8.8 gather_fusion.1
  1331.5 2.6 multiply_reduce_fusion
  1337.1 943.7 %while.25 = (s32[]{:T(128)}, f32[16,512]{1,0:T(8,128)}, f32[512,512]{1,0:T(8,128)}, s32[]{:T(128)}) while((s32[]{:T(128)}, f32[16,512]{1,0:T(8,128)}, f32[512,512]{1,0:T(8,128)}, s32[]{:T(128)}) %tuple.39), condition=%wide.region_7.8_spmd, body=%wide.region_6.7_spmd.sunk | while | flops 100687872 | bytes 5505117 | solution.py:88
  1341.8 73.9 %all-gather.5.cloned.1.call-done = f32[512,512]{1,0:T(8,128)} async-done(((f32[16,512]{1,0:T(8,128)}), f32[512,512]{1,0:T(8,128)}) %all-gather.5.cloned.1.call-update) | async-done | bytes 1048592 | tf_op jit(solution)/shard_map/while/body/eval_jaxpr/all_gather | solution.py:64
  1420.4 74.0 %all-gather.5.cloned.1.call-done = f32[512,512]{1,0:T(8,128)} async-done(((f32[16,512]{1,0:T(8,128)}), f32[512,512]{1,0:T(8,128)}) %all-gather.5.cloned.1.call-update) | async-done | bytes 1048592 | tf_op jit(solution)/shard_map/while/body/eval_jaxpr/all_gather | solution.py:64
  1499.0 74.0 %all-gather.5.cloned.1.call-done = f32[512,512]{1,0:T(8,128)} async-done(((f32[16,512]{1,0:T(8,128)}), f32[512,512]{1,0:T(8,128)}) %all-gather.5.cloned.1.call-update) | async-done | bytes 1048592 | tf_op jit(solution)/shard_map/while/body/eval_jaxpr/all_gather | solution.py:64
  1577.7 74.0 %all-gather.5.cloned.1.call-done = f32[512,512]{1,0:T(8,128)} async-done(((f32[16,512]{1,0:T(8,128)}), f32[512,512]{1,0:T(8,128)}) %all-gather.5.cloned.1.call-update) | async-done | bytes 1048592 | tf_op jit(solution)/shard_map/while/body/eval_jaxpr/all_gather | solution.py:64
  1656.3 74.0 %all-gather.5.cloned.1.call-done = f32[512,512]{1,0:T(8,128)} async-done(((f32[16,512]{1,0:T(8,128)}), f32[512,512]{1,0:T(8,128)}) %all-gather.5.cloned.1.call-update) | async-done | bytes 1048592 | tf_op jit(solution)/shard_map/while/body/eval_jaxpr/all_gather | solution.py:64
  1735.0 74.0 %all-gather.5.cloned.1.call-done = f32[512,512]{1,0:T(8,128)} async-done(((f32[16,512]{1,0:T(8,128)}), f32[512,512]{1,0:T(8,128)}) %all-gather.5.cloned.1.call-update) | async-done | bytes 1048592 | tf_op jit(solution)/shard_map/while/body/eval_jaxpr/all_gather | solution.py:64
  1813.6 74.0 %all-gather.5.cloned.1.call-done = f32[512,512]{1,0:T(8,128)} async-done(((f32[16,512]{1,0:T(8,128)}), f32[512,512]{1,0:T(8,128)}) %all-gather.5.cloned.1.call-update) | async-done | bytes 1048592 | tf_op jit(solution)/shard_map/while/body/eval_jaxpr/all_gather | solution.py:64
  1892.3 74.0 %all-gather.5.cloned.1.call-done = f32[512,512]{1,0:T(8,128)} async-done(((f32[16,512]{1,0:T(8,128)}), f32[512,512]{1,0:T(8,128)}) %all-gather.5.cloned.1.call-update) | async-done | bytes 1048592 | tf_op jit(solution)/shard_map/while/body/eval_jaxpr/all_gather | solution.py:64
  1970.9 74.0 %all-gather.5.cloned.1.call-done = f32[512,512]{1,0:T(8,128)} async-done(((f32[16,512]{1,0:T(8,128)}), f32[512,512]{1,0:T(8,128)}) %all-gather.5.cloned.1.call-update) | async-done | bytes 1048592 | tf_op jit(solution)/shard_map/while/body/eval_jaxpr/all_gather | solution.py:64
  2049.5 74.0 %all-gather.5.cloned.1.call-done = f32[512,512]{1,0:T(8,128)} async-done(((f32[16,512]{1,0:T(8,128)}), f32[512,512]{1,0:T(8,128)}) %all-gather.5.cloned.1.call-update) | async-done | bytes 1048592 | tf_op jit(solution)/shard_map/while/body/eval_jaxpr/all_gather | solution.py:64
  2128.2 74.0 %all-gather.5.cloned.1.call-done = f32[512,512]{1,0:T(8,128)} async-done(((f32[16,512]{1,0:T(8,128)}), f32[512,512]{1,0:T(8,128)}) %all-gather.5.cloned.1.call-update) | async-done | bytes 1048592 | tf_op jit(solution)/shard_map/while/body/eval_jaxpr/all_gather | solution.py:64
  2206.8 74.0 %all-gather.5.cloned.1.call-done = f32[512,512]{1,0:T(8,128)} async-done(((f32[16,512]{1,0:T(8,128)}), f32[512,512]{1,0:T(8,128)}) %all-gather.5.cloned.1.call-update) | async-done | bytes 1048592 | tf_op jit(solution)/shard_map/while/body/eval_jaxpr/all_gather | solution.py:64
  2280.8 8.8 fusion.2
  2290.0 6.1 collective-permute-start.1
  2296.1 23.0 collective-permute-done.1
  2321.5 5.3 copy.4
  (107 shorter events, 105.2 us)
Async XLA Ops:
  6.5 11.2 copy-start.1
  6.5 160.0 %all-reduce.3.cloned.1.call-start = ((), (), s32[]{:S(2)}) async-start(), calls=%async_computation | async-start | bytes 2097152 | tf_op jit(solution)/shard_map/psum | solution.py:75
  181.1 78.6 %all-gather.3.cloned.1.call-start = ((), (), s32[]{:S(2)}) async-start(), calls=%async_computation.2 | async-start | bytes 1081344 | tf_op jit(solution)/shard_map/while/body/eval_jaxpr/all_gather | solution.py:64
  259.7 78.7 %all-gather.3.cloned.1.call-start = ((), (), s32[]{:S(2)}) async-start(), calls=%async_computation.2 | async-start | bytes 1081344 | tf_op jit(solution)/shard_map/while/body/eval_jaxpr/all_gather | solution.py:64
  338.3 78.7 %all-gather.3.cloned.1.call-start = ((), (), s32[]{:S(2)}) async-start(), calls=%async_computation.2 | async-start | bytes 1081344 | tf_op jit(solution)/shard_map/while/body/eval_jaxpr/all_gather | solution.py:64
  417.0 78.7 %all-gather.3.cloned.1.call-start = ((), (), s32[]{:S(2)}) async-start(), calls=%async_computation.2 | async-start | bytes 1081344 | tf_op jit(solution)/shard_map/while/body/eval_jaxpr/all_gather | solution.py:64
  495.6 78.7 %all-gather.3.cloned.1.call-start = ((), (), s32[]{:S(2)}) async-start(), calls=%async_computation.2 | async-start | bytes 1081344 | tf_op jit(solution)/shard_map/while/body/eval_jaxpr/all_gather | solution.py:64
  574.3 78.7 %all-gather.3.cloned.1.call-start = ((), (), s32[]{:S(2)}) async-start(), calls=%async_computation.2 | async-start | bytes 1081344 | tf_op jit(solution)/shard_map/while/body/eval_jaxpr/all_gather | solution.py:64
  653.0 78.7 %all-gather.3.cloned.1.call-start = ((), (), s32[]{:S(2)}) async-start(), calls=%async_computation.2 | async-start | bytes 1081344 | tf_op jit(solution)/shard_map/while/body/eval_jaxpr/all_gather | solution.py:64
  731.6 78.7 %all-gather.3.cloned.1.call-start = ((), (), s32[]{:S(2)}) async-start(), calls=%async_computation.2 | async-start | bytes 1081344 | tf_op jit(solution)/shard_map/while/body/eval_jaxpr/all_gather | solution.py:64
  810.3 78.7 %all-gather.3.cloned.1.call-start = ((), (), s32[]{:S(2)}) async-start(), calls=%async_computation.2 | async-start | bytes 1081344 | tf_op jit(solution)/shard_map/while/body/eval_jaxpr/all_gather | solution.py:64
  888.9 78.7 %all-gather.3.cloned.1.call-start = ((), (), s32[]{:S(2)}) async-start(), calls=%async_computation.2 | async-start | bytes 1081344 | tf_op jit(solution)/shard_map/while/body/eval_jaxpr/all_gather | solution.py:64
  967.6 78.7 %all-gather.3.cloned.1.call-start = ((), (), s32[]{:S(2)}) async-start(), calls=%async_computation.2 | async-start | bytes 1081344 | tf_op jit(solution)/shard_map/while/body/eval_jaxpr/all_gather | solution.py:64
  1046.3 78.7 %all-gather.3.cloned.1.call-start = ((), (), s32[]{:S(2)}) async-start(), calls=%async_computation.2 | async-start | bytes 1081344 | tf_op jit(solution)/shard_map/while/body/eval_jaxpr/all_gather | solution.py:64
  1124.9 197.8 %all-reduce.5.cloned.1.call-start = ((), (), s32[]{:S(2)}) async-start(), calls=%async_computation.1 | async-start | bytes 2097152 | tf_op jit(solution)/shard_map/psum | solution.py:75
  1141.0 29.1 %collective-permute-start = (f32[2048,256]{0,1:T(8,128)S(1)}, f32[2048,256]{0,1:T(8,128)S(1)}, u32[]{:S(2)}, u32[]{:S(2)}) collective-permute-start(f32[2048,256]{0,1:T(8,128)S(1)} %get-tuple-element.60), channel_id=1, source_target_pairs={{0,1},{1,2},{2,3},{3,4},{4,5},{5,6},{6,7},{7,0},{8,9},{9,10},{10,1... | collective-permute-start | bytes 6291464 | tf_op jit(solution)/shard_map/ppermute | solution.py:16
  1170.1 1.3 copy-start
  1337.1 78.6 %all-gather.5.cloned.1.call-start = ((), (), s32[]{:S(2)}) async-start(), calls=%async_computation.3 | async-start | bytes 1081344 | tf_op jit(solution)/shard_map/while/body/eval_jaxpr/all_gather | solution.py:64
  1415.7 78.6 %all-gather.5.cloned.1.call-start = ((), (), s32[]{:S(2)}) async-start(), calls=%async_computation.3 | async-start | bytes 1081344 | tf_op jit(solution)/shard_map/while/body/eval_jaxpr/all_gather | solution.py:64
  1494.3 78.6 %all-gather.5.cloned.1.call-start = ((), (), s32[]{:S(2)}) async-start(), calls=%async_computation.3 | async-start | bytes 1081344 | tf_op jit(solution)/shard_map/while/body/eval_jaxpr/all_gather | solution.py:64
  1573.0 78.6 %all-gather.5.cloned.1.call-start = ((), (), s32[]{:S(2)}) async-start(), calls=%async_computation.3 | async-start | bytes 1081344 | tf_op jit(solution)/shard_map/while/body/eval_jaxpr/all_gather | solution.py:64
  1651.6 78.6 %all-gather.5.cloned.1.call-start = ((), (), s32[]{:S(2)}) async-start(), calls=%async_computation.3 | async-start | bytes 1081344 | tf_op jit(solution)/shard_map/while/body/eval_jaxpr/all_gather | solution.py:64
  1730.3 78.6 %all-gather.5.cloned.1.call-start = ((), (), s32[]{:S(2)}) async-start(), calls=%async_computation.3 | async-start | bytes 1081344 | tf_op jit(solution)/shard_map/while/body/eval_jaxpr/all_gather | solution.py:64
  1808.9 78.6 %all-gather.5.cloned.1.call-start = ((), (), s32[]{:S(2)}) async-start(), calls=%async_computation.3 | async-start | bytes 1081344 | tf_op jit(solution)/shard_map/while/body/eval_jaxpr/all_gather | solution.py:64
  1887.6 78.6 %all-gather.5.cloned.1.call-start = ((), (), s32[]{:S(2)}) async-start(), calls=%async_computation.3 | async-start | bytes 1081344 | tf_op jit(solution)/shard_map/while/body/eval_jaxpr/all_gather | solution.py:64
  1966.2 78.6 %all-gather.5.cloned.1.call-start = ((), (), s32[]{:S(2)}) async-start(), calls=%async_computation.3 | async-start | bytes 1081344 | tf_op jit(solution)/shard_map/while/body/eval_jaxpr/all_gather | solution.py:64
  2044.9 78.6 %all-gather.5.cloned.1.call-start = ((), (), s32[]{:S(2)}) async-start(), calls=%async_computation.3 | async-start | bytes 1081344 | tf_op jit(solution)/shard_map/while/body/eval_jaxpr/all_gather | solution.py:64
  2123.5 78.6 %all-gather.5.cloned.1.call-start = ((), (), s32[]{:S(2)}) async-start(), calls=%async_computation.3 | async-start | bytes 1081344 | tf_op jit(solution)/shard_map/while/body/eval_jaxpr/all_gather | solution.py:64
  2202.2 78.6 %all-gather.5.cloned.1.call-start = ((), (), s32[]{:S(2)}) async-start(), calls=%async_computation.3 | async-start | bytes 1081344 | tf_op jit(solution)/shard_map/while/body/eval_jaxpr/all_gather | solution.py:64
  2290.0 29.1 %collective-permute-start.1 = (f32[2048,256]{0,1:T(8,128)S(1)}, f32[2048,256]{0,1:T(8,128)S(1)}, u32[]{:S(2)}, u32[]{:S(2)}) collective-permute-start(f32[2048,256]{0,1:T(8,128)S(1)} %get-tuple-element.58), channel_id=1, source_target_pairs={{0,1},{1,2},{2,3},{3,4},{4,5},{5,6},{6,7},{7,0},{8,9},{9,10},{10,1... | collective-permute-start | bytes 6291464 | tf_op jit(solution)/shard_map/ppermute | solution.py:16
Sparse Core Ops, SparseCore 0:
  17.9 148.5 all-reduce.2
  185.9 73.7 all-gather.2
  264.5 73.7 all-gather.2
  343.1 73.7 all-gather.2
  421.8 73.7 all-gather.2
  500.5 73.7 all-gather.2
  579.1 73.7 all-gather.2
  657.8 73.7 all-gather.2
  736.4 73.7 all-gather.2
  815.1 73.7 all-gather.2
  893.8 73.7 all-gather.2
  972.4 73.7 all-gather.2
  1051.1 73.7 all-gather.2
  1179.5 143.1 all-reduce.4
  1341.9 73.7 all-gather.4
  1420.5 73.7 all-gather.4
  1499.1 73.7 all-gather.4
  1577.8 73.7 all-gather.4
  1656.4 73.7 all-gather.4
  1735.1 73.7 all-gather.4
  1813.7 73.7 all-gather.4
  1892.4 73.7 all-gather.4
  1971.0 73.7 all-gather.4
  2049.7 73.7 all-gather.4
  2128.3 73.7 all-gather.4
  2207.0 73.7 all-gather.4
where the time goes:
time: 2340 us; the launch traced here: 2330 us
  waiting for transfers between devices  2110 us (90%)
  matrix products  155 us (7%)
  local copies, waits for them, and re-layouts  27.6 us (1%)
    all_gather x24, waiting for transfers between devices, gather_iterate(): return lax.all_gather(iterate_rows, 'slab', axis=0, tiled=True)  1770 us
    psum x2, waiting for transfers between devices, local(): gram_matrix = lax.psum(inner_rows(current, current), 'slab')  290 us
    dot_general x26, matrix products, matmul_high(): jnp.dot(left, right, precision=lax.Precision.HIGHEST, preferred_element_t...  83.6 us
    dot_general x24, matrix products, outer_rows(): lax.dot_general(left, right, (((1,), (1,)), ((), ())), precision=lax.Prec...  52.6 us
  transfers between devices with their start and end apart: 28, of which 28 were waited for; matrix products, arithmetic and copies ran while one was open for 0% of the time, Pallas kernels for 0%

commit v1 on v0

v1 whole, which is shorter than its diff:
```python
import jax
import jax.numpy as jnp
from jax import lax
from jax.experimental import pallas as pl
from jax.experimental.pallas import tpu as pltpu
from jax.sharding import PartitionSpec as P

ROUNDS = 2
HALF = 256
SLABS = 32
CHUNK = 18
VMEM_BYTES = 40 * 2**20
EPS = 1e-6
F32 = jnp.float32
BF16 = jnp.bfloat16
NN = (((1,), (0,)), ((), ()))
NT = (((1,), (1,)), ((), ()))
TN = (((0,), (0,)), ((), ()))


def split(x):
    high = x.astype(BF16)
    low = (x - high.astype(F32)).astype(BF16)
    return high, low


def dot3(left, right, dims):
    def one(a, b):
        return lax.dot_general(a, b, dims, preferred_element_type=F32)
    return one(left[0], right[0]) + (one(left[0], right[1]) + one(left[1], right[0]))


def weight(gap, eye):
    gap_parts = split(gap)
    square = dot3(gap_parts, gap_parts, NN)
    inner = 0.375 * eye + 0.3125 * gap + 0.0625 * square
    return eye + 0.5 * gap + dot3(split(square), split(inner), NN)


def rotation_kernel(flag_ref, packed_ref, stay_ref, move_ref):
    left = [packed_ref[CHUNK * k:CHUNK * k + 8, :] for k in range(SLABS)]
    right = [packed_ref[CHUNK * k + 8:CHUNK * k + 16, :] for k in range(SLABS)]
    cross = jnp.concatenate([jnp.concatenate(left, 0), jnp.concatenate(right, 0)], 1)
    norm_a = jnp.concatenate([packed_ref[16:17, :], packed_ref[17:18, :]], 1)
    norm_m = jnp.concatenate([packed_ref[CHUNK + 16:CHUNK + 17, :], packed_ref[CHUNK + 17:CHUNK + 18, :]], 1)
    rows = lax.broadcasted_iota(jnp.int32, (HALF, HALF), 0)
    cols = lax.broadcasted_iota(jnp.int32, (HALF, HALF), 1)
    eye = (rows == cols).astype(F32)
    norm_a_col = jnp.transpose(jnp.broadcast_to(norm_a, (HALF, HALF)))
    diff = norm_a_col - norm_m
    total = norm_a_col + norm_m
    skew = -cross * diff / (diff * diff + 0.25 * total * total + EPS)
    scale = 1.0 / (4.0 * jnp.sqrt(2.0 * HALF + 2.0 * jnp.sum(skew * skew, keepdims=True)))
    start = scale * skew
    parts = split(start)
    s2 = scale * scale
    w1 = weight(eye - (s2 * eye + dot3(parts, parts, NT)), eye)
    w2 = weight(eye - (s2 * eye + dot3(parts, parts, TN)), eye)
    e1, e2 = scale * w1, scale * w2
    o = dot3(split(w1), parts, NN)

    def two_steps(_, carry):
        e1, e2, o = carry
        e1p, e2p, op = split(e1), split(e2), split(o)
        w1 = split(weight(eye - (dot3(e1p, e1p, NN) + dot3(op, op, NT)), eye))
        w2 = split(weight(eye - (dot3(e2p, e2p, NN) + dot3(op, op, TN)), eye))
        return dot3(w1, e1p, NN), dot3(w2, e2p, NN), dot3(w1, op, NN)

    e1, e2, o = lax.fori_loop(0, 5, two_steps, (e1, e2, o))
    minus_ot = -jnp.transpose(o)

    @pl.when(flag_ref[0] == 1)
    def _():
        move_ref[:HALF, :] = e1
        move_ref[HALF:, :] = minus_ot
        stay_ref[:HALF, :] = o
        stay_ref[HALF:, :] = e2

    @pl.when(flag_ref[0] != 1)
    def _():
        stay_ref[:HALF, :] = e1
        stay_ref[HALF:, :] = minus_ot
        move_ref[:HALF, :] = o
        move_ref[HALF:, :] = e2


def rotation(flag, packed):
    out = jax.ShapeDtypeStruct((2 * HALF, HALF), F32)
    return pl.pallas_call(
        rotation_kernel,
        out_shape=(out, out),
        in_specs=[pl.BlockSpec(memory_space=pltpu.SMEM), pl.BlockSpec(memory_space=pltpu.VMEM)],
        out_specs=[pl.BlockSpec(memory_space=pltpu.VMEM)] * 2,
        compiler_params=pltpu.CompilerParams(vmem_limit_bytes=VMEM_BYTES),
        name="rotation",
    )(flag, packed)


def gram_add(a, m, acc_ref, norm_ref):
    acc_ref[...] += dot3(split(a), split(m), TN)
    norm_ref[0:1, :] += jnp.sum(a * a, axis=0, keepdims=True)
    norm_ref[1:2, :] += jnp.sum(m * m, axis=0, keepdims=True)


def gram_pack(acc_ref, norm_ref, packed_ref):
    packed_ref[...] = jnp.zeros_like(packed_ref)
    for k in range(SLABS):
        packed_ref[CHUNK * k:CHUNK * k + 8, :] = acc_ref[8 * k:8 * k + 8, :128]
        packed_ref[CHUNK * k + 8:CHUNK * k + 16, :] = acc_ref[8 * k:8 * k + 8, 128:]
    for i in range(2):
        packed_ref[CHUNK * i + 16:CHUNK * i + 17, :] = norm_ref[i:i + 1, :128]
        packed_ref[CHUNK * i + 17:CHUNK * i + 18, :] = norm_ref[i:i + 1, 128:]


def gram_kernel(a_ref, m_ref, packed_ref, acc_ref, norm_ref):
    step = pl.program_id(0)

    @pl.when(step == 0)
    def _():
        acc_ref[...] = jnp.zeros_like(acc_ref)
        norm_ref[...] = jnp.zeros_like(norm_ref)

    gram_add(a_ref[...], m_ref[...], acc_ref, norm_ref)

    @pl.when(step == pl.num_programs(0) - 1)
    def _():
        gram_pack(acc_ref, norm_ref, packed_ref)


def gram(a, m, m_block, tile=512):
    return pl.pallas_call(
        gram_kernel,
        grid=(a.shape[0] // tile,),
        out_shape=jax.ShapeDtypeStruct((SLABS * CHUNK, 128), F32),
        in_specs=[
            pl.BlockSpec((tile, HALF), lambda i: (i, 0)),
            pl.BlockSpec((tile, HALF), lambda i: (i, m_block)),
        ],
        out_specs=pl.BlockSpec((SLABS * CHUNK, 128), lambda i: (0, 0)),
        scratch_shapes=[pltpu.VMEM((HALF, HALF), F32), pltpu.VMEM((8, HALF), F32)],
        compiler_params=pltpu.CompilerParams(vmem_limit_bytes=VMEM_BYTES),
        name="gram",
    )(a, m)


def rotate_kernel(a_ref, m_ref, q_ref, out_ref):
    out_ref[...] = dot3(split(a_ref[...]), split(q_ref[:HALF, :]), NN) + dot3(
        split(m_ref[...]), split(q_ref[HALF:, :]), NN
    )


def rotate(a, m, m_block, q, tile=512):
    return pl.pallas_call(
        rotate_kernel,
        grid=(a.shape[0] // tile,),
        out_shape=jax.ShapeDtypeStruct((a.shape[0], HALF), F32),
        in_specs=[
            pl.BlockSpec((tile, HALF), lambda i: (i, 0)),
            pl.BlockSpec((tile, HALF), lambda i: (i, m_block)),
            pl.BlockSpec((2 * HALF, HALF), lambda i: (0, 0)),
        ],
        out_specs=pl.BlockSpec((tile, HALF), lambda i: (i, 0)),
        compiler_params=pltpu.CompilerParams(vmem_limit_bytes=VMEM_BYTES),
        name="rotate",
    )(a, m, q)


def passed_along(value):
    count = lax.axis_size("blk")
    return lax.ppermute(value, "blk", [(source, (source + 1) % count) for source in range(count)])


def summed(packed):
    shares = packed.reshape(SLABS, CHUNK // 2, 2, 128)
    mine = jnp.sum(lax.all_to_all(shares, "slab", 0, 0), axis=0)
    whole = lax.all_to_all(jnp.broadcast_to(mine[None], shares.shape), "slab", 0, 0)
    return whole.reshape(SLABS * CHUNK, 128)


def local(columns, movers):
    a, m, m_block = columns, columns, 1
    for round_index in range(ROUNDS):
        packed = summed(gram(a, m, m_block))
        stay, move = rotation(movers[round_index], packed)
        arrived = passed_along(rotate(a, m, m_block, move))
        a, m, m_block = rotate(a, m, m_block, stay), arrived, 0
    return jnp.concatenate([a, m], axis=1)


def solution(mesh):
    placed = (P("slab", "blk"), P(None, "blk"))
    return jax.shard_map(
        local, mesh=mesh, in_specs=placed, out_specs=P("slab", "blk"), check_vma=False
    )
```

time: 2340 us -> 170 us (0.07)
  waiting for transfers between devices: 2110 us -> 51.1 us
  matrix products: 155 us -> 0 us
  blocking collectives: 0 us -> 52 us
  Pallas kernels: 0 us -> 39.8 us
    all_gather x24 -> x0, waiting for transfers between devices: 1770 us -> none  [gather_iterate(): return lax.all_gather(iterate_rows, 'slab', axis=0, tiled=True)]
    psum x2 -> x0, waiting for transfers between devices: 290 us -> none  [local(): gram_matrix = lax.psum(inner_rows(current, current), 'slab')]
    dot_general x52 -> x0, matrix products: 155 us -> none  [the longest x26 83.6 us: matmul_high(): jnp.dot(left, right, precision=lax.Precision.HIGHEST, preferred_element_t...]
    all_to_all x0 -> x3, blocking collectives: none -> 52 us  [the longest x2 37.6 us: summed(): mine = jnp.sum(lax.all_to_all(shares, 'slab', 0, 0), axis=0)]
    pallas_call x0 -> x8, Pallas kernels: none -> 39.8 us  [the longest x2 25.3 us: rotation(): pl.pallas_call(rotation_kernel, out_shape=(out, out), in_specs=[pl.BlockS...]
  transfers between devices with their start and end apart: 28 -> 3, of which waited for: 28 -> 3; matrix products, arithmetic and copies ran while one was open for 0% -> 0% of each run, Pallas kernels for 0% -> 3%
where the time goes in v1:
time: 170 us
  blocking collectives  52 us (31%)
  waiting for transfers between devices  51.1 us (30%)
  Pallas kernels  39.8 us (23%)
  starting transfers between devices  16.7 us (10%)
  local copies, waits for them, and re-layouts  7.5 us (4%)
  other arithmetic  2.88 us (2%)
    ppermute x2, waiting for transfers between devices, passed_along(): lax.ppermute(value, 'blk', [(source, (source + 1) % count) for source in...  40.8 us
    all_to_all x2, blocking collectives, summed(): mine = jnp.sum(lax.all_to_all(shares, 'slab', 0, 0), axis=0)  37.6 us
    pallas_call x2, Pallas kernels, rotation(): pl.pallas_call(rotation_kernel, out_shape=(out, out), in_specs=[pl.BlockS...  25.3 us
    all_to_all x1, blocking collectives, summed(): lax.all_to_all(jnp.broadcast_to(mine[None], shares.shape), 'slab', 0, 0)  14.4 us
    ppermute x2, starting transfers between devices, passed_along(): lax.ppermute(value, 'blk', [(source, (source + 1) % count) for source in...  12.1 us
    all_to_all x1, waiting for transfers between devices, summed(): lax.all_to_all(jnp.broadcast_to(mine[None], shares.shape), 'slab', 0, 0)  10.3 us
    pallas_call x4, Pallas kernels, rotate(): pl.pallas_call(rotate_kernel, grid=(a.shape[0] // tile,), out_shape=jax.S...  10.3 us
    unnamed x10, local copies, waits for them, and re-layouts  5.96 us
  transfers between devices with their start and end apart: 3, of which 3 were waited for; matrix products, arithmetic and copies ran while one was open for 0% of the time, Pallas kernels for 3%

profile of v1, /device:TPU:1, one launch (start us, length us, event | category | flops | bytes accessed | tf_op | source)
XLA Modules:
  0.0 170.0 jit_solution(5773329803148792835)
XLA Ops:
  0.0 0.0 copy-start
  0.0 2.2 %copy-done = f32[2048,512]{1,0:T(8,128)S(1)} copy-done((f32[2048,512]{1,0:T(8,128)S(1)}, f32[2048,512]{1,0:T(8,128)}, u32[]{:S(2)}) %copy-start) | copy-done | bytes 4194328
  2.2 0.0 copy-start.4
  2.2 2.3 %gram.2 = f32[576,128]{1,0:T(8,128)S(1)} custom-call(f32[2048,512]{1,0:T(8,128)S(1)} %copy-done, f32[2048,512]{1,0:T(8,128)S(1)} %copy-done), custom_call_target="tpu_custom_call" | custom-call | tf_op jit(solution)/shard_map/gram/pallas_call | solution.py:131
  4.5 23.7 %all_to_all.20 = f32[32,9,2,128]{3,2,1,0:T(2,128)S(1)} all-to-all(f32[32,9,2,128]{3,2,1,0:T(2,128)S(1)} %bitcast.6), channel_id=1, replica_groups=mesh['slab'=32,'blk'=8] {'slab'}, dimensions={0} | all-to-all | bytes 589824 | tf_op jit(solution)/shard_map/all_to_all | solution.py:175
  28.2 0.1 reduce_sum.18
  28.3 0.8 broadcast_in_dim.4
  29.1 4.6 %all-to-all-start.1 = ((f32[32,9,2,128]{3,2,1,0:T(2,128)}), f32[32,9,2,128]{3,2,1,0:T(2,128)S(1)}, u32[]{:S(2)}, u32[]{:S(2)}) async-start(f32[32,9,2,128]{3,2,1,0:T(2,128)} %broadcast_in_dim.4), calls=%async_computation.1 | async-start | bytes 589824 | tf_op jit(solution)/shard_map/all_to_all | solution.py:176
  33.7 0.0 copy-done.4
  33.7 0.7 fusion
  34.4 10.3 %all-to-all-done.1 = f32[32,9,2,128]{3,2,1,0:T(2,128)S(1)} async-done(((f32[32,9,2,128]{3,2,1,0:T(2,128)}), f32[32,9,2,128]{3,2,1,0:T(2,128)S(1)}, u32[]{:S(2)}, u32[]{:S(2)}) %all-to-all-start.1) | async-done | bytes 294944 | tf_op jit(solution)/shard_map/all_to_all | solution.py:176
  44.7 12.6 %rotation.2 = (f32[512,256]{1,0:T(8,128)S(1)}, f32[512,256]{1,0:T(8,128)S(1)}) custom-call(s32[1]{0:T(128)} %bitcast.flag_ref, f32[576,128]{1,0:T(8,128)S(1)} %bitcast.8), custom_call_target="tpu_custom_call" | custom-call | tf_op jit(solution)/shard_map/rotation/pallas_call | solution.py:89
  57.3 0.0 copy-start.1
  57.3 2.2 %copy-done.1 = f32[2048,512]{1,0:T(8,128)S(1)} copy-done((f32[2048,512]{1,0:T(8,128)S(1)}, f32[2048,512]{1,0:T(8,128)}, u32[]{:S(2)}) %copy-start.1) | copy-done | bytes 4194328
  59.5 2.7 %rotate.5 = f32[2048,256]{1,0:T(8,128)S(1)} custom-call(f32[2048,512]{1,0:T(8,128)S(1)} %copy-done.1, f32[2048,512]{1,0:T(8,128)S(1)} %copy-done.1, f32[512,256]{1,0:T(8,128)S(1)} %get-tuple-element.10.q_ref), custom_call_target="tpu_custom_call" | custom-call | tf_op jit(solution)/shard_map/rotate/pallas_call | solution.py:153
  62.2 5.0 %collective-permute-start = (f32[2048,256]{1,0:T(8,128)S(1)}, f32[2048,256]{1,0:T(8,128)S(1)}, u32[]{:S(2)}, u32[]{:S(2)}) collective-permute-start(f32[2048,256]{1,0:T(8,128)S(1)} %rotate.5), channel_id=1, source_target_pairs={{0,1},{1,2},{2,3},{3,4},{4,5},{5,6},{6,7},{7,0},{8,9},{9,10},{10,1... | collective-permute-start | bytes 6291464 | tf_op jit(solution)/shard_map/ppermute | solution.py:170
  67.2 2.7 %rotate.4.a_ref = f32[2048,256]{1,0:T(8,128)S(1)} custom-call(f32[2048,512]{1,0:T(8,128)S(1)} %copy-done.1, f32[2048,512]{1,0:T(8,128)S(1)} %copy-done.1, f32[512,256]{1,0:T(8,128)S(1)} %get-tuple-element.9.q_ref), custom_call_target="tpu_custom_call" | custom-call | tf_op jit(solution)/shard_map/rotate/pallas_call | solution.py:153
  69.9 20.2 %collective-permute-done.m_ref = f32[2048,256]{1,0:T(8,128)S(1)} collective-permute-done((f32[2048,256]{1,0:T(8,128)S(1)}, f32[2048,256]{1,0:T(8,128)S(1)}, u32[]{:S(2)}, u32[]{:S(2)}) %collective-permute-start) | collective-permute-done | bytes 2097184 | tf_op jit(solution)/shard_map/ppermute | solution.py:170
  90.2 0.0 copy-start.2
  90.2 1.9 %gram.3 = f32[576,128]{1,0:T(8,128)S(1)} custom-call(f32[2048,256]{1,0:T(8,128)S(1)} %rotate.4.a_ref, f32[2048,256]{1,0:T(8,128)S(1)} %collective-permute-done.m_ref), custom_call_target="tpu_custom_call" | custom-call | tf_op jit(solution)/shard_map/gram/pallas_call | solution.py:131
  92.1 0.0 copy-done.2
  92.2 13.8 %all_to_all.21 = f32[32,9,2,128]{3,2,1,0:T(2,128)S(1)} all-to-all(f32[32,9,2,128]{3,2,1,0:T(2,128)S(1)} %bitcast.7), channel_id=1, replica_groups=mesh['slab'=32,'blk'=8] {'slab'}, dimensions={0} | all-to-all | bytes 589824 | tf_op jit(solution)/shard_map/all_to_all | solution.py:175
  106.0 0.1 reduce_sum.19
  106.1 0.1 broadcast_in_dim.5
  106.2 14.4 %all_to_all.22 = f32[32,9,2,128]{3,2,1,0:T(2,128)S(1)} all-to-all(f32[32,9,2,128]{3,2,1,0:T(2,128)S(1)} %broadcast_in_dim.5), channel_id=1, replica_groups=mesh['slab'=32,'blk'=8] {'slab'}, dimensions={0} | all-to-all | bytes 589824 | tf_op jit(solution)/shard_map/all_to_all | solution.py:176
  120.6 12.7 %rotation.3 = (f32[512,256]{1,0:T(8,128)S(1)}, f32[512,256]{1,0:T(8,128)S(1)}) custom-call(s32[1]{0:T(128)} %bitcast.3.flag_ref, f32[576,128]{1,0:T(8,128)S(1)} %bitcast.9), custom_call_target="tpu_custom_call" | custom-call | tf_op jit(solution)/shard_map/rotation/pallas_call | solution.py:89
  133.3 0.0 copy-start.3
  133.3 1.6 copy-done.3
  134.9 2.4 %rotate.7 = f32[2048,256]{1,0:T(8,128)S(1)} custom-call(f32[2048,256]{1,0:T(8,128)S(1)} %rotate.4.a_ref, f32[2048,256]{1,0:T(8,128)S(1)} %copy-done.3, f32[512,256]{1,0:T(8,128)S(1)} %get-tuple-element.12.q_ref), custom_call_target="tpu_custom_call" | custom-call | tf_op jit(solution)/shard_map/rotate/pallas_call | solution.py:153
  137.3 7.0 %collective-permute-start.1 = (f32[2048,256]{1,0:T(8,128)S(1)}, f32[2048,256]{1,0:T(8,128)S(1)}, u32[]{:S(2)}, u32[]{:S(2)}) collective-permute-start(f32[2048,256]{1,0:T(8,128)S(1)} %rotate.7), channel_id=1, source_target_pairs={{0,1},{1,2},{2,3},{3,4},{4,5},{5,6},{6,7},{7,0},{8,9},{9,10},{10,1... | collective-permute-start | bytes 6291464 | tf_op jit(solution)/shard_map/ppermute | solution.py:170
  144.4 2.4 %rotate.6 = f32[2048,256]{1,0:T(8,128)S(1)} custom-call(f32[2048,256]{1,0:T(8,128)S(1)} %rotate.4.a_ref, f32[2048,256]{1,0:T(8,128)S(1)} %copy-done.3, f32[512,256]{1,0:T(8,128)S(1)} %get-tuple-element.11.q_ref), custom_call_target="tpu_custom_call" | custom-call | tf_op jit(solution)/shard_map/rotate/pallas_call | solution.py:153
  146.8 20.6 %collective-permute-done.1 = f32[2048,256]{1,0:T(8,128)S(1)} collective-permute-done((f32[2048,256]{1,0:T(8,128)S(1)}, f32[2048,256]{1,0:T(8,128)S(1)}, u32[]{:S(2)}, u32[]{:S(2)}) %collective-permute-start.1) | collective-permute-done | bytes 2097184 | tf_op jit(solution)/shard_map/ppermute | solution.py:170
  167.4 2.7 %pad_maximum_fusion = f32[2048,512]{1,0:T(8,128)} fusion(f32[2048,256]{1,0:T(8,128)S(1)} %collective-permute-done.1, f32[2048,256]{1,0:T(8,128)S(1)} %rotate.6), kind=kLoop, calls=%fused_computation | loop fusion | flops 1048576 | bytes 8388608 | tf_op jit(solution)/shard_map/concatenate | solution.py:187
Async XLA Ops:
  0.0 2.2 %copy-start = (f32[2048,512]{1,0:T(8,128)S(1)}, f32[2048,512]{1,0:T(8,128)}, u32[]{:S(2)}) copy-start(f32[2048,512]{1,0:T(8,128)} %m_ref.5) | copy-start | bytes 12582916
  2.2 31.5 %copy-start.4 = (s32[2,1]{0,1:T(1,128)S(1)}, s32[2,1]{0,1:T(1,128)}, u32[]{:S(2)}) copy-start(s32[2,1]{0,1:T(1,128)} %param.3) | copy-start | bytes 28
  29.1 15.6 %all-to-all-start.1 = ((f32[32,9,2,128]{3,2,1,0:T(2,128)}), f32[32,9,2,128]{3,2,1,0:T(2,128)S(1)}, u32[]{:S(2)}, u32[]{:S(2)}) async-start(f32[32,9,2,128]{3,2,1,0:T(2,128)} %broadcast_in_dim.4), calls=%async_computation.1 | async-start | bytes 589824 | tf_op jit(solution)/shard_map/all_to_all | solution.py:176
  57.3 2.2 %copy-start.1 = (f32[2048,512]{1,0:T(8,128)S(1)}, f32[2048,512]{1,0:T(8,128)}, u32[]{:S(2)}) copy-start(f32[2048,512]{1,0:T(8,128)} %m_ref.5) | copy-start | bytes 12582916
  62.2 28.0 %collective-permute-start = (f32[2048,256]{1,0:T(8,128)S(1)}, f32[2048,256]{1,0:T(8,128)S(1)}, u32[]{:S(2)}, u32[]{:S(2)}) collective-permute-start(f32[2048,256]{1,0:T(8,128)S(1)} %rotate.5), channel_id=1, source_target_pairs={{0,1},{1,2},{2,3},{3,4},{4,5},{5,6},{6,7},{7,0},{8,9},{9,10},{10,1... | collective-permute-start | bytes 6291464 | tf_op jit(solution)/shard_map/ppermute | solution.py:170
  90.2 1.9 %copy-start.2 = (f32[2048,256]{1,0:T(8,128)}, f32[2048,256]{1,0:T(8,128)S(1)}, u32[]{:S(2)}) copy-start(f32[2048,256]{1,0:T(8,128)S(1)} %collective-permute-done.m_ref) | copy-start | bytes 6291460
  133.3 1.6 copy-start.3
  137.3 30.0 %collective-permute-start.1 = (f32[2048,256]{1,0:T(8,128)S(1)}, f32[2048,256]{1,0:T(8,128)S(1)}, u32[]{:S(2)}, u32[]{:S(2)}) collective-permute-start(f32[2048,256]{1,0:T(8,128)S(1)} %rotate.7), channel_id=1, source_target_pairs={{0,1},{1,2},{2,3},{3,4},{4,5},{5,6},{6,7},{7,0},{8,9},{9,10},{10,1... | collective-permute-start | bytes 6291464 | tf_op jit(solution)/shard_map/ppermute | solution.py:170

commit v2 on v1

v2 whole, which is shorter than its diff:
```python
import jax
import jax.numpy as jnp
from jax import lax
from jax.experimental import pallas as pl
from jax.experimental.pallas import tpu as pltpu
from jax.sharding import PartitionSpec as P

HALF = 256
PAIR = 2 * HALF
SLABS = 32
CHUNK = 20
EPS = 1e-6
VMEM_BYTES = 40 * 2**20
F32 = jnp.float32
BF16 = jnp.bfloat16
NN = (((1,), (0,)), ((), ()))
NT = (((1,), (1,)), ((), ()))
TN = (((0,), (0,)), ((), ()))


def split(x):
    high = x.astype(BF16)
    low = (x - high.astype(F32)).astype(BF16)
    return high, low


def dot3(left, right, dims):
    def one(a, b):
        return lax.dot_general(a, b, dims, preferred_element_type=F32)

    return one(left[0], right[0]) + (one(left[0], right[1]) + one(left[1], right[0]))


def call(kernel, name, out_shape, flops, **kwargs):
    return pl.pallas_call(
        kernel,
        out_shape=out_shape,
        compiler_params=pltpu.CompilerParams(vmem_limit_bytes=VMEM_BYTES),
        cost_estimate=pl.CostEstimate(flops=flops, bytes_accessed=2**22, transcendentals=0),
        name=name,
        **kwargs,
    )


def blocks(tile, width, block=0):
    return pl.BlockSpec((tile, width), lambda i: (i, block))


def whole(shape):
    return pl.BlockSpec(shape, lambda i: (0,) * len(shape))


def two_steps(e1, e2, o, eye):
    op, e1p, e2p = split(o), split(e1), split(e2)
    d1 = eye - (dot3(op, op, NT) + dot3(e1p, e1p, NN))
    d2 = eye - (dot3(op, op, TN) + dot3(e2p, e2p, NN))
    w1, w2 = weights(d1, d2, eye)
    w1, w2 = split(w1), split(w2)
    return dot3(w1, e1p, NN), dot3(w2, e2p, NN), dot3(w1, op, NN)


def weights(d1, d2, eye):
    d1p, d2p = split(d1), split(d2)
    q1 = dot3(d1p, d1p, NN)
    q2 = dot3(d2p, d2p, NN)
    i1 = split(0.375 * eye + 0.3125 * d1 + 0.0625 * q1)
    i2 = split(0.375 * eye + 0.3125 * d2 + 0.0625 * q2)
    w1 = eye + 0.5 * d1 + dot3(split(q1), i1, NN)
    w2 = eye + 0.5 * d2 + dot3(split(q2), i2, NN)
    return w1, w2


def rotation_kernel(flag_ref, packed_ref, stay_ref, move_ref):
    left = [packed_ref[CHUNK * k:CHUNK * k + 8, :] for k in range(SLABS)]
    right = [packed_ref[CHUNK * k + 8:CHUNK * k + 16, :] for k in range(SLABS)]
    cross = jnp.concatenate([jnp.concatenate(left, 0), jnp.concatenate(right, 0)], 1)
    norms = packed_ref[16:20, :]
    for k in range(1, SLABS):
        norms = norms + packed_ref[CHUNK * k + 16:CHUNK * k + 20, :]
    norm_a = jnp.concatenate([norms[0:1], norms[1:2]], 1)
    norm_m = jnp.concatenate([norms[2:3], norms[3:4]], 1)
    rows = lax.broadcasted_iota(jnp.int32, (HALF, HALF), 0)
    cols = lax.broadcasted_iota(jnp.int32, (HALF, HALF), 1)
    eye = (rows == cols).astype(F32)
    norm_a = jnp.transpose(jnp.broadcast_to(norm_a, (HALF, HALF)))
    diff = norm_a - norm_m
    total = norm_a + norm_m
    skew = -cross * diff / (diff * diff + 0.25 * total * total + EPS)
    scale = 1.0 / (4.0 * jnp.sqrt(PAIR + 2.0 * jnp.sum(skew * skew, keepdims=True)))
    start = scale * skew
    parts = split(start)
    own = (1.0 - scale * scale) * eye
    w1, w2 = weights(own - dot3(parts, parts, NT), own - dot3(parts, parts, TN), eye)
    e1, e2, o = scale * w1, scale * w2, dot3(split(w1), parts, NN)
    for _ in range(5):
        e1, e2, o = two_steps(e1, e2, o, eye)
    minus_ot = -jnp.transpose(o)

    @pl.when(flag_ref[0] == 1)
    def _():
        move_ref[:HALF, :] = e1
        move_ref[HALF:, :] = minus_ot
        stay_ref[:HALF, :] = o
        stay_ref[HALF:, :] = e2

    @pl.when(flag_ref[0] != 1)
    def _():
        stay_ref[:HALF, :] = e1
        stay_ref[HALF:, :] = minus_ot
        move_ref[:HALF, :] = o
        move_ref[HALF:, :] = e2


def rotation(flag, packed):
    out = jax.ShapeDtypeStruct((PAIR, HALF), F32)
    return call(
        rotation_kernel,
        "rotation",
        (out, out),
        10**10,
        in_specs=[pl.BlockSpec(memory_space=pltpu.SMEM), pl.BlockSpec(memory_space=pltpu.VMEM)],
        out_specs=[pl.BlockSpec(memory_space=pltpu.VMEM)] * 2,
    )(flag, packed)


def inner_kernel(width, a_ref, m_ref, packed_ref, norm_ref, acc_ref):
    step = pl.program_id(0)

    @pl.when(step == 0)
    def _():
        acc_ref[...] = jnp.zeros_like(acc_ref)
        norm_ref[...] = jnp.zeros_like(norm_ref)

    a, m = a_ref[...], m_ref[...]
    acc_ref[...] += dot3(split(a), split(m), TN)
    norm_ref[0:1, :] += jnp.sum(a * a, axis=0, keepdims=True)
    if width == HALF:
        norm_ref[1:2, :] += jnp.sum(m * m, axis=0, keepdims=True)

    @pl.when(step == pl.num_programs(0) - 1)
    def _():
        per = 8 * width // 128
        for k in range(SLABS):
            for b in range(width // 128):
                packed_ref[per * k + 8 * b:per * k + 8 * b + 8, :] = acc_ref[8 * k:8 * k + 8, 128 * b:128 * b + 128]


def inner(a, m, width, block, tile=512):
    rows = HALF * width // 128
    return call(
        lambda *refs: inner_kernel(width, *refs),
        "inner",
        (jax.ShapeDtypeStruct((rows, 128), F32), jax.ShapeDtypeStruct((8, HALF), F32)),
        6 * a.shape[0] * HALF * width,
        grid=(a.shape[0] // tile,),
        in_specs=[blocks(tile, HALF), blocks(tile, width, block)],
        out_specs=[whole((rows, 128)), whole((8, HALF))],
        scratch_shapes=[pltpu.VMEM((HALF, width), F32)],
    )(a, m)


def fill(out_ref, cross, norm_a, norm_m):
    chunk = jnp.concatenate(
        [cross[:, :128], cross[:, 128:], norm_a[:, :128], norm_a[:, 128:], norm_m[:, :128], norm_m[:, 128:]], 0
    )
    for k in range(SLABS):
        out_ref[CHUNK * k:CHUNK * k + CHUNK, :] = chunk


def share_kernel(parts_ref, norm_ref, out_ref):
    total = parts_ref[0:16, :]
    for k in range(1, SLABS):
        total = total + parts_ref[16 * k:16 * k + 16, :]
    cross = jnp.concatenate([total[:8], total[8:]], 1)
    fill(out_ref, cross, norm_ref[0:1, :], norm_ref[1:2, :])


def project_kernel(parts_ref, move_ref, norm_a_ref, norm_m_ref, out_ref):
    total = parts_ref[0:32, :]
    for k in range(1, SLABS):
        total = total + parts_ref[32 * k:32 * k + 32, :]
    wide = jnp.concatenate([total[8 * b:8 * b + 8] for b in range(4)], 1)
    wide = jnp.concatenate([wide, wide], 0)
    cross = dot3(split(wide), split(move_ref[...]), NN)[:8]
    fill(out_ref, cross, norm_a_ref[0:1, :], norm_m_ref[0:1, :])


def payload(kernel, *arrays):
    return call(kernel, "payload", jax.ShapeDtypeStruct((SLABS * CHUNK, 128), F32), 10**7)(*arrays)


def turn_kernel(a_ref, q_ref, out_ref, norm_ref):
    @pl.when(pl.program_id(0) == 0)
    def _():
        norm_ref[...] = jnp.zeros_like(norm_ref)

    out = dot3(split(a_ref[...]), split(q_ref[...]), NN)
    out_ref[...] = out
    norm_ref[0:1, :] += jnp.sum(out * out, axis=0, keepdims=True)


def turn(a, q, tile=512):
    rows = a.shape[0]
    return call(
        turn_kernel,
        "turn",
        (jax.ShapeDtypeStruct((rows, HALF), F32), jax.ShapeDtypeStruct((8, HALF), F32)),
        6 * rows * PAIR * HALF,
        grid=(rows // tile,),
        in_specs=[blocks(tile, PAIR), whole(q.shape)],
        out_specs=[blocks(tile, HALF), whole((8, HALF))],
    )(a, q)


def last_kernel(a_ref, m_ref, q_ref, *refs):
    refs[-1][...] = dot3(split(a_ref[...]), split(q_ref[:HALF, :]), NN) + dot3(
        split(m_ref[...]), split(q_ref[HALF:, :]), NN
    )


def last(a, m, q, block, onto=None, tile=512):
    rows = a.shape[0]
    specs = [blocks(tile, HALF), blocks(tile, HALF), whole(q.shape)]
    extra = () if onto is None else (onto,)
    return call(
        last_kernel,
        "last",
        jax.ShapeDtypeStruct((rows, PAIR), F32),
        6 * rows * PAIR * HALF,
        grid=(rows // tile,),
        in_specs=specs + [pl.BlockSpec(memory_space=pl.ANY)] * len(extra),
        out_specs=blocks(tile, HALF, block),
        input_output_aliases={3: 0} if extra else {},
    )(a, m, q, *extra)


def passed_along(value):
    count = lax.axis_size("blk")
    return lax.ppermute(value, "blk", [(source, (source + 1) % count) for source in range(count)])


def exchanged(packed, shape):
    return lax.all_to_all(packed.reshape(SLABS, *shape), "slab", 0, 0).reshape(packed.shape)


def local(columns, movers):
    left_columns = passed_along(columns)

    cross, norms = inner(columns, columns, HALF, 1)
    parts = exchanged(cross, (16, 128))
    packed = exchanged(payload(share_kernel, parts, norms), (CHUNK // 2, 2, 128))
    stay, move = rotation(movers[0], packed)

    left_turn = passed_along(jnp.concatenate([move, stay], axis=0))
    left_move, left_stay = left_turn[:PAIR], left_turn[PAIR:]
    a, _ = turn(columns, stay)
    cross, norm_a = inner(a, left_columns, PAIR, 0)
    parts = exchanged(cross, (32, 128))
    m, norm_m = turn(left_columns, left_move)
    left_m = passed_along(m)
    packed = exchanged(payload(project_kernel, parts, left_move, norm_a, norm_m), (CHUNK // 2, 2, 128))
    stay, move = rotation(movers[1], packed)

    left_move = passed_along(move)
    left_a, _ = turn(left_columns, left_stay)
    out = last(a, m, stay, 0)
    return last(left_a, left_m, left_move, 1, out)


def solution(mesh):
    placed = (P("slab", "blk"), P(None, "blk"))
    return jax.shard_map(
        local, mesh=mesh, in_specs=placed, out_specs=P("slab", "blk"), check_vma=False
    )
```

time: 170 us -> 141 us (0.83)
  waiting for transfers between devices: 51.1 us -> 20.3 us
  Pallas kernels: 39.8 us -> 53.8 us
  blocking collectives: 52 us -> 41.2 us
  local copies, waits for them, and re-layouts: 7.5 us -> 4.89 us
  starting transfers between devices: 16.7 us -> 18.8 us
  other arithmetic: 2.88 us -> 1.04 us
    ppermute x2 -> x4, waiting for transfers between devices: 40.8 us -> 0.01 us  [passed_along(): lax.ppermute(value, 'blk', [(source, (source + 1) % count) for source in...]
    pallas_call x8 -> x11, Pallas kernels: 39.8 us -> 53.8 us  [the longest x2 21.9 us: rotation(): call(rotation_kernel, 'rotation', (out, out), 10 ** 10, in_specs=[pl.Bloc...]
    all_to_all x3 -> x2, blocking collectives: 52 us -> 41.2 us  [exchanged(): lax.all_to_all(packed.reshape(SLABS, *shape), 'slab', 0, 0)]
    all_to_all x1 -> x2, waiting for transfers between devices: 10.3 us -> 20.3 us  [exchanged(): lax.all_to_all(packed.reshape(SLABS, *shape), 'slab', 0, 0)]
    unnamed x10 -> x8, local copies, waits for them, and re-layouts: 5.96 us -> 2.23 us
    all_to_all x1 -> x2, starting transfers between devices: 4.61 us -> 7.76 us  [exchanged(): lax.all_to_all(packed.reshape(SLABS, *shape), 'slab', 0, 0)]
    slice x1 -> x2, local copies, waits for them, and re-layouts: 0.66 us -> 2.66 us  [the longest x1 2.06 us: local(): left_move, left_stay = (left_turn[:PAIR], left_turn[PAIR:])]
    ppermute x2 -> x4, starting transfers between devices: 12.1 us -> 11 us  [passed_along(): lax.ppermute(value, 'blk', [(source, (source + 1) % count) for source in...]
  transfers between devices with their start and end apart: 3 -> 6, of which waited for: 3 -> 2; matrix products, arithmetic and copies ran while one was open for 0% -> 3% of each run, Pallas kernels for 3% -> 35%
where the time goes in v2:
time: 141 us; the launch traced here: 140 us
  Pallas kernels  53.8 us (38%)
  blocking collectives  41.2 us (29%)
  waiting for transfers between devices  20.3 us (14%)
  starting transfers between devices  18.8 us (13%)
  local copies, waits for them, and re-layouts  4.89 us (3%)
    all_to_all x2, blocking collectives, exchanged(): lax.all_to_all(packed.reshape(SLABS, *shape), 'slab', 0, 0)  41.2 us
    pallas_call x2, Pallas kernels, rotation(): call(rotation_kernel, 'rotation', (out, out), 10 ** 10, in_specs=[pl.Bloc...  21.9 us
    all_to_all x2, waiting for transfers between devices, exchanged(): lax.all_to_all(packed.reshape(SLABS, *shape), 'slab', 0, 0)  20.3 us
    pallas_call x3, Pallas kernels, turn(): call(turn_kernel, 'turn', (jax.ShapeDtypeStruct((rows, HALF), F32), jax.S...  13.3 us
    ppermute x4, starting transfers between devices, passed_along(): lax.ppermute(value, 'blk', [(source, (source + 1) % count) for source in...  11 us
    pallas_call x2, Pallas kernels, last(): call(last_kernel, 'last', jax.ShapeDtypeStruct((rows, PAIR), F32), 6 * ro...  9.87 us
    all_to_all x2, starting transfers between devices, exchanged(): lax.all_to_all(packed.reshape(SLABS, *shape), 'slab', 0, 0)  7.76 us
    pallas_call x2, Pallas kernels, inner(): call(lambda *refs: inner_kernel(width, *refs), 'inner', (jax.ShapeDtypeSt...  7.64 us
  transfers between devices with their start and end apart: 6, of which 2 were waited for; matrix products, arithmetic and copies ran while one was open for 3% of the time, Pallas kernels for 35%

profile of v2, /device:TPU:1, one launch (start us, length us, event | category | flops | bytes accessed | tf_op | source)
XLA Modules:
  0.0 140.1 jit_solution(1453247927678817210)
XLA Ops:
  0.0 2.7 %collective-permute-start = (f32[2048,512]{1,0:T(8,128)}, f32[2048,512]{1,0:T(8,128)}, u32[]{:S(2)}, u32[]{:S(2)}) collective-permute-start(f32[2048,512]{1,0:T(8,128)} %a_ref.1), channel_id=1, source_target_pairs={{0,1},{1,2},{2,3},{3,4},{4,5},{5,6},{6,7},{7,0},{8,9},{9,10},{10,1... | collective-permute-start | bytes 12582920 | tf_op jit(solution)/shard_map/ppermute | solution.py:239
  2.7 0.0 copy-start
  2.7 2.2 %copy-done = f32[2048,512]{1,0:T(8,128)S(1)} copy-done((f32[2048,512]{1,0:T(8,128)S(1)}, f32[2048,512]{1,0:T(8,128)}, u32[]{:S(2)}) %copy-start) | copy-done | bytes 4194328
  4.9 0.0 copy-start.3
  4.9 2.3 %inner.2 = (f32[512,128]{1,0:T(8,128)S(1)}, f32[8,256]{1,0:T(8,128)S(1)}) custom-call(f32[2048,512]{1,0:T(8,128)S(1)} %copy-done, f32[2048,512]{1,0:T(8,128)S(1)} %copy-done), custom_call_target="tpu_custom_call" | custom-call | flops 805306368 | bytes 4194304 | tf_op jit(solution)/shard_map/inner/pallas_call | solution.py:150
  7.2 23.5 %all_to_all.20 = f32[32,16,128]{2,1,0:T(8,128)S(1)} all-to-all(f32[32,16,128]{2,1,0:T(8,128)S(1)} %bitcast.15), channel_id=1, replica_groups=mesh['slab'=32,'blk'=8] {'slab'}, dimensions={0} | all-to-all | bytes 524288 | tf_op jit(solution)/shard_map/all_to_all | solution.py:243
  30.7 0.8 payload.2
  31.5 3.9 %all-to-all-start.1 = ((f32[32,10,2,128]{3,2,1,0:T(2,128)}), f32[32,10,2,128]{3,2,1,0:T(2,128)S(1)}, u32[]{:S(2)}, u32[]{:S(2)}) async-start(f32[32,10,2,128]{3,2,1,0:T(2,128)} %bitcast.3), calls=%async_computation.1 | async-start | bytes 655360 | tf_op jit(solution)/shard_map/all_to_all | solution.py:243
  35.4 0.0 copy-done.3
  35.4 0.6 fusion.1
  36.0 12.7 %all-to-all-done.1 = f32[32,10,2,128]{3,2,1,0:T(2,128)S(1)} async-done(((f32[32,10,2,128]{3,2,1,0:T(2,128)}), f32[32,10,2,128]{3,2,1,0:T(2,128)S(1)}, u32[]{:S(2)}, u32[]{:S(2)}) %all-to-all-start.1) | async-done | bytes 327712 | tf_op jit(solution)/shard_map/all_to_all | solution.py:243
  48.7 0.0 copy-start.1
  48.7 11.0 %rotation.2 = (f32[512,256]{1,0:T(8,128)S(1)}, f32[512,256]{1,0:T(8,128)S(1)}) custom-call(s32[1]{0:T(128)} %bitcast.flag_ref, f32[640,128]{1,0:T(8,128)S(1)} %bitcast.13), custom_call_target="tpu_custom_call" | custom-call | flops 10000000000 | bytes 4194304 | tf_op jit(solution)/shard_map/rotation/pallas_call | solution.py:116
  59.7 1.0 pad_maximum_fusion
  60.7 2.9 %collective-permute-start.1 = (f32[1024,256]{1,0:T(8,128)}, f32[1024,256]{1,0:T(8,128)}, u32[]{:S(2)}, u32[]{:S(2)}) collective-permute-start(f32[1024,256]{1,0:T(8,128)} %pad_maximum_fusion), channel_id=1, source_target_pairs={{0,1},{1,2},{2,3},{3,4},{4,5},{5,6},{6,7},{7,0},{8,9},{9,10},{10,1... | collective-permute-start | bytes 3145736 | tf_op jit(solution)/shard_map/ppermute | solution.py:239
  63.7 0.0 copy-done.1
  63.7 3.1 %turn.5 = (f32[2048,256]{1,0:T(8,128)S(1)}, f32[8,256]{1,0:T(8,128)}) custom-call(f32[2048,512]{1,0:T(8,128)S(1)} %copy-done.1, f32[512,256]{1,0:T(8,128)S(1)} %get-tuple-element.20.q_ref), custom_call_target="tpu_custom_call" | custom-call | flops 1610612736 | bytes 4194304 | tf_op jit(solution)/shard_map/turn/pallas_call | solution.py:204
  66.8 0.0 collective-permute-done.a_ref.refs_1_
  66.8 5.4 %inner.3 = (f32[1024,128]{1,0:T(8,128)}, f32[8,256]{1,0:T(8,128)S(1)}) custom-call(f32[2048,256]{1,0:T(8,128)S(1)} %get-tuple-element.23.refs_0_.a_ref, f32[2048,512]{1,0:T(8,128)} %collective-permute-done.a_ref.refs_1_), custom_call_target="tpu_custom_call" | custom-call | flops 1610612736 | bytes 4194304 | tf_op jit(solution)/shard_map/inner/pallas_call | solution.py:150
  72.1 3.9 %all-to-all-start.2 = ((f32[32,32,128]{2,1,0:T(8,128)}), f32[32,32,128]{2,1,0:T(8,128)S(1)}, u32[]{:S(2)}, u32[]{:S(2)}) async-start(f32[32,32,128]{2,1,0:T(8,128)} %bitcast.6), calls=%async_computation.2 | async-start | bytes 1048576 | tf_op jit(solution)/shard_map/all_to_all | solution.py:243
  76.0 0.0 collective-permute-done.1
  76.0 2.1 %fusion = (f32[512,256]{1,0:T(8,128)S(1)}, f32[512,256]{1,0:T(8,128)}) fusion(f32[1024,256]{1,0:T(8,128)} %collective-permute-done.1), kind=kLoop, calls=%fused_computation.1 | loop fusion | bytes 2097152 | tf_op jit(solution)/shard_map/slice | solution.py:255
  78.1 5.3 %turn.4 = (f32[2048,256]{1,0:T(8,128)}, f32[8,256]{1,0:T(8,128)S(1)}) custom-call(f32[2048,512]{1,0:T(8,128)} %collective-permute-done.a_ref.refs_1_, f32[512,256]{1,0:T(8,128)S(1)} %get-tuple-element.29.q_ref.move_ref), custom_call_target="tpu_custom_call" | custom-call | flops 1610612736 | bytes 4194304 | tf_op jit(solution)/shard_map/turn/pallas_call | solution.py:204
  83.4 2.2 %collective-permute-start.2 = (f32[2048,256]{1,0:T(8,128)}, f32[2048,256]{1,0:T(8,128)}, u32[]{:S(2)}, u32[]{:S(2)}) collective-permute-start(f32[2048,256]{1,0:T(8,128)} %get-tuple-element.22.m_ref), channel_id=1, source_target_pairs={{0,1},{1,2},{2,3},{3,4},{4,5},{5,6},{6,7},{7,0},{8,9},{9,10},{10,1... | collective-permute-start | bytes 6291464 | tf_op jit(solution)/shard_map/ppermute | solution.py:239
  85.6 7.6 %all-to-all-done.2 = f32[32,32,128]{2,1,0:T(8,128)S(1)} async-done(((f32[32,32,128]{2,1,0:T(8,128)}), f32[32,32,128]{2,1,0:T(8,128)S(1)}, u32[]{:S(2)}, u32[]{:S(2)}) %all-to-all-start.2) | async-done | bytes 524320 | tf_op jit(solution)/shard_map/all_to_all | solution.py:243
  93.2 0.3 payload.3
  93.5 17.7 %all_to_all.21 = f32[32,10,2,128]{3,2,1,0:T(2,128)S(1)} all-to-all(f32[32,10,2,128]{3,2,1,0:T(2,128)S(1)} %bitcast.11), channel_id=1, replica_groups=mesh['slab'=32,'blk'=8] {'slab'}, dimensions={0} | all-to-all | bytes 655360 | tf_op jit(solution)/shard_map/all_to_all | solution.py:243
  111.1 0.0 copy-start.2
  111.1 10.9 %rotation.3 = (f32[512,256]{1,0:T(8,128)S(1)}, f32[512,256]{1,0:T(8,128)S(1)}) custom-call(s32[1]{0:T(128)} %bitcast.5.flag_ref, f32[640,128]{1,0:T(8,128)S(1)} %bitcast.14), custom_call_target="tpu_custom_call" | custom-call | flops 10000000000 | bytes 4194304 | tf_op jit(solution)/shard_map/rotation/pallas_call | solution.py:116
  122.1 3.2 %collective-permute-start.3 = (f32[512,256]{1,0:T(8,128)S(1)}, f32[512,256]{1,0:T(8,128)S(1)}, u32[]{:S(2)}, u32[]{:S(2)}) collective-permute-start(f32[512,256]{1,0:T(8,128)S(1)} %get-tuple-element.27), channel_id=1, source_target_pairs={{0,1},{1,2},{2,3},{3,4},{4,5},{5,6},{6,7},{7,0},{8,9},{9,10},{10,1... | collective-permute-start | bytes 1572872 | tf_op jit(solution)/shard_map/ppermute | solution.py:239
  125.3 0.0 copy-done.2
  125.3 5.0 %turn.3 = (f32[2048,256]{1,0:T(8,128)S(1)}, f32[8,256]{1,0:T(8,128)}) custom-call(f32[2048,512]{1,0:T(8,128)} %collective-permute-done.a_ref.refs_1_, f32[512,256]{1,0:T(8,128)S(1)} %copy-done.2), custom_call_target="tpu_custom_call" | custom-call | flops 1610612736 | bytes 4194304 | tf_op jit(solution)/shard_map/turn/pallas_call | solution.py:204
  130.2 4.9 %last.2.refs_0_ = f32[2048,512]{1,0:T(8,128)} custom-call(f32[2048,256]{1,0:T(8,128)S(1)} %get-tuple-element.23.refs_0_.a_ref, f32[2048,256]{1,0:T(8,128)} %get-tuple-element.22.m_ref, f32[512,256]{1,0:T(8,128)S(1)} %get-tuple-element.28.q_ref), custom_call_target="tpu_custom_call" | custom-call | flops 1610612736 | bytes 4194304 | tf_op jit(solution)/shard_map/last/pallas_call | solution.py:225
  135.2 0.0 collective-permute-done.2.m_ref
  135.2 0.0 collective-permute-done.3.q_ref
  135.2 4.9 %last.3 = f32[2048,512]{1,0:T(8,128)} custom-call(f32[2048,256]{1,0:T(8,128)S(1)} %get-tuple-element.21.a_ref, f32[2048,256]{1,0:T(8,128)} %collective-permute-done.2.m_ref, f32[512,256]{1,0:T(8,128)S(1)} %collective-permute-done.3.q_ref, f32[2048,512]{1,0:T(8,128)} %last.2.refs_0_), custom_call_target="tpu_custom_call", output_to_operand_aliasing={{}: (3, {})} | custom-call | flops 1610612736 | bytes 4194304 | tf_op jit(solution)/shard_map/last/pallas_call | solution.py:225
Async XLA Ops:
  0.0 66.8 %collective-permute-start = (f32[2048,512]{1,0:T(8,128)}, f32[2048,512]{1,0:T(8,128)}, u32[]{:S(2)}, u32[]{:S(2)}) collective-permute-start(f32[2048,512]{1,0:T(8,128)} %a_ref.1), channel_id=1, source_target_pairs={{0,1},{1,2},{2,3},{3,4},{4,5},{5,6},{6,7},{7,0},{8,9},{9,10},{10,1... | collective-permute-start | bytes 12582920 | tf_op jit(solution)/shard_map/ppermute | solution.py:239
  2.7 2.2 %copy-start = (f32[2048,512]{1,0:T(8,128)S(1)}, f32[2048,512]{1,0:T(8,128)}, u32[]{:S(2)}) copy-start(f32[2048,512]{1,0:T(8,128)} %a_ref.1) | copy-start | bytes 12582916
  4.9 30.5 %copy-start.3 = (s32[2,1]{0,1:T(1,128)S(1)}, s32[2,1]{0,1:T(1,128)}, u32[]{:S(2)}) copy-start(s32[2,1]{0,1:T(1,128)} %param.3) | copy-start | bytes 28
  31.5 17.2 %all-to-all-start.1 = ((f32[32,10,2,128]{3,2,1,0:T(2,128)}), f32[32,10,2,128]{3,2,1,0:T(2,128)S(1)}, u32[]{:S(2)}, u32[]{:S(2)}) async-start(f32[32,10,2,128]{3,2,1,0:T(2,128)} %bitcast.3), calls=%async_computation.1 | async-start | bytes 655360 | tf_op jit(solution)/shard_map/all_to_all | solution.py:243
  48.7 15.0 %copy-start.1 = (f32[2048,512]{1,0:T(8,128)S(1)}, f32[2048,512]{1,0:T(8,128)}, u32[]{:S(2)}) copy-start(f32[2048,512]{1,0:T(8,128)} %a_ref.1) | copy-start | bytes 12582916
  60.7 15.3 %collective-permute-start.1 = (f32[1024,256]{1,0:T(8,128)}, f32[1024,256]{1,0:T(8,128)}, u32[]{:S(2)}, u32[]{:S(2)}) collective-permute-start(f32[1024,256]{1,0:T(8,128)} %pad_maximum_fusion), channel_id=1, source_target_pairs={{0,1},{1,2},{2,3},{3,4},{4,5},{5,6},{6,7},{7,0},{8,9},{9,10},{10,1... | collective-permute-start | bytes 3145736 | tf_op jit(solution)/shard_map/ppermute | solution.py:239
  72.1 21.1 %all-to-all-start.2 = ((f32[32,32,128]{2,1,0:T(8,128)}), f32[32,32,128]{2,1,0:T(8,128)S(1)}, u32[]{:S(2)}, u32[]{:S(2)}) async-start(f32[32,32,128]{2,1,0:T(8,128)} %bitcast.6), calls=%async_computation.2 | async-start | bytes 1048576 | tf_op jit(solution)/shard_map/all_to_all | solution.py:243
  83.4 51.7 %collective-permute-start.2 = (f32[2048,256]{1,0:T(8,128)}, f32[2048,256]{1,0:T(8,128)}, u32[]{:S(2)}, u32[]{:S(2)}) collective-permute-start(f32[2048,256]{1,0:T(8,128)} %get-tuple-element.22.m_ref), channel_id=1, source_target_pairs={{0,1},{1,2},{2,3},{3,4},{4,5},{5,6},{6,7},{7,0},{8,9},{9,10},{10,1... | collective-permute-start | bytes 6291464 | tf_op jit(solution)/shard_map/ppermute | solution.py:239
  111.1 14.2 %copy-start.2 = (f32[512,256]{1,0:T(8,128)S(1)}, f32[512,256]{1,0:T(8,128)}, u32[]{:S(2)}) copy-start(f32[512,256]{1,0:T(8,128)} %get-tuple-element.30.q_ref) | copy-start | bytes 1572868
  122.1 13.1 %collective-permute-start.3 = (f32[512,256]{1,0:T(8,128)S(1)}, f32[512,256]{1,0:T(8,128)S(1)}, u32[]{:S(2)}, u32[]{:S(2)}) collective-permute-start(f32[512,256]{1,0:T(8,128)S(1)} %get-tuple-element.27), channel_id=1, source_target_pairs={{0,1},{1,2},{2,3},{3,4},{4,5},{5,6},{6,7},{7,0},{8,9},{9,10},{10,1... | collective-permute-start | bytes 1572872 | tf_op jit(solution)/shard_map/ppermute | solution.py:239

commit v3 on v2

v3 whole, which is shorter than its diff:
```python
import jax
import jax.numpy as jnp
from jax import lax
from jax.experimental import pallas as pl
from jax.experimental.pallas import tpu as pltpu
from jax.sharding import PartitionSpec as P

HALF = 256
PAIR = 2 * HALF
SLABS = 32
CHUNK = 20
EPS = 1e-6
VMEM_BYTES = 20 * 2**20
F32 = jnp.float32
BF16 = jnp.bfloat16
NN = (((1,), (0,)), ((), ()))
NT = (((1,), (1,)), ((), ()))
TN = (((0,), (0,)), ((), ()))


def split(x):
    high = x.astype(BF16)
    low = (x - high.astype(F32)).astype(BF16)
    return high, low


def dot3(left, right, dims):
    def one(a, b):
        return lax.dot_general(a, b, dims, preferred_element_type=F32)

    return one(left[0], right[0]) + (one(left[0], right[1]) + one(left[1], right[0]))


def square3(parts):
    high, low = parts
    mixed = lax.dot_general(high, low, NN, preferred_element_type=F32)
    return lax.dot_general(high, high, NN, preferred_element_type=F32) + (mixed + jnp.transpose(mixed))


def call(kernel, name, out_shape, flops, **kwargs):
    return pl.pallas_call(
        kernel,
        out_shape=out_shape,
        compiler_params=pltpu.CompilerParams(vmem_limit_bytes=VMEM_BYTES),
        cost_estimate=pl.CostEstimate(flops=flops, bytes_accessed=2**22, transcendentals=0),
        name=name,
        **kwargs,
    )


VMEM = pl.BlockSpec(memory_space=pltpu.VMEM)
HBM = pl.BlockSpec(memory_space=pltpu.HBM)


def two_steps(e1, e2, o, eye):
    op, e1p, e2p = split(o), split(e1), split(e2)
    d1 = (eye - square3(e1p)) - dot3(op, op, NT)
    d2 = (eye - square3(e2p)) - dot3(op, op, TN)
    w1, w2 = weights(d1, d2, eye)
    w1, w2 = split(w1), split(w2)
    o = dot3(w1, op, NN)
    return dot3(w1, e1p, NN), dot3(w2, e2p, NN), o


def weights(d1, d2, eye):
    d1p, d2p = split(d1), split(d2)
    q1 = square3(d1p)
    q2 = square3(d2p)
    i1 = split(0.375 * eye + 0.3125 * d1 + 0.0625 * q1)
    i2 = split(0.375 * eye + 0.3125 * d2 + 0.0625 * q2)
    w1 = eye + 0.5 * d1 + dot3(split(q1), i1, NN)
    w2 = eye + 0.5 * d2 + dot3(split(q2), i2, NN)
    return w1, w2


def rotation_kernel(flag_ref, packed_ref, *outs):
    move_ref, stay_ref = outs if len(outs) == 2 else (outs[0].at[:PAIR], outs[0].at[PAIR:])
    left = [packed_ref[CHUNK * k:CHUNK * k + 8, :] for k in range(SLABS)]
    right = [packed_ref[CHUNK * k + 8:CHUNK * k + 16, :] for k in range(SLABS)]
    cross = jnp.concatenate([jnp.concatenate(left, 0), jnp.concatenate(right, 0)], 1)
    norms = packed_ref[16:20, :]
    for k in range(1, SLABS):
        norms = norms + packed_ref[CHUNK * k + 16:CHUNK * k + 20, :]
    norm_a = jnp.concatenate([norms[0:1], norms[1:2]], 1)
    norm_m = jnp.concatenate([norms[2:3], norms[3:4]], 1)
    rows = lax.broadcasted_iota(jnp.int32, (HALF, HALF), 0)
    cols = lax.broadcasted_iota(jnp.int32, (HALF, HALF), 1)
    eye = (rows == cols).astype(F32)
    norm_a = jnp.transpose(jnp.broadcast_to(norm_a, (HALF, HALF)))
    diff = norm_a - norm_m
    total = norm_a + norm_m
    skew = -cross * diff / (diff * diff + 0.25 * total * total + EPS)
    scale = 1.0 / (4.0 * jnp.sqrt(PAIR + 2.0 * jnp.sum(skew * skew, keepdims=True)))
    start = scale * skew
    parts = split(start)
    own = (1.0 - scale * scale) * eye
    w1, w2 = weights(own - dot3(parts, parts, NT), own - dot3(parts, parts, TN), eye)
    e1, e2, o = scale * w1, scale * w2, dot3(split(w1), parts, NN)
    for _ in range(5):
        e1, e2, o = two_steps(e1, e2, o, eye)
    minus_ot = -jnp.transpose(o)

    @pl.when(flag_ref[0] == 1)
    def _():
        move_ref[:HALF, :] = e1
        move_ref[HALF:, :] = minus_ot
        stay_ref[:HALF, :] = o
        stay_ref[HALF:, :] = e2

    @pl.when(flag_ref[0] != 1)
    def _():
        stay_ref[:HALF, :] = e1
        stay_ref[HALF:, :] = minus_ot
        move_ref[:HALF, :] = o
        move_ref[HALF:, :] = e2


def rotation(flag, packed, rows):
    return call(
        rotation_kernel,
        "rotation",
        [jax.ShapeDtypeStruct((n, HALF), F32) for n in rows],
        10**10,
        in_specs=[pl.BlockSpec(memory_space=pltpu.SMEM), VMEM],
        out_specs=[VMEM] * len(rows),
    )(flag, packed)


def pack(packed_ref, value):
    width = value.shape[1]
    per = 8 * width // 128
    for k in range(SLABS):
        for b in range(width // 128):
            packed_ref[per * k + 8 * b:per * k + 8 * b + 8, :] = value[8 * k:8 * k + 8, 128 * b:128 * b + 128]


def row_tiles(ref, tile):
    return [pl.ds(start, tile) for start in range(0, ref.shape[0], tile)]


def squares(x):
    return jnp.sum(x.reshape(-1, 8, x.shape[1]) ** 2, axis=0)


def first_kernel(x_ref, packed_ref, norm_ref):
    total, norm = 0.0, 0.0
    for rows in row_tiles(x_ref, 256):
        x = x_ref[rows, :]
        total += dot3(split(x[:, :HALF]), split(x[:, HALF:]), TN)
        norm += squares(x)
    pack(packed_ref, total)
    norm_ref[...] = jnp.concatenate([norm[:, :HALF], norm[:, HALF:]], 0)


def first_inner(x):
    return call(
        first_kernel,
        "first_inner",
        (jax.ShapeDtypeStruct((HALF * HALF // 128, 128), F32), jax.ShapeDtypeStruct((16, HALF), F32)),
        6 * x.shape[0] * HALF * HALF,
        in_specs=[VMEM],
        out_specs=[VMEM] * 2,
    )(x)


def meet_kernel(x_ref, q_ref, left_ref, a_ref, norm_ref, packed_ref, held_ref, sem):
    copy = pltpu.make_async_copy(left_ref, held_ref, sem)
    copy.start()
    q = split(q_ref[PAIR:, :])
    norm, total = 0.0, 0.0
    for rows in row_tiles(x_ref, 512):
        a = dot3(split(x_ref[rows, :]), q, NN)
        a_ref[rows, :] = a
        norm += squares(a)
    norm_ref[...] = norm
    copy.wait()
    for rows in row_tiles(x_ref, 512):
        total += dot3(split(a_ref[rows, :]), split(held_ref[rows, :]), TN)
    pack(packed_ref, total)


def meet(x, q, left):
    rows = x.shape[0]
    return call(
        meet_kernel,
        "meet",
        (
            jax.ShapeDtypeStruct((rows, HALF), F32),
            jax.ShapeDtypeStruct((8, HALF), F32),
            jax.ShapeDtypeStruct((HALF * PAIR // 128, 128), F32),
        ),
        12 * rows * PAIR * HALF,
        in_specs=[VMEM, VMEM, HBM],
        out_specs=[VMEM] * 3,
        scratch_shapes=[pltpu.VMEM((rows, PAIR), F32), pltpu.SemaphoreType.DMA],
    )(x, q, left)


def fill(out_ref, cross, norm_a, norm_m):
    norm_a = jnp.sum(norm_a, axis=0, keepdims=True)
    norm_m = jnp.sum(norm_m, axis=0, keepdims=True)
    chunk = jnp.concatenate(
        [cross[:, :128], cross[:, 128:], norm_a[:, :128], norm_a[:, 128:], norm_m[:, :128], norm_m[:, 128:]], 0
    )
    for k in range(SLABS):
        out_ref[CHUNK * k:CHUNK * k + CHUNK, :] = chunk


def share_kernel(parts_ref, norm_ref, out_ref):
    total = parts_ref[0:16, :]
    for k in range(1, SLABS):
        total = total + parts_ref[16 * k:16 * k + 16, :]
    cross = jnp.concatenate([total[:8], total[8:]], 1)
    fill(out_ref, cross, norm_ref[:8, :], norm_ref[8:, :])


def project_kernel(parts_ref, high_ref, low_ref, norm_a_ref, norm_m_ref, out_ref):
    total = parts_ref[0:32, :]
    for k in range(1, SLABS):
        total = total + parts_ref[32 * k:32 * k + 32, :]
    wide = jnp.concatenate([total[8 * b:8 * b + 8] for b in range(4)], 1)
    wide = jnp.concatenate([wide, wide], 0)
    cross = dot3(split(wide), (high_ref[...], low_ref[...]), NN)[:8]
    fill(out_ref, cross, norm_a_ref[...], norm_m_ref[...])


def payload(kernel, *arrays):
    out = jax.ShapeDtypeStruct((SLABS * CHUNK, 128), F32)
    return call(kernel, "payload", out, 10**7, in_specs=[VMEM] * len(arrays), out_specs=VMEM)(*arrays)


def turn_kernel(first, x_ref, q_ref, out_ref, *refs):
    held_ref, sem = refs[-2:]
    copy = pltpu.make_async_copy(x_ref, held_ref, sem)
    copy.start()
    q = split(q_ref[first:first + PAIR, :])
    copy.wait()
    norm = 0.0
    for rows in row_tiles(held_ref, 512):
        out = dot3(split(held_ref[rows, :]), q, NN)
        out_ref[rows, :] = out
        norm += squares(out)
    if len(refs) > 2:
        norm_ref, high_ref, low_ref = refs[:3]
        norm_ref[...] = norm
        high_ref[...], low_ref[...] = q


def turn(x, q, first, more):
    rows = x.shape[0]
    extra = (
        jax.ShapeDtypeStruct((8, HALF), F32),
        jax.ShapeDtypeStruct((PAIR, HALF), BF16),
        jax.ShapeDtypeStruct((PAIR, HALF), BF16),
    )
    out = (jax.ShapeDtypeStruct((rows, HALF), F32),) + (extra if more else ())
    return call(
        lambda *refs: turn_kernel(first, *refs),
        "turn",
        out,
        6 * rows * PAIR * HALF,
        in_specs=[HBM, VMEM],
        out_specs=(VMEM,) * len(out),
        scratch_shapes=[pltpu.VMEM((rows, PAIR), F32), pltpu.SemaphoreType.DMA],
    )(x, q)


def last_kernel(block, a_ref, m_ref, q_ref, *refs):
    out_ref, came_ref, held_ref, in_sem, out_sems = refs[-5:]
    copy = pltpu.make_async_copy(m_ref, came_ref, in_sem)
    copy.start()
    qa, qm = split(q_ref[:HALF, :]), split(q_ref[HALF:, :])
    for rows in row_tiles(a_ref, 512):
        held_ref[rows, :] = dot3(split(a_ref[rows, :]), qa, NN)
    copy.wait()
    outs = []
    for i, rows in enumerate(row_tiles(a_ref, 512)):
        held_ref[rows, :] += dot3(split(came_ref[rows, :]), qm, NN)
        there = out_ref.at[rows, pl.ds(HALF * block, HALF)]
        outs.append(pltpu.make_async_copy(held_ref.at[rows], there, out_sems.at[i]))
        outs[-1].start()
    for copy in outs:
        copy.wait()


def last(a, m, q, block, onto=None):
    rows = a.shape[0]
    extra = () if onto is None else (onto,)
    held = pltpu.VMEM((rows, HALF), F32)
    return call(
        lambda *refs: last_kernel(block, *refs),
        "last",
        jax.ShapeDtypeStruct((rows, PAIR), F32),
        6 * rows * PAIR * HALF,
        in_specs=[VMEM, HBM, VMEM] + [HBM] * len(extra),
        out_specs=HBM,
        scratch_shapes=[held, held, pltpu.SemaphoreType.DMA, pltpu.SemaphoreType.DMA((rows // 512,))],
        input_output_aliases={3: 0} if extra else {},
    )(a, m, q, *extra)


def passed_along(value):
    count = lax.axis_size("blk")
    return lax.ppermute(value, "blk", [(source, (source + 1) % count) for source in range(count)])


def exchanged(packed, shape):
    return lax.all_to_all(packed.reshape(SLABS, *shape), "slab", 0, 0).reshape(packed.shape)


def local(columns, movers):
    left_columns = passed_along(columns)

    cross, norms = first_inner(columns)
    parts = exchanged(cross, (16, 128))
    packed = exchanged(payload(share_kernel, parts, norms), (CHUNK // 2, 2, 128))
    (both,) = rotation(movers[0], packed, (2 * PAIR,))

    left_both = passed_along(both)
    a, norm_a, cross = meet(columns, both, left_columns)
    parts = exchanged(cross, (32, 128))
    m, norm_m, high, low = turn(left_columns, left_both, 0, True)
    left_m = passed_along(m)
    packed = exchanged(payload(project_kernel, parts, high, low, norm_a, norm_m), (CHUNK // 2, 2, 128))
    move, stay = rotation(movers[1], packed, (PAIR, PAIR))

    left_move = passed_along(move)
    (left_a,) = turn(left_columns, left_both, PAIR, False)
    out = last(a, m, stay, 0)
    return last(left_a, left_m, left_move, 1, out)


def solution(mesh):
    placed = (P("slab", "blk"), P(None, "blk"))
    return jax.shard_map(
        local, mesh=mesh, in_specs=placed, out_specs=P("slab", "blk"), check_vma=False
    )
```

time: 141 us -> 134 us (0.950)
  Pallas kernels: 53.8 us -> 49.2 us
  local copies, waits for them, and re-layouts: 4.89 us -> 2.88 us
    pallas_call x11 -> x10, Pallas kernels: 53.8 us -> 49.2 us  [the longest x2 20.4 us: rotation(): call(rotation_kernel, 'rotation', [jax.ShapeDtypeStruct((n, HALF), F32) f...]
    ppermute x4, waiting for transfers between devices: 0.01 us -> 2.07 us  [passed_along(): lax.ppermute(value, 'blk', [(source, (source + 1) % count) for source in...]
    slice x2 -> x1, local copies, waits for them, and re-layouts: 2.66 us -> 0.65 us  [local(): move, stay = rotation(movers[1], packed, (PAIR, PAIR))]
    all_to_all x2, waiting for transfers between devices: 20.3 us -> 18.7 us  [exchanged(): lax.all_to_all(packed.reshape(SLABS, *shape), 'slab', 0, 0)]
  transfers between devices with their start and end apart: 6 -> 6, of which waited for: 2 -> 3; matrix products, arithmetic and copies ran while one was open for 3% -> 0% of each run, Pallas kernels for 35% -> 34%
where the time goes in v3:
time: 134 us; the launch traced here: 133 us
  Pallas kernels  49.2 us (37%)
  blocking collectives  41.1 us (31%)
  waiting for transfers between devices  20.7 us (15%)
  starting transfers between devices  19.2 us (14%)
  local copies, waits for them, and re-layouts  2.88 us (2%)
    all_to_all x2, blocking collectives, exchanged(): lax.all_to_all(packed.reshape(SLABS, *shape), 'slab', 0, 0)  41.1 us
    pallas_call x2, Pallas kernels, rotation(): call(rotation_kernel, 'rotation', [jax.ShapeDtypeStruct((n, HALF), F32) f...  20.4 us
    all_to_all x2, waiting for transfers between devices, exchanged(): lax.all_to_all(packed.reshape(SLABS, *shape), 'slab', 0, 0)  18.7 us
    pallas_call x2, Pallas kernels, turn(): call(lambda *refs: turn_kernel(first, *refs), 'turn', out, 6 * rows * PAI...  11.8 us
    ppermute x4, starting transfers between devices, passed_along(): lax.ppermute(value, 'blk', [(source, (source + 1) % count) for source in...  11.4 us
    pallas_call x2, Pallas kernels, last(): call(lambda *refs: last_kernel(block, *refs), 'last', jax.ShapeDtypeStruc...  8.66 us
    all_to_all x2, starting transfers between devices, exchanged(): lax.all_to_all(packed.reshape(SLABS, *shape), 'slab', 0, 0)  7.78 us
    pallas_call x1, Pallas kernels, meet(): call(meet_kernel, 'meet', (jax.ShapeDtypeStruct((rows, HALF), F32), jax.S...  6.08 us
  transfers between devices with their start and end apart: 6, of which 3 were waited for; matrix products, arithmetic and copies ran while one was open for 0% of the time, Pallas kernels for 34%

profile of v3, /device:TPU:1, one launch (start us, length us, event | category | flops | bytes accessed | tf_op | source)
XLA Modules:
  0.0 133.3 jit_solution(6577118806001271373)
XLA Ops:
  0.0 2.7 %collective-permute-start = (f32[2048,512]{1,0:T(8,128)}, f32[2048,512]{1,0:T(8,128)}, u32[]{:S(2)}, u32[]{:S(2)}) collective-permute-start(f32[2048,512]{1,0:T(8,128)} %x_ref.3), channel_id=1, source_target_pairs={{0,1},{1,2},{2,3},{3,4},{4,5},{5,6},{6,7},{7,0},{8,9},{9,10},{10,1... | collective-permute-start | bytes 12582920 | tf_op jit(solution)/shard_map/ppermute | solution.py:304
  2.7 0.0 copy-start
  2.7 2.2 %copy-done = f32[2048,512]{1,0:T(8,128)S(1)} copy-done((f32[2048,512]{1,0:T(8,128)S(1)}, f32[2048,512]{1,0:T(8,128)}, u32[]{:S(2)}) %copy-start) | copy-done | bytes 4194328
  4.9 0.0 copy-start.2
  4.9 1.1 first_inner.1
  6.0 23.5 %all_to_all.20 = f32[32,16,128]{2,1,0:T(8,128)S(1)} all-to-all(f32[32,16,128]{2,1,0:T(8,128)S(1)} %bitcast.15), channel_id=1, replica_groups=mesh['slab'=32,'blk'=8] {'slab'}, dimensions={0} | all-to-all | bytes 524288 | tf_op jit(solution)/shard_map/all_to_all | solution.py:308
  29.6 0.8 payload.2
  30.3 3.9 %all-to-all-start.1 = ((f32[32,10,2,128]{3,2,1,0:T(2,128)}), f32[32,10,2,128]{3,2,1,0:T(2,128)S(1)}, u32[]{:S(2)}, u32[]{:S(2)}) async-start(f32[32,10,2,128]{3,2,1,0:T(2,128)} %bitcast.3), calls=%async_computation.1 | async-start | bytes 655360 | tf_op jit(solution)/shard_map/all_to_all | solution.py:308
  34.2 0.0 copy-done.2
  34.2 0.7 fusion
  34.9 12.6 %all-to-all-done.1 = f32[32,10,2,128]{3,2,1,0:T(2,128)S(1)} async-done(((f32[32,10,2,128]{3,2,1,0:T(2,128)}), f32[32,10,2,128]{3,2,1,0:T(2,128)S(1)}, u32[]{:S(2)}, u32[]{:S(2)}) %all-to-all-start.1) | async-done | bytes 327712 | tf_op jit(solution)/shard_map/all_to_all | solution.py:308
  47.5 0.0 copy-start.1
  47.5 10.7 %rotation.2.q_ref = f32[1024,256]{1,0:T(8,128)} custom-call(s32[1]{0:T(128)} %bitcast.flag_ref, f32[640,128]{1,0:T(8,128)S(1)} %bitcast.13), custom_call_target="tpu_custom_call" | custom-call | flops 10000000000 | bytes 4194304 | tf_op jit(solution)/shard_map/rotation/pallas_call | solution.py:119
  58.2 3.0 %collective-permute-start.1 = (f32[1024,256]{1,0:T(8,128)}, f32[1024,256]{1,0:T(8,128)}, u32[]{:S(2)}, u32[]{:S(2)}) collective-permute-start(f32[1024,256]{1,0:T(8,128)} %rotation.2.q_ref), channel_id=1, source_target_pairs={{0,1},{1,2},{2,3},{3,4},{4,5},{5,6},{6,7},{7,0},{8,9},{9,10},{10,1... | collective-permute-start | bytes 3145736 | tf_op jit(solution)/shard_map/ppermute | solution.py:304
  61.2 0.0 collective-permute-done.refs_0_.left_ref
  61.2 0.0 copy-done.1
  61.2 6.1 %meet.1 = (f32[2048,256]{1,0:T(8,128)S(1)}, f32[8,256]{1,0:T(8,128)S(1)}, f32[1024,128]{1,0:T(8,128)}) custom-call(f32[2048,512]{1,0:T(8,128)S(1)} %copy-done.1, f32[1024,256]{1,0:T(8,128)} %rotation.2.q_ref, f32[2048,512]{1,0:T(8,128)} %collective-permute-done.refs_0_.left_ref), custom_call_target="tpu_custom_call" | custom-call | flops 3221225472 | bytes 4194304 | tf_op jit(solution)/shard_map/meet/pallas_call | solution.py:184
  67.3 3.9 %all-to-all-start.2 = ((f32[32,32,128]{2,1,0:T(8,128)}), f32[32,32,128]{2,1,0:T(8,128)S(1)}, u32[]{:S(2)}, u32[]{:S(2)}) async-start(f32[32,32,128]{2,1,0:T(8,128)} %bitcast.6), calls=%async_computation.2 | async-start | bytes 1048576 | tf_op jit(solution)/shard_map/all_to_all | solution.py:308
  71.2 2.1 %collective-permute-done.1.refs_1_ = f32[1024,256]{1,0:T(8,128)} collective-permute-done((f32[1024,256]{1,0:T(8,128)}, f32[1024,256]{1,0:T(8,128)}, u32[]{:S(2)}, u32[]{:S(2)}) %collective-permute-start.1) | collective-permute-done | bytes 1048608 | tf_op jit(solution)/shard_map/ppermute | solution.py:304
  73.3 6.6 %turn.3 = (f32[2048,256]{1,0:T(8,128)}, f32[8,256]{1,0:T(8,128)S(1)}, bf16[512,256]{1,0:T(8,128)(2,1)S(1)}, bf16[512,256]{1,0:T(8,128)(2,1)S(1)}) custom-call(f32[2048,512]{1,0:T(8,128)} %collective-permute-done.refs_0_.left_ref, f32[1024,256]{1,0:T(8,128)} %collective-permute-done.1.refs_1_), custom_call_target="tpu_custom_call" | custom-call | flops 1610612736 | bytes 4194304 | tf_op jit(solution)/shard_map/turn/pallas_call | solution.py:257
  79.9 2.5 %collective-permute-start.2 = (f32[2048,256]{1,0:T(8,128)}, f32[2048,256]{1,0:T(8,128)}, u32[]{:S(2)}, u32[]{:S(2)}) collective-permute-start(f32[2048,256]{1,0:T(8,128)} %get-tuple-element.18.refs_1_), channel_id=1, source_target_pairs={{0,1},{1,2},{2,3},{3,4},{4,5},{5,6},{6,7},{7,0},{8,9},{9,10},{10,1... | collective-permute-start | bytes 6291464 | tf_op jit(solution)/shard_map/ppermute | solution.py:304
  82.4 6.0 %all-to-all-done.2 = f32[32,32,128]{2,1,0:T(8,128)S(1)} async-done(((f32[32,32,128]{2,1,0:T(8,128)}), f32[32,32,128]{2,1,0:T(8,128)S(1)}, u32[]{:S(2)}, u32[]{:S(2)}) %all-to-all-start.2) | async-done | bytes 524320 | tf_op jit(solution)/shard_map/all_to_all | solution.py:308
  88.4 0.3 payload.3
  88.7 17.6 %all_to_all.21 = f32[32,10,2,128]{3,2,1,0:T(2,128)S(1)} all-to-all(f32[32,10,2,128]{3,2,1,0:T(2,128)S(1)} %bitcast.11), channel_id=1, replica_groups=mesh['slab'=32,'blk'=8] {'slab'}, dimensions={0} | all-to-all | bytes 655360 | tf_op jit(solution)/shard_map/all_to_all | solution.py:308
  106.3 9.7 %rotation.3 = (f32[512,256]{1,0:T(8,128)S(1)}, f32[512,256]{1,0:T(8,128)S(1)}) custom-call(s32[1]{0:T(128)} %bitcast.5.flag_ref, f32[640,128]{1,0:T(8,128)S(1)} %bitcast.14), custom_call_target="tpu_custom_call" | custom-call | flops 10000000000 | bytes 4194304 | tf_op jit(solution)/shard_map/rotation/pallas_call | solution.py:119
  116.0 3.2 %collective-permute-start.3 = (f32[512,256]{1,0:T(8,128)S(1)}, f32[512,256]{1,0:T(8,128)S(1)}, u32[]{:S(2)}, u32[]{:S(2)}) collective-permute-start(f32[512,256]{1,0:T(8,128)S(1)} %get-tuple-element.24), channel_id=1, source_target_pairs={{0,1},{1,2},{2,3},{3,4},{4,5},{5,6},{6,7},{7,0},{8,9},{9,10},{10,1... | collective-permute-start | bytes 1572872 | tf_op jit(solution)/shard_map/ppermute | solution.py:304
  119.3 5.2 %turn.2.refs_0_ = f32[2048,256]{1,0:T(8,128)S(1)} custom-call(f32[2048,512]{1,0:T(8,128)} %collective-permute-done.refs_0_.left_ref, f32[1024,256]{1,0:T(8,128)} %collective-permute-done.1.refs_1_), custom_call_target="tpu_custom_call" | custom-call | flops 1610612736 | bytes 4194304 | tf_op jit(solution)/shard_map/turn/pallas_call | solution.py:257
  124.5 4.3 %last.2.refs_3_ = f32[2048,512]{1,0:T(8,128)} custom-call(f32[2048,256]{1,0:T(8,128)S(1)} %get-tuple-element.25.refs_0_, f32[2048,256]{1,0:T(8,128)} %get-tuple-element.18.refs_1_, f32[512,256]{1,0:T(8,128)S(1)} %get-tuple-element.26.refs_2_), custom_call_target="tpu_custom_call" | custom-call | flops 1610612736 | bytes 4194304 | tf_op jit(solution)/shard_map/last/pallas_call | solution.py:290
  128.8 0.0 collective-permute-done.2.refs_1_
  128.8 0.0 collective-permute-done.3.refs_2_
  128.8 4.3 %last.3 = f32[2048,512]{1,0:T(8,128)} custom-call(f32[2048,256]{1,0:T(8,128)S(1)} %turn.2.refs_0_, f32[2048,256]{1,0:T(8,128)} %collective-permute-done.2.refs_1_, f32[512,256]{1,0:T(8,128)S(1)} %collective-permute-done.3.refs_2_, f32[2048,512]{1,0:T(8,128)} %last.2.refs_3_), custom_call_target="tpu_custom_call", output_to_operand_aliasing={{}: (3, {})} | custom-call | flops 1610612736 | bytes 4194304 | tf_op jit(solution)/shard_map/last/pallas_call | solution.py:290
Async XLA Ops:
  0.0 61.2 %collective-permute-start = (f32[2048,512]{1,0:T(8,128)}, f32[2048,512]{1,0:T(8,128)}, u32[]{:S(2)}, u32[]{:S(2)}) collective-permute-start(f32[2048,512]{1,0:T(8,128)} %x_ref.3), channel_id=1, source_target_pairs={{0,1},{1,2},{2,3},{3,4},{4,5},{5,6},{6,7},{7,0},{8,9},{9,10},{10,1... | collective-permute-start | bytes 12582920 | tf_op jit(solution)/shard_map/ppermute | solution.py:304
  2.7 2.2 %copy-start = (f32[2048,512]{1,0:T(8,128)S(1)}, f32[2048,512]{1,0:T(8,128)}, u32[]{:S(2)}) copy-start(f32[2048,512]{1,0:T(8,128)} %x_ref.3) | copy-start | bytes 12582916
  4.9 29.3 %copy-start.2 = (s32[2,1]{0,1:T(1,128)S(1)}, s32[2,1]{0,1:T(1,128)}, u32[]{:S(2)}) copy-start(s32[2,1]{0,1:T(1,128)} %param.3) | copy-start | bytes 28
  30.3 17.2 %all-to-all-start.1 = ((f32[32,10,2,128]{3,2,1,0:T(2,128)}), f32[32,10,2,128]{3,2,1,0:T(2,128)S(1)}, u32[]{:S(2)}, u32[]{:S(2)}) async-start(f32[32,10,2,128]{3,2,1,0:T(2,128)} %bitcast.3), calls=%async_computation.1 | async-start | bytes 655360 | tf_op jit(solution)/shard_map/all_to_all | solution.py:308
  47.5 13.7 %copy-start.1 = (f32[2048,512]{1,0:T(8,128)S(1)}, f32[2048,512]{1,0:T(8,128)}, u32[]{:S(2)}) copy-start(f32[2048,512]{1,0:T(8,128)} %x_ref.3) | copy-start | bytes 12582916
  58.2 15.1 %collective-permute-start.1 = (f32[1024,256]{1,0:T(8,128)}, f32[1024,256]{1,0:T(8,128)}, u32[]{:S(2)}, u32[]{:S(2)}) collective-permute-start(f32[1024,256]{1,0:T(8,128)} %rotation.2.q_ref), channel_id=1, source_target_pairs={{0,1},{1,2},{2,3},{3,4},{4,5},{5,6},{6,7},{7,0},{8,9},{9,10},{10,1... | collective-permute-start | bytes 3145736 | tf_op jit(solution)/shard_map/ppermute | solution.py:304
  67.3 21.1 %all-to-all-start.2 = ((f32[32,32,128]{2,1,0:T(8,128)}), f32[32,32,128]{2,1,0:T(8,128)S(1)}, u32[]{:S(2)}, u32[]{:S(2)}) async-start(f32[32,32,128]{2,1,0:T(8,128)} %bitcast.6), calls=%async_computation.2 | async-start | bytes 1048576 | tf_op jit(solution)/shard_map/all_to_all | solution.py:308
  79.9 48.9 %collective-permute-start.2 = (f32[2048,256]{1,0:T(8,128)}, f32[2048,256]{1,0:T(8,128)}, u32[]{:S(2)}, u32[]{:S(2)}) collective-permute-start(f32[2048,256]{1,0:T(8,128)} %get-tuple-element.18.refs_1_), channel_id=1, source_target_pairs={{0,1},{1,2},{2,3},{3,4},{4,5},{5,6},{6,7},{7,0},{8,9},{9,10},{10,1... | collective-permute-start | bytes 6291464 | tf_op jit(solution)/shard_map/ppermute | solution.py:304
  116.0 12.8 %collective-permute-start.3 = (f32[512,256]{1,0:T(8,128)S(1)}, f32[512,256]{1,0:T(8,128)S(1)}, u32[]{:S(2)}, u32[]{:S(2)}) collective-permute-start(f32[512,256]{1,0:T(8,128)S(1)} %get-tuple-element.24), channel_id=1, source_target_pairs={{0,1},{1,2},{2,3},{3,4},{4,5},{5,6},{6,7},{7,0},{8,9},{9,10},{10,1... | collective-permute-start | bytes 1572872 | tf_op jit(solution)/shard_map/ppermute | solution.py:304

commit v4 on v3

--- a/solution.py
+++ b/solution.py
@@ -10,7 +10,7 @@
 SLABS = 32
 CHUNK = 20
 EPS = 1e-6
-VMEM_BYTES = 20 * 2**20
+VMEM_BYTES = 24 * 2**20
 F32 = jnp.float32
 BF16 = jnp.bfloat16
 NN = (((1,), (0,)), ((), ()))
@@ -52,6 +52,18 @@
 HBM = pl.BlockSpec(memory_space=pltpu.HBM)
 
 
+def in_hbm(x):
+    return pltpu.with_memory_space_constraint(x, pltpu.HBM)
+
+
+def in_vmem(x):
+    return pltpu.with_memory_space_constraint(x, pltpu.VMEM)
+
+
+def row_tiles(ref, tile):
+    return [pl.ds(start, tile) for start in range(0, ref.shape[0], tile)]
+
+
 def two_steps(e1, e2, o, eye):
     op, e1p, e2p = split(o), split(e1), split(e2)
     d1 = (eye - square3(e1p)) - dot3(op, op, NT)
@@ -73,8 +85,7 @@
     return w1, w2
 
 
-def rotation_kernel(flag_ref, packed_ref, *outs):
-    move_ref, stay_ref = outs if len(outs) == 2 else (outs[0].at[:PAIR], outs[0].at[PAIR:])
+def rotation_kernel(index, movers_ref, packed_ref, move_ref, stay_ref):
     left = [packed_ref[CHUNK * k:CHUNK * k + 8, :] for k in range(SLABS)]
     right = [packed_ref[CHUNK * k + 8:CHUNK * k + 16, :] for k in range(SLABS)]
     cross = jnp.concatenate([jnp.concatenate(left, 0), jnp.concatenate(right, 0)], 1)
@@ -100,30 +111,34 @@
         e1, e2, o = two_steps(e1, e2, o, eye)
     minus_ot = -jnp.transpose(o)
 
-    @pl.when(flag_ref[0] == 1)
+    @pl.when(movers_ref[index] == 1)
     def _():
         move_ref[:HALF, :] = e1
-        move_ref[HALF:, :] = minus_ot
+        move_ref[HALF:PAIR, :] = minus_ot
         stay_ref[:HALF, :] = o
         stay_ref[HALF:, :] = e2
 
-    @pl.when(flag_ref[0] != 1)
+    @pl.when(movers_ref[index] != 1)
     def _():
         stay_ref[:HALF, :] = e1
         stay_ref[HALF:, :] = minus_ot
         move_ref[:HALF, :] = o
-        move_ref[HALF:, :] = e2
-
-
-def rotation(flag, packed, rows):
-    return call(
-        rotation_kernel,
+        move_ref[HALF:PAIR, :] = e2
+
+    if move_ref.shape[0] > PAIR:
+        move_ref[PAIR:, :] = stay_ref[...]
+
+
+def rotation(index, movers, packed, rows=PAIR):
+    sizes = (rows, PAIR)
+    return call(
+        lambda *refs: rotation_kernel(index, *refs),
         "rotation",
-        [jax.ShapeDtypeStruct((n, HALF), F32) for n in rows],
+        [jax.ShapeDtypeStruct((n, HALF), F32) for n in sizes],
         10**10,
         in_specs=[pl.BlockSpec(memory_space=pltpu.SMEM), VMEM],
-        out_specs=[VMEM] * len(rows),
-    )(flag, packed)
+        out_specs=[VMEM] * 2,
+    )(movers, packed)
 
 
 def pack(packed_ref, value):
@@ -132,10 +147,6 @@
     for k in range(SLABS):
         for b in range(width // 128):
             packed_ref[per * k + 8 * b:per * k + 8 * b + 8, :] = value[8 * k:8 * k + 8, 128 * b:128 * b + 128]
-
-
-def row_tiles(ref, tile):
-    return [pl.ds(start, tile) for start in range(0, ref.shape[0], tile)]
 
 
 def squares(x):
@@ -160,22 +171,19 @@
         6 * x.shape[0] * HALF * HALF,
         in_specs=[VMEM],
         out_specs=[VMEM] * 2,
-    )(x)
-
-
-def meet_kernel(x_ref, q_ref, left_ref, a_ref, norm_ref, packed_ref, held_ref, sem):
-    copy = pltpu.make_async_copy(left_ref, held_ref, sem)
-    copy.start()
-    q = split(q_ref[PAIR:, :])
+    )(in_vmem(x))
+
+
+def meet_kernel(x_ref, q_ref, left_ref, a_ref, norm_ref, packed_ref):
+    q = split(q_ref[...])
     norm, total = 0.0, 0.0
     for rows in row_tiles(x_ref, 512):
         a = dot3(split(x_ref[rows, :]), q, NN)
         a_ref[rows, :] = a
         norm += squares(a)
     norm_ref[...] = norm
-    copy.wait()
     for rows in row_tiles(x_ref, 512):
-        total += dot3(split(a_ref[rows, :]), split(held_ref[rows, :]), TN)
+        total += dot3(split(a_ref[rows, :]), split(left_ref[rows, :]), TN)
     pack(packed_ref, total)
 
 
@@ -190,10 +198,9 @@
             jax.ShapeDtypeStruct((HALF * PAIR // 128, 128), F32),
         ),
         12 * rows * PAIR * HALF,
-        in_specs=[VMEM, VMEM, HBM],
+        in_specs=[VMEM] * 3,
         out_specs=[VMEM] * 3,
-        scratch_shapes=[pltpu.VMEM((rows, PAIR), F32), pltpu.SemaphoreType.DMA],
-    )(x, q, left)
+    )(in_vmem(x), q, in_vmem(left))
 
 
 def fill(out_ref, cross, norm_a, norm_m):
@@ -229,74 +236,112 @@
     return call(kernel, "payload", out, 10**7, in_specs=[VMEM] * len(arrays), out_specs=VMEM)(*arrays)
 
 
-def turn_kernel(first, x_ref, q_ref, out_ref, *refs):
-    held_ref, sem = refs[-2:]
-    copy = pltpu.make_async_copy(x_ref, held_ref, sem)
-    copy.start()
-    q = split(q_ref[first:first + PAIR, :])
-    copy.wait()
-    norm = 0.0
-    for rows in row_tiles(held_ref, 512):
-        out = dot3(split(held_ref[rows, :]), q, NN)
-        out_ref[rows, :] = out
+def turn_kernel(x_ref, q_ref, out_ref, norm_ref, high_ref, low_ref, held_ref, turn_ref, out_sems):
+    pltpu.sync_copy(q_ref.at[pl.ds(0, PAIR)], turn_ref)
+    q = split(turn_ref[...])
+    high_ref[...], low_ref[...] = q
+    norm, outs = 0.0, []
+    for i, rows in enumerate(row_tiles(x_ref, 512)):
+        out = dot3(split(x_ref[rows, :]), q, NN)
+        held_ref[rows, :] = out
         norm += squares(out)
-    if len(refs) > 2:
-        norm_ref, high_ref, low_ref = refs[:3]
-        norm_ref[...] = norm
-        high_ref[...], low_ref[...] = q
-
-
-def turn(x, q, first, more):
+        outs.append(pltpu.make_async_copy(held_ref.at[rows], out_ref.at[rows], out_sems.at[i]))
+        outs[-1].start()
+    norm_ref[...] = norm
+    for copy in outs:
+        copy.wait()
+
+
+def turn(x, q):
     rows = x.shape[0]
-    extra = (
-        jax.ShapeDtypeStruct((8, HALF), F32),
-        jax.ShapeDtypeStruct((PAIR, HALF), BF16),
-        jax.ShapeDtypeStruct((PAIR, HALF), BF16),
-    )
-    out = (jax.ShapeDtypeStruct((rows, HALF), F32),) + (extra if more else ())
-    return call(
-        lambda *refs: turn_kernel(first, *refs),
+    return call(
+        turn_kernel,
         "turn",
-        out,
+        (
+            pltpu.HBM((rows, HALF), F32),
+            jax.ShapeDtypeStruct((8, HALF), F32),
+            jax.ShapeDtypeStruct((PAIR, HALF), BF16),
+            jax.ShapeDtypeStruct((PAIR, HALF), BF16),
+        ),
+        30 * 10**9,
+        in_specs=[VMEM, HBM],
+        out_specs=[HBM] + [VMEM] * 3,
+        scratch_shapes=[
+            pltpu.VMEM((rows, HALF), F32),
+            pltpu.VMEM((PAIR, HALF), F32),
+            pltpu.SemaphoreType.DMA((rows // 512,)),
+        ],
+    )(in_vmem(x), in_hbm(q))
+
+
+def ready_kernel(x_ref, m_ref, q_ref, high_ref, low_ref):
+    q = split(q_ref[PAIR:, :])
+    for rows in row_tiles(x_ref, 512):
+        high_ref[rows, HALF:], low_ref[rows, HALF:] = split(m_ref[rows, :])
+        out = dot3(split(x_ref[rows, :]), q, NN)
+        high_ref[rows, :HALF], low_ref[rows, :HALF] = split(out)
+
+
+def ready(x, m, q):
+    rows = x.shape[0]
+    out = jax.ShapeDtypeStruct((rows, PAIR), BF16)
+    return call(
+        ready_kernel,
+        "ready",
+        (out, out),
         6 * rows * PAIR * HALF,
-        in_specs=[HBM, VMEM],
-        out_specs=(VMEM,) * len(out),
-        scratch_shapes=[pltpu.VMEM((rows, PAIR), F32), pltpu.SemaphoreType.DMA],
-    )(x, q)
-
-
-def last_kernel(block, a_ref, m_ref, q_ref, *refs):
-    out_ref, came_ref, held_ref, in_sem, out_sems = refs[-5:]
-    copy = pltpu.make_async_copy(m_ref, came_ref, in_sem)
-    copy.start()
-    qa, qm = split(q_ref[:HALF, :]), split(q_ref[HALF:, :])
-    for rows in row_tiles(a_ref, 512):
-        held_ref[rows, :] = dot3(split(a_ref[rows, :]), qa, NN)
-    copy.wait()
+        in_specs=[VMEM] * 3,
+        out_specs=[VMEM] * 2,
+    )(in_vmem(x), in_vmem(m), in_vmem(q))
+
+
+def right_kernel(high_ref, low_ref, q_ref, onto_ref, out_ref, held_ref, sems):
+    q = split(q_ref[...])
     outs = []
-    for i, rows in enumerate(row_tiles(a_ref, 512)):
-        held_ref[rows, :] += dot3(split(came_ref[rows, :]), qm, NN)
-        there = out_ref.at[rows, pl.ds(HALF * block, HALF)]
-        outs.append(pltpu.make_async_copy(held_ref.at[rows], there, out_sems.at[i]))
+    for i, rows in enumerate(row_tiles(high_ref, 512)):
+        held_ref[rows, :] = dot3((high_ref[rows, :], low_ref[rows, :]), q, NN)
+        outs.append(pltpu.make_async_copy(held_ref.at[rows], out_ref.at[rows, pl.ds(HALF, HALF)], sems.at[i]))
         outs[-1].start()
     for copy in outs:
         copy.wait()
 
 
-def last(a, m, q, block, onto=None):
-    rows = a.shape[0]
-    extra = () if onto is None else (onto,)
-    held = pltpu.VMEM((rows, HALF), F32)
-    return call(
-        lambda *refs: last_kernel(block, *refs),
-        "last",
+def right(high, low, q, onto):
+    rows = high.shape[0]
+    return call(
+        right_kernel,
+        "right",
         jax.ShapeDtypeStruct((rows, PAIR), F32),
         6 * rows * PAIR * HALF,
-        in_specs=[VMEM, HBM, VMEM] + [HBM] * len(extra),
+        in_specs=[VMEM, VMEM, VMEM, HBM],
         out_specs=HBM,
-        scratch_shapes=[held, held, pltpu.SemaphoreType.DMA, pltpu.SemaphoreType.DMA((rows // 512,))],
-        input_output_aliases={3: 0} if extra else {},
-    )(a, m, q, *extra)
+        scratch_shapes=[pltpu.VMEM((rows, HALF), F32), pltpu.SemaphoreType.DMA((rows // 512,))],
+        input_output_aliases={3: 0},
+    )(high, low, q, onto)
+
+
+def left_kernel(a_ref, m_ref, q_ref, out_ref, held_ref, sems):
+    qa, qm = split(q_ref[:HALF, :]), split(q_ref[HALF:, :])
+    outs = []
+    for i, rows in enumerate(row_tiles(a_ref, 512)):
+        held_ref[rows, :] = dot3(split(a_ref[rows, :]), qa, NN) + dot3(split(m_ref[rows, :]), qm, NN)
+        outs.append(pltpu.make_async_copy(held_ref.at[rows], out_ref.at[rows, pl.ds(0, HALF)], sems.at[i]))
+        outs[-1].start()
+    for copy in outs:
+        copy.wait()
+
+
+def left(a, m, q):
+    rows = a.shape[0]
+    return call(
+        left_kernel,
+        "left",
+        jax.ShapeDtypeStruct((rows, PAIR), F32),
+        6 * rows * PAIR * HALF,
+        in_specs=[VMEM] * 3,
+        out_specs=HBM,
+        scratch_shapes=[pltpu.VMEM((rows, HALF), F32), pltpu.SemaphoreType.DMA((rows // 512,))],
+    )(a, in_vmem(m), q)
 
 
 def passed_along(value):
@@ -312,22 +357,23 @@
     left_columns = passed_along(columns)
 
     cross, norms = first_inner(columns)
+    movers, cross = lax.optimization_barrier((movers[:, 0], cross))
     parts = exchanged(cross, (16, 128))
     packed = exchanged(payload(share_kernel, parts, norms), (CHUNK // 2, 2, 128))
-    (both,) = rotation(movers[0], packed, (2 * PAIR,))
+    both, stay = rotation(0, movers, packed, 2 * PAIR)
 
     left_both = passed_along(both)
-    a, norm_a, cross = meet(columns, both, left_columns)
+    a, norm_a, cross = meet(columns, stay, left_columns)
     parts = exchanged(cross, (32, 128))
-    m, norm_m, high, low = turn(left_columns, left_both, 0, True)
+    m, norm_m, high, low = turn(left_columns, left_both)
     left_m = passed_along(m)
     packed = exchanged(payload(project_kernel, parts, high, low, norm_a, norm_m), (CHUNK // 2, 2, 128))
-    move, stay = rotation(movers[1], packed, (PAIR, PAIR))
+    move, stay = rotation(1, movers, packed)
 
     left_move = passed_along(move)
-    (left_a,) = turn(left_columns, left_both, PAIR, False)
-    out = last(a, m, stay, 0)
-    return last(left_a, left_m, left_move, 1, out)
+    left_high, left_low = ready(left_columns, left_m, left_both)
+    out = left(a, m, stay)
+    return right(left_high, left_low, left_move, out)
 
 
 def solution(mesh):

time: 134 us -> 127 us (0.948)
  blocking collectives: 41.1 us -> 57.7 us
  waiting for transfers between devices: 20.7 us -> 8.55 us
  Pallas kernels: 49.2 us -> 40.1 us
  starting transfers between devices: 19.2 us -> 15.3 us
  local copies, waits for them, and re-layouts: 2.88 us -> 4.43 us
    all_to_all x2 -> x3, blocking collectives: 41.1 us -> 57.7 us  [exchanged(): lax.all_to_all(packed.reshape(SLABS, *shape), 'slab', 0, 0)]
    all_to_all x2 -> x1, waiting for transfers between devices: 18.7 us -> 4.88 us  [exchanged(): lax.all_to_all(packed.reshape(SLABS, *shape), 'slab', 0, 0)]
    pallas_call x6, Pallas kernels: 40.9 us -> 34.2 us  [the longest x2 20.2 us: rotation(): call(lambda *refs: rotation_kernel(index, *refs), 'rotation', [jax.ShapeD...]
    all_to_all x2 -> x1, starting transfers between devices: 7.78 us -> 3.89 us  [exchanged(): lax.all_to_all(packed.reshape(SLABS, *shape), 'slab', 0, 0)]
    unnamed x6 -> x14, local copies, waits for them, and re-layouts: 2.23 us -> 4.43 us
    ppermute x4, waiting for transfers between devices: 2.07 us -> 3.67 us  [passed_along(): lax.ppermute(value, 'blk', [(source, (source + 1) % count) for source in...]
    pallas_call x1, Pallas kernels: 6.08 us -> 4.49 us  [meet(): call(meet_kernel, 'meet', (jax.ShapeDtypeStruct((rows, HALF), F32), jax.S...]
  transfers between devices with their start and end apart: 6 -> 5, of which waited for: 3 -> 2; matrix products, arithmetic and copies ran while one was open for 0% -> 0% of each run, Pallas kernels for 34% -> 29%
where the time goes in v4:
time: 127 us; the launch traced here: 126 us
  blocking collectives  57.7 us (45%)
  Pallas kernels  40.1 us (32%)
  starting transfers between devices  15.3 us (12%)
  waiting for transfers between devices  8.55 us (7%)
  local copies, waits for them, and re-layouts  4.43 us (3%)
    all_to_all x3, blocking collectives, exchanged(): lax.all_to_all(packed.reshape(SLABS, *shape), 'slab', 0, 0)  57.7 us
    pallas_call x2, Pallas kernels, rotation(): call(lambda *refs: rotation_kernel(index, *refs), 'rotation', [jax.ShapeD...  20.2 us
    ppermute x4, starting transfers between devices, passed_along(): lax.ppermute(value, 'blk', [(source, (source + 1) % count) for source in...  11.5 us
    all_to_all x1, waiting for transfers between devices, exchanged(): lax.all_to_all(packed.reshape(SLABS, *shape), 'slab', 0, 0)  4.88 us
    pallas_call x1, Pallas kernels, meet(): call(meet_kernel, 'meet', (jax.ShapeDtypeStruct((rows, HALF), F32), jax.S...  4.49 us
    unnamed x14, local copies, waits for them, and re-layouts  4.43 us
    pallas_call x1, Pallas kernels, ready(): call(ready_kernel, 'ready', (out, out), 6 * rows * PAIR * HALF, in_specs=...  4.26 us
    pallas_call x1, Pallas kernels, turn(): call(turn_kernel, 'turn', (pltpu.HBM((rows, HALF), F32), jax.ShapeDtypeSt...  3.97 us
  transfers between devices with their start and end apart: 5, of which 2 were waited for; matrix products, arithmetic and copies ran while one was open for 0% of the time, Pallas kernels for 29%

profile of v4, /device:TPU:1, one launch (start us, length us, event | category | flops | bytes accessed | tf_op | source)
XLA Modules:
  0.0 126.4 jit_solution(10682271392953422032)
XLA Ops:
  0.0 2.7 %collective-permute-start = (f32[2048,512]{1,0:T(8,128)}, f32[2048,512]{1,0:T(8,128)S(1)}, u32[]{:S(2)}, u32[]{:S(2)}) collective-permute-start(f32[2048,512]{1,0:T(8,128)} %x_ref.3), channel_id=1, source_target_pairs={{0,1},{1,2},{2,3},{3,4},{4,5},{5,6},{6,7},{7,0},{8,9},{9,10},{10,1... | collective-permute-start | bytes 12582920 | tf_op jit(solution)/shard_map/ppermute | solution.py:349
  2.7 0.0 copy-start.3
  2.7 2.2 %copy-done.3 = f32[2048,512]{1,0:T(8,128)S(1)} copy-done((f32[2048,512]{1,0:T(8,128)S(1)}, f32[2048,512]{1,0:T(8,128)}, u32[]{:S(2)}) %copy-start.3) | copy-done | bytes 4194328
  4.9 0.0 copy-start.6
  4.9 1.1 first_inner.1
  6.0 23.5 %all_to_all.20 = f32[32,16,128]{2,1,0:T(8,128)S(1)} all-to-all(f32[32,16,128]{2,1,0:T(8,128)S(1)} %bitcast.15), channel_id=1, replica_groups=mesh['slab'=32,'blk'=8] {'slab'}, dimensions={0} | all-to-all | bytes 524288 | tf_op jit(solution)/shard_map/all_to_all | solution.py:353
  29.6 0.1 payload.2
  29.6 16.6 %all_to_all.21 = f32[32,10,2,128]{3,2,1,0:T(2,128)S(1)} all-to-all(f32[32,10,2,128]{3,2,1,0:T(2,128)S(1)} %bitcast.10), channel_id=1, replica_groups=mesh['slab'=32,'blk'=8] {'slab'}, dimensions={0} | all-to-all | bytes 655360 | tf_op jit(solution)/shard_map/all_to_all | solution.py:353
  46.2 0.0 copy-done.6
  46.2 0.0 copy-start.4
  46.2 10.6 %rotation.2 = (f32[1024,256]{1,0:T(8,128)}, f32[512,256]{1,0:T(8,128)S(1)}) custom-call(s32[2]{0:T(128)S(1)} %bitcast.16, f32[640,128]{1,0:T(8,128)S(1)} %bitcast.13), custom_call_target="tpu_custom_call" | custom-call | flops 10000000000 | bytes 4194304 | tf_op jit(solution)/shard_map/rotation/pallas_call | solution.py:134
  56.8 3.1 %collective-permute-start.1 = (f32[1024,256]{1,0:T(8,128)}, f32[1024,256]{1,0:T(8,128)}, u32[]{:S(2)}, u32[]{:S(2)}) collective-permute-start(f32[1024,256]{1,0:T(8,128)} %get-tuple-element.26), channel_id=1, source_target_pairs={{0,1},{1,2},{2,3},{3,4},{4,5},{5,6},{6,7},{7,0},{8,9},{9,10},{10,1... | collective-permute-start | bytes 3145736 | tf_op jit(solution)/shard_map/ppermute | solution.py:349
  59.9 0.0 collective-permute-done.x_ref.left_ref
  60.0 0.0 copy-start
  60.0 0.0 copy-done.4
  60.0 4.5 %meet.1 = (f32[2048,256]{1,0:T(8,128)S(1)}, f32[8,256]{1,0:T(8,128)S(1)}, f32[1024,128]{1,0:T(8,128)}) custom-call(f32[2048,512]{1,0:T(8,128)S(1)} %copy-done.4, f32[512,256]{1,0:T(8,128)S(1)} %get-tuple-element.30.q_ref, f32[2048,512]{1,0:T(8,128)S(1)} %collective-permute-done.x_ref.left_ref), custom_call_target="tpu_custom_call" | custom-call | flops 3221225472 | bytes 4194304 | tf_op jit(solution)/shard_map/meet/pallas_call | solution.py:192
  64.4 0.0 copy-done
  64.4 3.9 %all-to-all-start.2 = ((f32[32,32,128]{2,1,0:T(8,128)}), f32[32,32,128]{2,1,0:T(8,128)S(1)}, u32[]{:S(2)}, u32[]{:S(2)}) async-start(f32[32,32,128]{2,1,0:T(8,128)} %bitcast.5), calls=%async_computation.2 | async-start | bytes 1048576 | tf_op jit(solution)/shard_map/all_to_all | solution.py:353
  68.3 3.7 %collective-permute-done.1.q_ref = f32[1024,256]{1,0:T(8,128)} collective-permute-done((f32[1024,256]{1,0:T(8,128)}, f32[1024,256]{1,0:T(8,128)}, u32[]{:S(2)}, u32[]{:S(2)}) %collective-permute-start.1) | collective-permute-done | bytes 1048608 | tf_op jit(solution)/shard_map/ppermute | solution.py:349
  72.0 0.0 copy-start.1
  72.0 2.2 %copy-done.1 = f32[2048,512]{1,0:T(8,128)S(1)} copy-done((f32[2048,512]{1,0:T(8,128)S(1)}, f32[2048,512]{1,0:T(8,128)}, u32[]{:S(2)}) %copy-start.1) | copy-done | bytes 4194328
  74.2 4.0 %turn.1 = (f32[2048,256]{1,0:T(8,128)}, f32[8,256]{1,0:T(8,128)S(1)}, bf16[512,256]{1,0:T(8,128)(2,1)S(1)}, bf16[512,256]{1,0:T(8,128)(2,1)S(1)}) custom-call(f32[2048,512]{1,0:T(8,128)S(1)} %copy-done.1, f32[1024,256]{1,0:T(8,128)} %collective-permute-done.1.q_ref), custom_call_target="tpu_custom_call" | custom-call | flops 30000001024 | bytes 4194304 | tf_op jit(solution)/shard_map/turn/pallas_call | solution.py:257
  78.2 2.5 %collective-permute-start.2 = (f32[2048,256]{1,0:T(8,128)}, f32[2048,256]{1,0:T(8,128)}, u32[]{:S(2)}, u32[]{:S(2)}) collective-permute-start(f32[2048,256]{1,0:T(8,128)} %get-tuple-element.27.m_ref), channel_id=1, source_target_pairs={{0,1},{1,2},{2,3},{3,4},{4,5},{5,6},{6,7},{7,0},{8,9},{9,10},{10,1... | collective-permute-start | bytes 6291464 | tf_op jit(solution)/shard_map/ppermute | solution.py:349
  80.7 4.9 %all-to-all-done.2 = f32[32,32,128]{2,1,0:T(8,128)S(1)} async-done(((f32[32,32,128]{2,1,0:T(8,128)}), f32[32,32,128]{2,1,0:T(8,128)S(1)}, u32[]{:S(2)}, u32[]{:S(2)}) %all-to-all-start.2) | async-done | bytes 524320 | tf_op jit(solution)/shard_map/all_to_all | solution.py:353
  85.6 0.3 payload.3
  85.8 17.6 %all_to_all.22 = f32[32,10,2,128]{3,2,1,0:T(2,128)S(1)} all-to-all(f32[32,10,2,128]{3,2,1,0:T(2,128)S(1)} %bitcast.11), channel_id=1, replica_groups=mesh['slab'=32,'blk'=8] {'slab'}, dimensions={0} | all-to-all | bytes 655360 | tf_op jit(solution)/shard_map/all_to_all | solution.py:353
  103.4 0.0 copy-start.5
  103.4 9.7 %rotation.3 = (f32[512,256]{1,0:T(8,128)S(1)}, f32[512,256]{1,0:T(8,128)S(1)}) custom-call(s32[2]{0:T(128)S(1)} %bitcast.17, f32[640,128]{1,0:T(8,128)S(1)} %bitcast.14), custom_call_target="tpu_custom_call" | custom-call | flops 10000000000 | bytes 4194304 | tf_op jit(solution)/shard_map/rotation/pallas_call | solution.py:134
  113.1 3.2 %collective-permute-start.3 = (f32[512,256]{1,0:T(8,128)S(1)}, f32[512,256]{1,0:T(8,128)S(1)}, u32[]{:S(2)}, u32[]{:S(2)}) collective-permute-start(f32[512,256]{1,0:T(8,128)S(1)} %get-tuple-element.36), channel_id=1, source_target_pairs={{0,1},{1,2},{2,3},{3,4},{4,5},{5,6},{6,7},{7,0},{8,9},{9,10},{10,1... | collective-permute-start | bytes 1572872 | tf_op jit(solution)/shard_map/ppermute | solution.py:349
  116.2 0.0 copy-done.5
  116.2 0.0 copy-start.2
  116.2 2.9 %left.1.onto_ref = f32[2048,512]{1,0:T(8,128)} custom-call(f32[2048,256]{1,0:T(8,128)S(1)} %get-tuple-element.37.a_ref, f32[2048,256]{1,0:T(8,128)S(1)} %copy-done.5, f32[512,256]{1,0:T(8,128)S(1)} %get-tuple-element.38.q_ref), custom_call_target="tpu_custom_call" | custom-call | flops 1610612736 | bytes 4194304 | tf_op jit(solution)/shard_map/left/pallas_call | solution.py:336
  119.1 0.0 collective-permute-done.2.m_ref
  119.1 0.0 copy-done.2
  119.1 4.3 %ready.1 = (bf16[2048,512]{1,0:T(8,128)(2,1)S(1)}, bf16[2048,512]{1,0:T(8,128)(2,1)S(1)}) custom-call(f32[2048,512]{1,0:T(8,128)S(1)} %copy-done.2, f32[2048,256]{1,0:T(8,128)} %collective-permute-done.2.m_ref, f32[1024,256]{1,0:T(8,128)} %collective-permute-done.1.q_ref), custom_call_target="tpu_custom_call" | custom-call | flops 1610612736 | bytes 4194304 | tf_op jit(solution)/shard_map/ready/pallas_call | solution.py:288
  123.4 0.0 collective-permute-done.3.q_ref
  123.4 2.8 %right.1 = f32[2048,512]{1,0:T(8,128)} custom-call(bf16[2048,512]{1,0:T(8,128)(2,1)S(1)} %get-tuple-element.28.high_ref, bf16[2048,512]{1,0:T(8,128)(2,1)S(1)} %get-tuple-element.29.low_ref, f32[512,256]{1,0:T(8,128)S(1)} %collective-permute-done.3.q_ref, f32[2048,512]{1,0:T(8,128)} %left.1.onto_ref), custom_call_target="tpu_custom_call", output_to_operand_aliasing={{}: (3, {})} | custom-call | flops 1610612736 | bytes 4194304 | tf_op jit(solution)/shard_map/right/pallas_call | solution.py:311
Async XLA Ops:
  0.0 60.0 %collective-permute-start = (f32[2048,512]{1,0:T(8,128)}, f32[2048,512]{1,0:T(8,128)S(1)}, u32[]{:S(2)}, u32[]{:S(2)}) collective-permute-start(f32[2048,512]{1,0:T(8,128)} %x_ref.3), channel_id=1, source_target_pairs={{0,1},{1,2},{2,3},{3,4},{4,5},{5,6},{6,7},{7,0},{8,9},{9,10},{10,1... | collective-permute-start | bytes 12582920 | tf_op jit(solution)/shard_map/ppermute | solution.py:349
  2.7 2.2 %copy-start.3 = (f32[2048,512]{1,0:T(8,128)S(1)}, f32[2048,512]{1,0:T(8,128)}, u32[]{:S(2)}) copy-start(f32[2048,512]{1,0:T(8,128)} %x_ref.3) | copy-start | bytes 12582916
  4.9 41.3 %copy-start.6 = (s32[2,1]{0,1:T(1,128)S(1)}, s32[2,1]{0,1:T(1,128)}, u32[]{:S(2)}) copy-start(s32[2,1]{0,1:T(1,128)} %param.3) | copy-start | bytes 28
  46.2 13.7 %copy-start.4 = (f32[2048,512]{1,0:T(8,128)S(1)}, f32[2048,512]{1,0:T(8,128)}, u32[]{:S(2)}) copy-start(f32[2048,512]{1,0:T(8,128)} %x_ref.3) | copy-start | bytes 12582916
  56.8 15.2 %collective-permute-start.1 = (f32[1024,256]{1,0:T(8,128)}, f32[1024,256]{1,0:T(8,128)}, u32[]{:S(2)}, u32[]{:S(2)}) collective-permute-start(f32[1024,256]{1,0:T(8,128)} %get-tuple-element.26), channel_id=1, source_target_pairs={{0,1},{1,2},{2,3},{3,4},{4,5},{5,6},{6,7},{7,0},{8,9},{9,10},{10,1... | collective-permute-start | bytes 3145736 | tf_op jit(solution)/shard_map/ppermute | solution.py:349
  60.0 4.5 %copy-start = (f32[2048,512]{1,0:T(8,128)}, f32[2048,512]{1,0:T(8,128)S(1)}, u32[]{:S(2)}) copy-start(f32[2048,512]{1,0:T(8,128)S(1)} %collective-permute-done.x_ref.left_ref) | copy-start | bytes 12582916
  64.4 21.1 %all-to-all-start.2 = ((f32[32,32,128]{2,1,0:T(8,128)}), f32[32,32,128]{2,1,0:T(8,128)S(1)}, u32[]{:S(2)}, u32[]{:S(2)}) async-start(f32[32,32,128]{2,1,0:T(8,128)} %bitcast.5), calls=%async_computation.2 | async-start | bytes 1048576 | tf_op jit(solution)/shard_map/all_to_all | solution.py:353
  72.0 2.2 %copy-start.1 = (f32[2048,512]{1,0:T(8,128)S(1)}, f32[2048,512]{1,0:T(8,128)}, u32[]{:S(2)}) copy-start(f32[2048,512]{1,0:T(8,128)} %copy-done) | copy-start | bytes 12582916
  78.2 40.9 %collective-permute-start.2 = (f32[2048,256]{1,0:T(8,128)}, f32[2048,256]{1,0:T(8,128)}, u32[]{:S(2)}, u32[]{:S(2)}) collective-permute-start(f32[2048,256]{1,0:T(8,128)} %get-tuple-element.27.m_ref), channel_id=1, source_target_pairs={{0,1},{1,2},{2,3},{3,4},{4,5},{5,6},{6,7},{7,0},{8,9},{9,10},{10,1... | collective-permute-start | bytes 6291464 | tf_op jit(solution)/shard_map/ppermute | solution.py:349
  103.4 12.8 %copy-start.5 = (f32[2048,256]{1,0:T(8,128)S(1)}, f32[2048,256]{1,0:T(8,128)}, u32[]{:S(2)}) copy-start(f32[2048,256]{1,0:T(8,128)} %get-tuple-element.27.m_ref) | copy-start | bytes 6291460
  113.1 10.3 %collective-permute-start.3 = (f32[512,256]{1,0:T(8,128)S(1)}, f32[512,256]{1,0:T(8,128)S(1)}, u32[]{:S(2)}, u32[]{:S(2)}) collective-permute-start(f32[512,256]{1,0:T(8,128)S(1)} %get-tuple-element.36), channel_id=1, source_target_pairs={{0,1},{1,2},{2,3},{3,4},{4,5},{5,6},{6,7},{7,0},{8,9},{9,10},{10,1... | collective-permute-start | bytes 1572872 | tf_op jit(solution)/shard_map/ppermute | solution.py:349
  116.2 2.9 %copy-start.2 = (f32[2048,512]{1,0:T(8,128)S(1)}, f32[2048,512]{1,0:T(8,128)}, u32[]{:S(2)}) copy-start(f32[2048,512]{1,0:T(8,128)} %copy-done) | copy-start | bytes 12582916

commit v5 on v4

--- a/solution.py
+++ b/solution.py
@@ -64,10 +64,18 @@
     return [pl.ds(start, tile) for start in range(0, ref.shape[0], tile)]
 
 
+def outer3(e, o, dims):
+    def one(a, b, dims):
+        return lax.dot_general(a, b, dims, preferred_element_type=F32)
+
+    mixed = one(e[0], e[1], NN) + one(o[0], o[1], dims)
+    return (one(e[0], e[0], NN) + one(o[0], o[0], dims)) + (mixed + jnp.transpose(mixed))
+
+
 def two_steps(e1, e2, o, eye):
     op, e1p, e2p = split(o), split(e1), split(e2)
-    d1 = (eye - square3(e1p)) - dot3(op, op, NT)
-    d2 = (eye - square3(e2p)) - dot3(op, op, TN)
+    d1 = eye - outer3(e1p, op, NT)
+    d2 = eye - outer3(e2p, op, TN)
     w1, w2 = weights(d1, d2, eye)
     w1, w2 = split(w1), split(w2)
     o = dot3(w1, op, NN)
@@ -85,7 +93,7 @@
     return w1, w2
 
 
-def rotation_kernel(index, movers_ref, packed_ref, move_ref, stay_ref):
+def rotation_kernel(index, movers_ref, packed_ref, *outs):
     left = [packed_ref[CHUNK * k:CHUNK * k + 8, :] for k in range(SLABS)]
     right = [packed_ref[CHUNK * k + 8:CHUNK * k + 16, :] for k in range(SLABS)]
     cross = jnp.concatenate([jnp.concatenate(left, 0), jnp.concatenate(right, 0)], 1)
@@ -97,7 +105,7 @@
     rows = lax.broadcasted_iota(jnp.int32, (HALF, HALF), 0)
     cols = lax.broadcasted_iota(jnp.int32, (HALF, HALF), 1)
     eye = (rows == cols).astype(F32)
-    norm_a = jnp.transpose(jnp.broadcast_to(norm_a, (HALF, HALF)))
+    norm_a = jnp.transpose(jnp.broadcast_to(norm_a, (8, HALF)))[:, :1]
     diff = norm_a - norm_m
     total = norm_a + norm_m
     skew = -cross * diff / (diff * diff + 0.25 * total * total + EPS)
@@ -111,33 +119,34 @@
         e1, e2, o = two_steps(e1, e2, o, eye)
     minus_ot = -jnp.transpose(o)
 
-    @pl.when(movers_ref[index] == 1)
+    firsts = movers_ref[index] == 1
+
+    def put(move_a, move_m, stay_a, stay_m):
+        if len(outs) == 2:
+            for i, block in enumerate((move_a, move_m, stay_a, stay_m)):
+                outs[0][HALF * i:HALF * i + HALF, :] = block
+        else:
+            outs[0][...], outs[1][...] = move_a, move_m
+        outs[-1][:HALF, :] = stay_a
+        outs[-1][HALF:, :] = stay_m
+
+    @pl.when(firsts)
     def _():
-        move_ref[:HALF, :] = e1
-        move_ref[HALF:PAIR, :] = minus_ot
-        stay_ref[:HALF, :] = o
-        stay_ref[HALF:, :] = e2
-
-    @pl.when(movers_ref[index] != 1)
+        put(e1, minus_ot, o, e2)
+
+    @pl.when(jnp.logical_not(firsts))
     def _():
-        stay_ref[:HALF, :] = e1
-        stay_ref[HALF:, :] = minus_ot
-        move_ref[:HALF, :] = o
-        move_ref[HALF:PAIR, :] = e2
-
-    if move_ref.shape[0] > PAIR:
-        move_ref[PAIR:, :] = stay_ref[...]
-
-
-def rotation(index, movers, packed, rows=PAIR):
-    sizes = (rows, PAIR)
+        put(o, e2, e1, minus_ot)
+
+
+def rotation(index, movers, packed, sizes):
     return call(
         lambda *refs: rotation_kernel(index, *refs),
         "rotation",
         [jax.ShapeDtypeStruct((n, HALF), F32) for n in sizes],
         10**10,
         in_specs=[pl.BlockSpec(memory_space=pltpu.SMEM), VMEM],
-        out_specs=[VMEM] * 2,
+        out_specs=[VMEM] * len(sizes),
     )(movers, packed)
 
 
@@ -236,17 +245,23 @@
     return call(kernel, "payload", out, 10**7, in_specs=[VMEM] * len(arrays), out_specs=VMEM)(*arrays)
 
 
-def turn_kernel(x_ref, q_ref, out_ref, norm_ref, high_ref, low_ref, held_ref, turn_ref, out_sems):
-    pltpu.sync_copy(q_ref.at[pl.ds(0, PAIR)], turn_ref)
-    q = split(turn_ref[...])
-    high_ref[...], low_ref[...] = q
+def turn_kernel(
+    x_ref, q_ref, out_ref, norm_ref, high_ref, low_ref, a_high_ref, a_low_ref, held_ref, turn_ref, part_ref, sems
+):
+    pltpu.sync_copy(q_ref, turn_ref)
+    move, stay = split(turn_ref[:PAIR, :]), split(turn_ref[PAIR:, :])
+    high_ref[...], low_ref[...] = move
     norm, outs = 0.0, []
     for i, rows in enumerate(row_tiles(x_ref, 512)):
-        out = dot3(split(x_ref[rows, :]), q, NN)
+        x = split(x_ref[rows, :])
+        out = dot3(x, move, NN)
         held_ref[rows, :] = out
         norm += squares(out)
-        outs.append(pltpu.make_async_copy(held_ref.at[rows], out_ref.at[rows], out_sems.at[i]))
-        outs[-1].start()
+        part_ref[0, rows, :], part_ref[1, rows, :] = split(dot3(x, stay, NN))
+        goes = ((held_ref, out_ref), (part_ref.at[0], a_high_ref), (part_ref.at[1], a_low_ref))
+        for j, (here, there) in enumerate(goes):
+            outs.append(pltpu.make_async_copy(here.at[rows], there.at[rows], sems.at[i, j]))
+            outs[-1].start()
     norm_ref[...] = norm
     for copy in outs:
         copy.wait()
@@ -254,6 +269,7 @@
 
 def turn(x, q):
     rows = x.shape[0]
+    part = pltpu.HBM((rows, HALF), BF16)
     return call(
         turn_kernel,
         "turn",
@@ -262,62 +278,78 @@
             jax.ShapeDtypeStruct((8, HALF), F32),
             jax.ShapeDtypeStruct((PAIR, HALF), BF16),
             jax.ShapeDtypeStruct((PAIR, HALF), BF16),
+            part,
+            part,
         ),
         30 * 10**9,
         in_specs=[VMEM, HBM],
-        out_specs=[HBM] + [VMEM] * 3,
+        out_specs=[HBM] + [VMEM] * 3 + [HBM] * 2,
         scratch_shapes=[
             pltpu.VMEM((rows, HALF), F32),
-            pltpu.VMEM((PAIR, HALF), F32),
-            pltpu.SemaphoreType.DMA((rows // 512,)),
+            pltpu.VMEM((2 * PAIR, HALF), F32),
+            pltpu.VMEM((2, rows, HALF), BF16),
+            pltpu.SemaphoreType.DMA((rows // 512, 3)),
         ],
     )(in_vmem(x), in_hbm(q))
 
 
-def ready_kernel(x_ref, m_ref, q_ref, high_ref, low_ref):
-    q = split(q_ref[PAIR:, :])
-    for rows in row_tiles(x_ref, 512):
-        high_ref[rows, HALF:], low_ref[rows, HALF:] = split(m_ref[rows, :])
-        out = dot3(split(x_ref[rows, :]), q, NN)
-        high_ref[rows, :HALF], low_ref[rows, :HALF] = split(out)
-
-
-def ready(x, m, q):
-    rows = x.shape[0]
-    out = jax.ShapeDtypeStruct((rows, PAIR), BF16)
+def ready_kernel(m_ref, high_ref, low_ref):
+    high_ref[...], low_ref[...] = split(m_ref[...])
+
+
+def ready(m):
+    out = jax.ShapeDtypeStruct(m.shape, BF16)
     return call(
         ready_kernel,
         "ready",
         (out, out),
-        6 * rows * PAIR * HALF,
+        10**6,
+        in_specs=[VMEM],
+        out_specs=[VMEM] * 2,
+    )(in_vmem(m))
+
+
+def right_a_kernel(high_ref, low_ref, q_ref, out_ref):
+    q = split(q_ref[...])
+    for rows in row_tiles(high_ref, 512):
+        out_ref[rows, :] = dot3((high_ref[rows, :], low_ref[rows, :]), q, NN)
+
+
+def right_a(high, low, q):
+    rows = high.shape[0]
+    return call(
+        right_a_kernel,
+        "right_a",
+        jax.ShapeDtypeStruct((rows, HALF), F32),
+        6 * rows * HALF * HALF,
         in_specs=[VMEM] * 3,
-        out_specs=[VMEM] * 2,
-    )(in_vmem(x), in_vmem(m), in_vmem(q))
-
-
-def right_kernel(high_ref, low_ref, q_ref, onto_ref, out_ref, held_ref, sems):
+        out_specs=VMEM,
+    )(high, low, q)
+
+
+def right_kernel(high_ref, low_ref, q_ref, part_ref, onto_ref, out_ref, held_ref, sems):
     q = split(q_ref[...])
     outs = []
     for i, rows in enumerate(row_tiles(high_ref, 512)):
-        held_ref[rows, :] = dot3((high_ref[rows, :], low_ref[rows, :]), q, NN)
+        held_ref[rows, :] = part_ref[rows, :] + dot3((high_ref[rows, :], low_ref[rows, :]), q, NN)
         outs.append(pltpu.make_async_copy(held_ref.at[rows], out_ref.at[rows, pl.ds(HALF, HALF)], sems.at[i]))
         outs[-1].start()
     for copy in outs:
         copy.wait()
 
 
-def right(high, low, q, onto):
+def right(high, low, q, part, onto):
     rows = high.shape[0]
     return call(
         right_kernel,
         "right",
         jax.ShapeDtypeStruct((rows, PAIR), F32),
-        6 * rows * PAIR * HALF,
-        in_specs=[VMEM, VMEM, VMEM, HBM],
+        6 * rows * HALF * HALF,
+        in_specs=[VMEM] * 4 + [HBM],
         out_specs=HBM,
         scratch_shapes=[pltpu.VMEM((rows, HALF), F32), pltpu.SemaphoreType.DMA((rows // 512,))],
-        input_output_aliases={3: 0},
-    )(high, low, q, onto)
+        input_output_aliases={4: 0},
+    )(high, low, q, part, onto)
 
 
 def left_kernel(a_ref, m_ref, q_ref, out_ref, held_ref, sems):
@@ -360,20 +392,23 @@
     movers, cross = lax.optimization_barrier((movers[:, 0], cross))
     parts = exchanged(cross, (16, 128))
     packed = exchanged(payload(share_kernel, parts, norms), (CHUNK // 2, 2, 128))
-    both, stay = rotation(0, movers, packed, 2 * PAIR)
+    both, stay = rotation(0, movers, packed, (2 * PAIR, PAIR))
 
     left_both = passed_along(both)
     a, norm_a, cross = meet(columns, stay, left_columns)
     parts = exchanged(cross, (32, 128))
-    m, norm_m, high, low = turn(left_columns, left_both)
+    m, norm_m, high, low, *left_a = turn(left_columns, left_both)
     left_m = passed_along(m)
     packed = exchanged(payload(project_kernel, parts, high, low, norm_a, norm_m), (CHUNK // 2, 2, 128))
-    move, stay = rotation(1, movers, packed)
-
-    left_move = passed_along(move)
-    left_high, left_low = ready(left_columns, left_m, left_both)
+    move_a, move_m, stay = rotation(1, movers, packed, (HALF, HALF, PAIR))
+
+    left_move_a = passed_along(move_a)
+    left_move_m = passed_along(move_m)
+    left_m = ready(left_m)
     out = left(a, m, stay)
-    return right(left_high, left_low, left_move, out)
+    left_a, left_m, out = lax.optimization_barrier((left_a, left_m, out))
+    part = right_a(*left_a, left_move_a)
+    return right(*left_m, left_move_m, part, out)
 
 
 def solution(mesh):

time: 127 us -> 124 us (0.976)
  waiting for transfers between devices: 8.55 us -> 6.98 us
  Pallas kernels: 40.1 us -> 38.8 us
    all_to_all x1, waiting for transfers between devices: 4.88 us -> 3.08 us  [exchanged(): lax.all_to_all(packed.reshape(SLABS, *shape), 'slab', 0, 0)]
    pallas_call x1, Pallas kernels: 3.97 us -> 5.73 us  [turn(): call(turn_kernel, 'turn', (pltpu.HBM((rows, HALF), F32), jax.ShapeDtypeSt...]
    pallas_call x1 -> x2, Pallas kernels: 4.26 us -> 2.87 us  [the longest x1 1.88 us: ready(): call(ready_kernel, 'ready', (out, out), 10 ** 6, in_specs=[VMEM], out_spe...]
    ppermute x4 -> x5, waiting for transfers between devices: 3.67 us -> 3.9 us  [passed_along(): lax.ppermute(value, 'blk', [(source, (source + 1) % count) for source in...]
    ppermute x4 -> x5, starting transfers between devices: 11.5 us -> 11.4 us  [passed_along(): lax.ppermute(value, 'blk', [(source, (source + 1) % count) for source in...]
    unnamed x14 -> x16, local copies, waits for them, and re-layouts: 4.43 us -> 4.43 us
  transfers between devices with their start and end apart: 5 -> 6, of which waited for: 2 -> 3; matrix products, arithmetic and copies ran while one was open for 0% -> 0% of each run, Pallas kernels for 29% -> 30%
where the time goes in v5:
time: 124 us
  blocking collectives  57.9 us (47%)
  Pallas kernels  38.8 us (31%)
  starting transfers between devices  15.2 us (12%)
  waiting for transfers between devices  6.98 us (6%)
  local copies, waits for them, and re-layouts  4.43 us (4%)
    all_to_all x3, blocking collectives, exchanged(): lax.all_to_all(packed.reshape(SLABS, *shape), 'slab', 0, 0)  57.9 us
    pallas_call x2, Pallas kernels, rotation(): call(lambda *refs: rotation_kernel(index, *refs), 'rotation', [jax.ShapeD...  19.2 us
    ppermute x5, starting transfers between devices, passed_along(): lax.ppermute(value, 'blk', [(source, (source + 1) % count) for source in...  11.4 us
    pallas_call x1, Pallas kernels, turn(): call(turn_kernel, 'turn', (pltpu.HBM((rows, HALF), F32), jax.ShapeDtypeSt...  5.73 us
    pallas_call x1, Pallas kernels, meet(): call(meet_kernel, 'meet', (jax.ShapeDtypeStruct((rows, HALF), F32), jax.S...  4.55 us
    unnamed x16, local copies, waits for them, and re-layouts  4.43 us
    ppermute x5, waiting for transfers between devices, passed_along(): lax.ppermute(value, 'blk', [(source, (source + 1) % count) for source in...  3.9 us
    all_to_all x1, starting transfers between devices, exchanged(): lax.all_to_all(packed.reshape(SLABS, *shape), 'slab', 0, 0)  3.89 us
  transfers between devices with their start and end apart: 6, of which 3 were waited for; matrix products, arithmetic and copies ran while one was open for 0% of the time, Pallas kernels for 30%

profile of v5, /device:TPU:1, one launch (start us, length us, event | category | flops | bytes accessed | tf_op | source)
XLA Modules:
  0.0 123.6 jit_solution(4758044975407460729)
XLA Ops:
  0.0 2.7 %collective-permute-start = (f32[2048,512]{1,0:T(8,128)}, f32[2048,512]{1,0:T(8,128)S(1)}, u32[]{:S(2)}, u32[]{:S(2)}) collective-permute-start(f32[2048,512]{1,0:T(8,128)} %x_ref.3), channel_id=1, source_target_pairs={{0,1},{1,2},{2,3},{3,4},{4,5},{5,6},{6,7},{7,0},{8,9},{9,10},{10,1... | collective-permute-start | bytes 12582920 | tf_op jit(solution)/shard_map/ppermute | solution.py:381
  2.7 0.0 copy-start
  2.7 2.2 %copy-done = f32[2048,512]{1,0:T(8,128)S(1)} copy-done((f32[2048,512]{1,0:T(8,128)S(1)}, f32[2048,512]{1,0:T(8,128)}, u32[]{:S(2)}) %copy-start) | copy-done | bytes 4194328
  4.9 0.0 copy-start.7
  4.9 1.1 first_inner.1
  6.0 23.5 %all_to_all.20 = f32[32,16,128]{2,1,0:T(8,128)S(1)} all-to-all(f32[32,16,128]{2,1,0:T(8,128)S(1)} %bitcast.15), channel_id=1, replica_groups=mesh['slab'=32,'blk'=8] {'slab'}, dimensions={0} | all-to-all | bytes 524288 | tf_op jit(solution)/shard_map/all_to_all | solution.py:385
  29.6 0.1 payload.2
  29.6 16.6 %all_to_all.21 = f32[32,10,2,128]{3,2,1,0:T(2,128)S(1)} all-to-all(f32[32,10,2,128]{3,2,1,0:T(2,128)S(1)} %bitcast.10), channel_id=1, replica_groups=mesh['slab'=32,'blk'=8] {'slab'}, dimensions={0} | all-to-all | bytes 655360 | tf_op jit(solution)/shard_map/all_to_all | solution.py:385
  46.2 0.0 copy-done.7
  46.2 0.0 copy-start.1
  46.2 10.2 %rotation.2 = (f32[1024,256]{1,0:T(8,128)}, f32[512,256]{1,0:T(8,128)S(1)}) custom-call(s32[2]{0:T(128)S(1)} %bitcast.16, f32[640,128]{1,0:T(8,128)S(1)} %bitcast.14), custom_call_target="tpu_custom_call" | custom-call | flops 10000000000 | bytes 4194304 | tf_op jit(solution)/shard_map/rotation/pallas_call | solution.py:143
  56.4 3.1 %collective-permute-start.1 = (f32[1024,256]{1,0:T(8,128)}, f32[1024,256]{1,0:T(8,128)}, u32[]{:S(2)}, u32[]{:S(2)}) collective-permute-start(f32[1024,256]{1,0:T(8,128)} %get-tuple-element.34), channel_id=1, source_target_pairs={{0,1},{1,2},{2,3},{3,4},{4,5},{5,6},{6,7},{7,0},{8,9},{9,10},{10,1... | collective-permute-start | bytes 3145736 | tf_op jit(solution)/shard_map/ppermute | solution.py:381
  59.5 0.0 collective-permute-done.x_ref.left_ref
  59.5 0.0 copy-start.5
  59.5 0.0 copy-done.1
  59.5 4.5 %meet.1 = (f32[2048,256]{1,0:T(8,128)S(1)}, f32[8,256]{1,0:T(8,128)S(1)}, f32[1024,128]{1,0:T(8,128)}) custom-call(f32[2048,512]{1,0:T(8,128)S(1)} %copy-done.1, f32[512,256]{1,0:T(8,128)S(1)} %get-tuple-element.40.q_ref, f32[2048,512]{1,0:T(8,128)S(1)} %collective-permute-done.x_ref.left_ref), custom_call_target="tpu_custom_call" | custom-call | flops 3221225472 | bytes 4194304 | tf_op jit(solution)/shard_map/meet/pallas_call | solution.py:201
  64.1 0.0 copy-done.5
  64.1 3.9 %all-to-all-start.2 = ((f32[32,32,128]{2,1,0:T(8,128)}), f32[32,32,128]{2,1,0:T(8,128)S(1)}, u32[]{:S(2)}, u32[]{:S(2)}) async-start(f32[32,32,128]{2,1,0:T(8,128)} %bitcast.5), calls=%async_computation.2 | async-start | bytes 1048576 | tf_op jit(solution)/shard_map/all_to_all | solution.py:385
  68.0 3.6 %collective-permute-done.1.q_ref = f32[1024,256]{1,0:T(8,128)} collective-permute-done((f32[1024,256]{1,0:T(8,128)}, f32[1024,256]{1,0:T(8,128)}, u32[]{:S(2)}, u32[]{:S(2)}) %collective-permute-start.1) | collective-permute-done | bytes 1048608 | tf_op jit(solution)/shard_map/ppermute | solution.py:381
  71.6 0.0 copy-start.6
  71.6 2.2 %copy-done.6 = f32[2048,512]{1,0:T(8,128)S(1)} copy-done((f32[2048,512]{1,0:T(8,128)S(1)}, f32[2048,512]{1,0:T(8,128)}, u32[]{:S(2)}) %copy-start.6) | copy-done | bytes 4194328
  73.8 5.7 %turn.1 = (f32[2048,256]{1,0:T(8,128)}, f32[8,256]{1,0:T(8,128)S(1)}, bf16[512,256]{1,0:T(8,128)(2,1)S(1)}, bf16[512,256]{1,0:T(8,128)(2,1)S(1)}, bf16[2048,256]{1,0:T(8,128)(2,1)}, /*index=5*/bf16[2048,256]{1,0:T(8,128)(2,1)}) custom-call(f32[2048,512]{1,0:T(8,128)S(1)} %copy-done.6, f32[1024,256]{1,0:T(8,128)} %collective-permute-done.1.q_ref), custom_call_target="tpu_custom_call" | custom-call | flops 30000001024 | bytes 4194304 | tf_op jit(solution)/shard_map/turn/pallas_call | solution.py:273
  79.5 2.5 %collective-permute-start.2 = (f32[2048,256]{1,0:T(8,128)}, f32[2048,256]{1,0:T(8,128)}, u32[]{:S(2)}, u32[]{:S(2)}) collective-permute-start(f32[2048,256]{1,0:T(8,128)} %get-tuple-element.37.m_ref), channel_id=1, source_target_pairs={{0,1},{1,2},{2,3},{3,4},{4,5},{5,6},{6,7},{7,0},{8,9},{9,10},{10,1... | collective-permute-start | bytes 6291464 | tf_op jit(solution)/shard_map/ppermute | solution.py:381
  82.0 3.1 %all-to-all-done.2 = f32[32,32,128]{2,1,0:T(8,128)S(1)} async-done(((f32[32,32,128]{2,1,0:T(8,128)}), f32[32,32,128]{2,1,0:T(8,128)S(1)}, u32[]{:S(2)}, u32[]{:S(2)}) %all-to-all-start.2) | async-done | bytes 524320 | tf_op jit(solution)/shard_map/all_to_all | solution.py:385
  85.1 0.3 payload.3
  85.4 17.7 %all_to_all.22 = f32[32,10,2,128]{3,2,1,0:T(2,128)S(1)} all-to-all(f32[32,10,2,128]{3,2,1,0:T(2,128)S(1)} %bitcast.11), channel_id=1, replica_groups=mesh['slab'=32,'blk'=8] {'slab'}, dimensions={0} | all-to-all | bytes 655360 | tf_op jit(solution)/shard_map/all_to_all | solution.py:385
  103.1 0.0 copy-start.2
  103.1 9.0 %rotation.3 = (f32[256,256]{1,0:T(8,128)S(1)}, f32[256,256]{1,0:T(8,128)S(1)}, f32[512,256]{1,0:T(8,128)S(1)}) custom-call(s32[2]{0:T(128)S(1)} %bitcast.17, f32[640,128]{1,0:T(8,128)S(1)} %bitcast.13), custom_call_target="tpu_custom_call" | custom-call | flops 10000000000 | bytes 4194304 | tf_op jit(solution)/shard_map/rotation/pallas_call | solution.py:143
  112.2 3.0 %collective-permute-start.4 = (f32[256,256]{1,0:T(8,128)S(1)}, f32[256,256]{1,0:T(8,128)S(1)}, u32[]{:S(2)}, u32[]{:S(2)}) collective-permute-start(f32[256,256]{1,0:T(8,128)S(1)} %get-tuple-element.53), channel_id=1, source_target_pairs={{0,1},{1,2},{2,3},{3,4},{4,5},{5,6},{6,7},{7,0},{8,9},{9,10},{10,1... | collective-permute-start | bytes 786440 | tf_op jit(solution)/shard_map/ppermute | solution.py:381
  115.2 0.0 collective-permute-start.3
  115.2 0.0 copy-done.2
  115.2 0.0 copy-start.3
  115.2 0.0 copy-start.4
  115.2 2.9 %left.1.onto_ref = f32[2048,512]{1,0:T(8,128)} custom-call(f32[2048,256]{1,0:T(8,128)S(1)} %get-tuple-element.41.a_ref, f32[2048,256]{1,0:T(8,128)S(1)} %copy-done.2, f32[512,256]{1,0:T(8,128)S(1)} %get-tuple-element.47.q_ref), custom_call_target="tpu_custom_call" | custom-call | flops 1610612736 | bytes 4194304 | tf_op jit(solution)/shard_map/left/pallas_call | solution.py:368
  118.1 0.0 collective-permute-done.2.m_ref
  118.1 1.9 %ready.1 = (bf16[2048,256]{1,0:T(8,128)(2,1)S(1)}, bf16[2048,256]{1,0:T(8,128)(2,1)S(1)}) custom-call(f32[2048,256]{1,0:T(8,128)} %collective-permute-done.2.m_ref), custom_call_target="tpu_custom_call" | custom-call | flops 1000000 | bytes 4194304 | tf_op jit(solution)/shard_map/ready/pallas_call | solution.py:302
  120.0 0.0 collective-permute-done.4.q_ref
  120.0 0.0 copy-done.3
  120.0 0.0 copy-done.4
  120.0 1.0 right_a.1.part_ref
  121.0 0.3 collective-permute-done.3.q_ref
  121.3 2.1 %right.1 = f32[2048,512]{1,0:T(8,128)} custom-call(bf16[2048,256]{1,0:T(8,128)(2,1)S(1)} %get-tuple-element.48.high_ref, bf16[2048,256]{1,0:T(8,128)(2,1)S(1)} %get-tuple-element.49.low_ref, f32[256,256]{1,0:T(8,128)S(1)} %collective-permute-done.3.q_ref, f32[2048,256]{1,0:T(8,128)S(1)} %right_a.1.part_ref, ...), custom_call_target="tpu_custom_call", output_to_operand_aliasing={{}: (4, {})} | custom-call | flops 805306368 | bytes 4194304 | tf_op jit(solution)/shard_map/right/pallas_call | solution.py:343
Async XLA Ops:
  0.0 59.5 %collective-permute-start = (f32[2048,512]{1,0:T(8,128)}, f32[2048,512]{1,0:T(8,128)S(1)}, u32[]{:S(2)}, u32[]{:S(2)}) collective-permute-start(f32[2048,512]{1,0:T(8,128)} %x_ref.3), channel_id=1, source_target_pairs={{0,1},{1,2},{2,3},{3,4},{4,5},{5,6},{6,7},{7,0},{8,9},{9,10},{10,1... | collective-permute-start | bytes 12582920 | tf_op jit(solution)/shard_map/ppermute | solution.py:381
  2.7 2.2 %copy-start = (f32[2048,512]{1,0:T(8,128)S(1)}, f32[2048,512]{1,0:T(8,128)}, u32[]{:S(2)}) copy-start(f32[2048,512]{1,0:T(8,128)} %x_ref.3) | copy-start | bytes 12582916
  4.9 41.3 %copy-start.7 = (s32[2,1]{0,1:T(1,128)S(1)}, s32[2,1]{0,1:T(1,128)}, u32[]{:S(2)}) copy-start(s32[2,1]{0,1:T(1,128)} %param.3) | copy-start | bytes 28
  46.2 13.3 %copy-start.1 = (f32[2048,512]{1,0:T(8,128)S(1)}, f32[2048,512]{1,0:T(8,128)}, u32[]{:S(2)}) copy-start(f32[2048,512]{1,0:T(8,128)} %x_ref.3) | copy-start | bytes 12582916
  56.4 15.2 %collective-permute-start.1 = (f32[1024,256]{1,0:T(8,128)}, f32[1024,256]{1,0:T(8,128)}, u32[]{:S(2)}, u32[]{:S(2)}) collective-permute-start(f32[1024,256]{1,0:T(8,128)} %get-tuple-element.34), channel_id=1, source_target_pairs={{0,1},{1,2},{2,3},{3,4},{4,5},{5,6},{6,7},{7,0},{8,9},{9,10},{10,1... | collective-permute-start | bytes 3145736 | tf_op jit(solution)/shard_map/ppermute | solution.py:381
  59.5 4.6 %copy-start.5 = (f32[2048,512]{1,0:T(8,128)}, f32[2048,512]{1,0:T(8,128)S(1)}, u32[]{:S(2)}) copy-start(f32[2048,512]{1,0:T(8,128)S(1)} %collective-permute-done.x_ref.left_ref) | copy-start | bytes 12582916
  64.1 21.0 %all-to-all-start.2 = ((f32[32,32,128]{2,1,0:T(8,128)}), f32[32,32,128]{2,1,0:T(8,128)S(1)}, u32[]{:S(2)}, u32[]{:S(2)}) async-start(f32[32,32,128]{2,1,0:T(8,128)} %bitcast.5), calls=%async_computation.2 | async-start | bytes 1048576 | tf_op jit(solution)/shard_map/all_to_all | solution.py:385
  71.6 2.2 %copy-start.6 = (f32[2048,512]{1,0:T(8,128)S(1)}, f32[2048,512]{1,0:T(8,128)}, u32[]{:S(2)}) copy-start(f32[2048,512]{1,0:T(8,128)} %copy-done.5) | copy-start | bytes 12582916
  79.5 38.6 %collective-permute-start.2 = (f32[2048,256]{1,0:T(8,128)}, f32[2048,256]{1,0:T(8,128)}, u32[]{:S(2)}, u32[]{:S(2)}) collective-permute-start(f32[2048,256]{1,0:T(8,128)} %get-tuple-element.37.m_ref), channel_id=1, source_target_pairs={{0,1},{1,2},{2,3},{3,4},{4,5},{5,6},{6,7},{7,0},{8,9},{9,10},{10,1... | collective-permute-start | bytes 6291464 | tf_op jit(solution)/shard_map/ppermute | solution.py:381
  103.1 12.1 %copy-start.2 = (f32[2048,256]{1,0:T(8,128)S(1)}, f32[2048,256]{1,0:T(8,128)}, u32[]{:S(2)}) copy-start(f32[2048,256]{1,0:T(8,128)} %get-tuple-element.37.m_ref) | copy-start | bytes 6291460
  112.2 7.8 %collective-permute-start.4 = (f32[256,256]{1,0:T(8,128)S(1)}, f32[256,256]{1,0:T(8,128)S(1)}, u32[]{:S(2)}, u32[]{:S(2)}) collective-permute-start(f32[256,256]{1,0:T(8,128)S(1)} %get-tuple-element.53), channel_id=1, source_target_pairs={{0,1},{1,2},{2,3},{3,4},{4,5},{5,6},{6,7},{7,0},{8,9},{9,10},{10,1... | collective-permute-start | bytes 786440 | tf_op jit(solution)/shard_map/ppermute | solution.py:381
  115.2 6.1 %collective-permute-start.3 = (f32[256,256]{1,0:T(8,128)S(1)}, f32[256,256]{1,0:T(8,128)S(1)}, u32[]{:S(2)}, u32[]{:S(2)}) collective-permute-start(f32[256,256]{1,0:T(8,128)S(1)} %get-tuple-element.50), channel_id=1, source_target_pairs={{0,1},{1,2},{2,3},{3,4},{4,5},{5,6},{6,7},{7,0},{8,9},{9,10},{10,1... | collective-permute-start | bytes 786440 | tf_op jit(solution)/shard_map/ppermute | solution.py:381
  115.2 4.8 %copy-start.3 = (bf16[2048,256]{1,0:T(8,128)(2,1)S(1)}, bf16[2048,256]{1,0:T(8,128)(2,1)}, u32[]{:S(2)}) copy-start(bf16[2048,256]{1,0:T(8,128)(2,1)} %get-tuple-element.51.high_ref) | copy-start | bytes 3145732
  115.2 4.8 %copy-start.4 = (bf16[2048,256]{1,0:T(8,128)(2,1)S(1)}, bf16[2048,256]{1,0:T(8,128)(2,1)}, u32[]{:S(2)}) copy-start(bf16[2048,256]{1,0:T(8,128)(2,1)} %get-tuple-element.52.low_ref) | copy-start | bytes 3145732

commit v6 on v5

--- a/solution.py
+++ b/solution.py
@@ -9,6 +9,7 @@
 PAIR = 2 * HALF
 SLABS = 32
 CHUNK = 20
+FIRST = 17
 EPS = 1e-6
 VMEM_BYTES = 24 * 2**20
 F32 = jnp.float32
@@ -94,12 +95,16 @@
 
 
 def rotation_kernel(index, movers_ref, packed_ref, *outs):
-    left = [packed_ref[CHUNK * k:CHUNK * k + 8, :] for k in range(SLABS)]
-    right = [packed_ref[CHUNK * k + 8:CHUNK * k + 16, :] for k in range(SLABS)]
+    chunk = packed_ref.shape[0] // SLABS
+    left = [packed_ref[chunk * k:chunk * k + 8, :] for k in range(SLABS)]
+    right = [packed_ref[chunk * k + 8:chunk * k + 16, :] for k in range(SLABS)]
     cross = jnp.concatenate([jnp.concatenate(left, 0), jnp.concatenate(right, 0)], 1)
-    norms = packed_ref[16:20, :]
-    for k in range(1, SLABS):
-        norms = norms + packed_ref[CHUNK * k + 16:CHUNK * k + 20, :]
+    if chunk == FIRST:
+        norms = jnp.concatenate([packed_ref[FIRST * k + 16:FIRST * k + 17, :] for k in range(4)], 0)
+    else:
+        norms = packed_ref[16:20, :]
+        for k in range(1, SLABS):
+            norms = norms + packed_ref[CHUNK * k + 16:CHUNK * k + 20, :]
     norm_a = jnp.concatenate([norms[0:1], norms[1:2]], 1)
     norm_m = jnp.concatenate([norms[2:3], norms[3:4]], 1)
     rows = lax.broadcasted_iota(jnp.int32, (HALF, HALF), 0)
@@ -162,24 +167,27 @@
     return jnp.sum(x.reshape(-1, 8, x.shape[1]) ** 2, axis=0)
 
 
-def first_kernel(x_ref, packed_ref, norm_ref):
+def first_kernel(x_ref, packed_ref):
     total, norm = 0.0, 0.0
     for rows in row_tiles(x_ref, 256):
         x = x_ref[rows, :]
         total += dot3(split(x[:, :HALF]), split(x[:, HALF:]), TN)
         norm += squares(x)
-    pack(packed_ref, total)
-    norm_ref[...] = jnp.concatenate([norm[:, :HALF], norm[:, HALF:]], 0)
+    norm = jnp.sum(norm, axis=0, keepdims=True)
+    for k in range(SLABS):
+        packed_ref[FIRST * k:FIRST * k + 8, :] = total[8 * k:8 * k + 8, :128]
+        packed_ref[FIRST * k + 8:FIRST * k + 16, :] = total[8 * k:8 * k + 8, 128:]
+        packed_ref[FIRST * k + 16:FIRST * k + 17, :] = norm[:, 128 * (k % 4):128 * (k % 4) + 128]
 
 
 def first_inner(x):
     return call(
         first_kernel,
         "first_inner",
-        (jax.ShapeDtypeStruct((HALF * HALF // 128, 128), F32), jax.ShapeDtypeStruct((16, HALF), F32)),
+        jax.ShapeDtypeStruct((SLABS * FIRST, 128), F32),
         6 * x.shape[0] * HALF * HALF,
         in_specs=[VMEM],
-        out_specs=[VMEM] * 2,
+        out_specs=VMEM,
     )(in_vmem(x))
 
 
@@ -222,12 +230,12 @@
         out_ref[CHUNK * k:CHUNK * k + CHUNK, :] = chunk
 
 
-def share_kernel(parts_ref, norm_ref, out_ref):
-    total = parts_ref[0:16, :]
+def share_kernel(parts_ref, out_ref):
+    total = parts_ref[:FIRST, :]
     for k in range(1, SLABS):
-        total = total + parts_ref[16 * k:16 * k + 16, :]
-    cross = jnp.concatenate([total[:8], total[8:]], 1)
-    fill(out_ref, cross, norm_ref[:8, :], norm_ref[8:, :])
+        total = total + parts_ref[FIRST * k:FIRST * k + FIRST, :]
+    for k in range(SLABS):
+        out_ref[FIRST * k:FIRST * k + FIRST, :] = total
 
 
 def project_kernel(parts_ref, high_ref, low_ref, norm_a_ref, norm_m_ref, out_ref):
@@ -240,8 +248,8 @@
     fill(out_ref, cross, norm_a_ref[...], norm_m_ref[...])
 
 
-def payload(kernel, *arrays):
-    out = jax.ShapeDtypeStruct((SLABS * CHUNK, 128), F32)
+def payload(kernel, chunk, *arrays):
+    out = jax.ShapeDtypeStruct((SLABS * chunk, 128), F32)
     return call(kernel, "payload", out, 10**7, in_specs=[VMEM] * len(arrays), out_specs=VMEM)(*arrays)
 
 
@@ -388,10 +396,10 @@
 def local(columns, movers):
     left_columns = passed_along(columns)
 
-    cross, norms = first_inner(columns)
+    cross = first_inner(columns)
     movers, cross = lax.optimization_barrier((movers[:, 0], cross))
-    parts = exchanged(cross, (16, 128))
-    packed = exchanged(payload(share_kernel, parts, norms), (CHUNK // 2, 2, 128))
+    parts = exchanged(cross, (FIRST, 1, 128))
+    packed = exchanged(payload(share_kernel, FIRST, parts), (FIRST, 1, 128))
     both, stay = rotation(0, movers, packed, (2 * PAIR, PAIR))
 
     left_both = passed_along(both)
@@ -399,7 +407,7 @@
     parts = exchanged(cross, (32, 128))
     m, norm_m, high, low, *left_a = turn(left_columns, left_both)
     left_m = passed_along(m)
-    packed = exchanged(payload(project_kernel, parts, high, low, norm_a, norm_m), (CHUNK // 2, 2, 128))
+    packed = exchanged(payload(project_kernel, CHUNK, parts, high, low, norm_a, norm_m), (CHUNK // 2, 2, 128))
     move_a, move_m, stay = rotation(1, movers, packed, (HALF, HALF, PAIR))
 
     left_move_a = passed_along(move_a)

time: 124 us -> 124 us (level)
  no operation moved by 1% of the time
where the time goes in v6:
time: 124 us; the launch traced here: 123 us
  blocking collectives  57.4 us (46%)
  Pallas kernels  38.8 us (31%)
  starting transfers between devices  15.2 us (12%)
  waiting for transfers between devices  6.97 us (6%)
  local copies, waits for them, and re-layouts  4.43 us (4%)
    all_to_all x3, blocking collectives, exchanged(): lax.all_to_all(packed.reshape(SLABS, *shape), 'slab', 0, 0)  57.4 us
    pallas_call x2, Pallas kernels, rotation(): call(lambda *refs: rotation_kernel(index, *refs), 'rotation', [jax.ShapeD...  19.2 us
    ppermute x5, starting transfers between devices, passed_along(): lax.ppermute(value, 'blk', [(source, (source + 1) % count) for source in...  11.3 us
    pallas_call x1, Pallas kernels, turn(): call(turn_kernel, 'turn', (pltpu.HBM((rows, HALF), F32), jax.ShapeDtypeSt...  5.72 us
    pallas_call x1, Pallas kernels, meet(): call(meet_kernel, 'meet', (jax.ShapeDtypeStruct((rows, HALF), F32), jax.S...  4.52 us
    unnamed x16, local copies, waits for them, and re-layouts  4.43 us
    ppermute x5, waiting for transfers between devices, passed_along(): lax.ppermute(value, 'blk', [(source, (source + 1) % count) for source in...  3.91 us
    all_to_all x1, starting transfers between devices, exchanged(): lax.all_to_all(packed.reshape(SLABS, *shape), 'slab', 0, 0)  3.89 us
  transfers between devices with their start and end apart: 6, of which 3 were waited for; matrix products, arithmetic and copies ran while one was open for 0% of the time, Pallas kernels for 30%

profile of v6, /device:TPU:1, one launch (start us, length us, event | category | flops | bytes accessed | tf_op | source)
XLA Modules:
  0.0 123.1 jit_solution(10883151925431384520)
XLA Ops:
  0.0 2.7 %collective-permute-start = (f32[2048,512]{1,0:T(8,128)}, f32[2048,512]{1,0:T(8,128)S(1)}, u32[]{:S(2)}, u32[]{:S(2)}) collective-permute-start(f32[2048,512]{1,0:T(8,128)} %x_ref.3), channel_id=1, source_target_pairs={{0,1},{1,2},{2,3},{3,4},{4,5},{5,6},{6,7},{7,0},{8,9},{9,10},{10,1... | collective-permute-start | bytes 12582920 | tf_op jit(solution)/shard_map/ppermute | solution.py:389
  2.7 0.0 copy-start
  2.7 2.2 %copy-done = f32[2048,512]{1,0:T(8,128)S(1)} copy-done((f32[2048,512]{1,0:T(8,128)S(1)}, f32[2048,512]{1,0:T(8,128)}, u32[]{:S(2)}) %copy-start) | copy-done | bytes 4194328
  4.9 0.0 copy-start.7
  4.9 1.1 first_inner.1
  6.0 23.8 %all_to_all.20 = f32[32,17,1,128]{3,2,1,0:T(1,128)S(1)} all-to-all(f32[32,17,1,128]{3,2,1,0:T(1,128)S(1)} %bitcast.11), channel_id=1, replica_groups=mesh['slab'=32,'blk'=8] {'slab'}, dimensions={0} | all-to-all | bytes 557056 | tf_op jit(solution)/shard_map/all_to_all | solution.py:393
  29.8 0.1 payload.2
  29.9 15.9 %all_to_all.21 = f32[32,17,1,128]{3,2,1,0:T(1,128)S(1)} all-to-all(f32[32,17,1,128]{3,2,1,0:T(1,128)S(1)} %bitcast.13), channel_id=1, replica_groups=mesh['slab'=32,'blk'=8] {'slab'}, dimensions={0} | all-to-all | bytes 557056 | tf_op jit(solution)/shard_map/all_to_all | solution.py:393
  45.8 0.0 copy-done.7
  45.8 0.0 copy-start.1
  45.8 10.2 %rotation.2 = (f32[1024,256]{1,0:T(8,128)}, f32[512,256]{1,0:T(8,128)S(1)}) custom-call(s32[2]{0:T(128)S(1)} %bitcast.16, f32[544,128]{1,0:T(8,128)S(1)} %bitcast.15), custom_call_target="tpu_custom_call" | custom-call | flops 10000000000 | bytes 4194304 | tf_op jit(solution)/shard_map/rotation/pallas_call | solution.py:148
  56.0 3.1 %collective-permute-start.1 = (f32[1024,256]{1,0:T(8,128)}, f32[1024,256]{1,0:T(8,128)}, u32[]{:S(2)}, u32[]{:S(2)}) collective-permute-start(f32[1024,256]{1,0:T(8,128)} %get-tuple-element.30), channel_id=1, source_target_pairs={{0,1},{1,2},{2,3},{3,4},{4,5},{5,6},{6,7},{7,0},{8,9},{9,10},{10,1... | collective-permute-start | bytes 3145736 | tf_op jit(solution)/shard_map/ppermute | solution.py:389
  59.1 0.0 collective-permute-done.x_ref.left_ref
  59.1 0.0 copy-start.5
  59.1 0.0 copy-done.1
  59.1 4.5 %meet.1 = (f32[2048,256]{1,0:T(8,128)S(1)}, f32[8,256]{1,0:T(8,128)S(1)}, f32[1024,128]{1,0:T(8,128)}) custom-call(f32[2048,512]{1,0:T(8,128)S(1)} %copy-done.1, f32[512,256]{1,0:T(8,128)S(1)} %get-tuple-element.36.q_ref, f32[2048,512]{1,0:T(8,128)S(1)} %collective-permute-done.x_ref.left_ref), custom_call_target="tpu_custom_call" | custom-call | flops 3221225472 | bytes 4194304 | tf_op jit(solution)/shard_map/meet/pallas_call | solution.py:209
  63.6 0.0 copy-done.5
  63.6 3.9 %all-to-all-start.2 = ((f32[32,32,128]{2,1,0:T(8,128)}), f32[32,32,128]{2,1,0:T(8,128)S(1)}, u32[]{:S(2)}, u32[]{:S(2)}) async-start(f32[32,32,128]{2,1,0:T(8,128)} %bitcast.5), calls=%async_computation.2 | async-start | bytes 1048576 | tf_op jit(solution)/shard_map/all_to_all | solution.py:393
  67.5 3.6 %collective-permute-done.1.q_ref = f32[1024,256]{1,0:T(8,128)} collective-permute-done((f32[1024,256]{1,0:T(8,128)}, f32[1024,256]{1,0:T(8,128)}, u32[]{:S(2)}, u32[]{:S(2)}) %collective-permute-start.1) | collective-permute-done | bytes 1048608 | tf_op jit(solution)/shard_map/ppermute | solution.py:389
  71.1 0.0 copy-start.6
  71.1 2.2 %copy-done.6 = f32[2048,512]{1,0:T(8,128)S(1)} copy-done((f32[2048,512]{1,0:T(8,128)S(1)}, f32[2048,512]{1,0:T(8,128)}, u32[]{:S(2)}) %copy-start.6) | copy-done | bytes 4194328
  73.3 5.7 %turn.1 = (f32[2048,256]{1,0:T(8,128)}, f32[8,256]{1,0:T(8,128)S(1)}, bf16[512,256]{1,0:T(8,128)(2,1)S(1)}, bf16[512,256]{1,0:T(8,128)(2,1)S(1)}, bf16[2048,256]{1,0:T(8,128)(2,1)}, /*index=5*/bf16[2048,256]{1,0:T(8,128)(2,1)}) custom-call(f32[2048,512]{1,0:T(8,128)S(1)} %copy-done.6, f32[1024,256]{1,0:T(8,128)} %collective-permute-done.1.q_ref), custom_call_target="tpu_custom_call" | custom-call | flops 30000001024 | bytes 4194304 | tf_op jit(solution)/shard_map/turn/pallas_call | solution.py:281
  79.0 2.5 %collective-permute-start.2 = (f32[2048,256]{1,0:T(8,128)}, f32[2048,256]{1,0:T(8,128)}, u32[]{:S(2)}, u32[]{:S(2)}) collective-permute-start(f32[2048,256]{1,0:T(8,128)} %get-tuple-element.33.m_ref), channel_id=1, source_target_pairs={{0,1},{1,2},{2,3},{3,4},{4,5},{5,6},{6,7},{7,0},{8,9},{9,10},{10,1... | collective-permute-start | bytes 6291464 | tf_op jit(solution)/shard_map/ppermute | solution.py:389
  81.5 3.1 %all-to-all-done.2 = f32[32,32,128]{2,1,0:T(8,128)S(1)} async-done(((f32[32,32,128]{2,1,0:T(8,128)}), f32[32,32,128]{2,1,0:T(8,128)S(1)}, u32[]{:S(2)}, u32[]{:S(2)}) %all-to-all-start.2) | async-done | bytes 524320 | tf_op jit(solution)/shard_map/all_to_all | solution.py:393
  84.6 0.3 payload.3
  84.9 17.7 %all_to_all.22 = f32[32,10,2,128]{3,2,1,0:T(2,128)S(1)} all-to-all(f32[32,10,2,128]{3,2,1,0:T(2,128)S(1)} %bitcast.10), channel_id=1, replica_groups=mesh['slab'=32,'blk'=8] {'slab'}, dimensions={0} | all-to-all | bytes 655360 | tf_op jit(solution)/shard_map/all_to_all | solution.py:393
  102.6 0.0 copy-start.2
  102.6 9.0 %rotation.3 = (f32[256,256]{1,0:T(8,128)S(1)}, f32[256,256]{1,0:T(8,128)S(1)}, f32[512,256]{1,0:T(8,128)S(1)}) custom-call(s32[2]{0:T(128)S(1)} %bitcast.17, f32[640,128]{1,0:T(8,128)S(1)} %bitcast.14), custom_call_target="tpu_custom_call" | custom-call | flops 10000000000 | bytes 4194304 | tf_op jit(solution)/shard_map/rotation/pallas_call | solution.py:148
  111.6 3.1 %collective-permute-start.4 = (f32[256,256]{1,0:T(8,128)S(1)}, f32[256,256]{1,0:T(8,128)S(1)}, u32[]{:S(2)}, u32[]{:S(2)}) collective-permute-start(f32[256,256]{1,0:T(8,128)S(1)} %get-tuple-element.49), channel_id=1, source_target_pairs={{0,1},{1,2},{2,3},{3,4},{4,5},{5,6},{6,7},{7,0},{8,9},{9,10},{10,1... | collective-permute-start | bytes 786440 | tf_op jit(solution)/shard_map/ppermute | solution.py:389
  114.7 0.0 collective-permute-start.3
  114.7 0.0 copy-done.2
  114.7 0.0 copy-start.3
  114.7 0.0 copy-start.4
  114.7 2.9 %left.1.onto_ref = f32[2048,512]{1,0:T(8,128)} custom-call(f32[2048,256]{1,0:T(8,128)S(1)} %get-tuple-element.37.a_ref, f32[2048,256]{1,0:T(8,128)S(1)} %copy-done.2, f32[512,256]{1,0:T(8,128)S(1)} %get-tuple-element.43.q_ref), custom_call_target="tpu_custom_call" | custom-call | flops 1610612736 | bytes 4194304 | tf_op jit(solution)/shard_map/left/pallas_call | solution.py:376
  117.6 0.0 collective-permute-done.2.m_ref
  117.6 1.9 %ready.1 = (bf16[2048,256]{1,0:T(8,128)(2,1)S(1)}, bf16[2048,256]{1,0:T(8,128)(2,1)S(1)}) custom-call(f32[2048,256]{1,0:T(8,128)} %collective-permute-done.2.m_ref), custom_call_target="tpu_custom_call" | custom-call | flops 1000000 | bytes 4194304 | tf_op jit(solution)/shard_map/ready/pallas_call | solution.py:310
  119.5 0.0 collective-permute-done.4.q_ref
  119.5 0.0 copy-done.3
  119.6 0.0 copy-done.4
  119.6 1.0 right_a.1.part_ref
  120.6 0.3 collective-permute-done.3.q_ref
  120.8 2.1 %right.1 = f32[2048,512]{1,0:T(8,128)} custom-call(bf16[2048,256]{1,0:T(8,128)(2,1)S(1)} %get-tuple-element.44.high_ref, bf16[2048,256]{1,0:T(8,128)(2,1)S(1)} %get-tuple-element.45.low_ref, f32[256,256]{1,0:T(8,128)S(1)} %collective-permute-done.3.q_ref, f32[2048,256]{1,0:T(8,128)S(1)} %right_a.1.part_ref, ...), custom_call_target="tpu_custom_call", output_to_operand_aliasing={{}: (4, {})} | custom-call | flops 805306368 | bytes 4194304 | tf_op jit(solution)/shard_map/right/pallas_call | solution.py:351
Async XLA Ops:
  0.0 59.1 %collective-permute-start = (f32[2048,512]{1,0:T(8,128)}, f32[2048,512]{1,0:T(8,128)S(1)}, u32[]{:S(2)}, u32[]{:S(2)}) collective-permute-start(f32[2048,512]{1,0:T(8,128)} %x_ref.3), channel_id=1, source_target_pairs={{0,1},{1,2},{2,3},{3,4},{4,5},{5,6},{6,7},{7,0},{8,9},{9,10},{10,1... | collective-permute-start | bytes 12582920 | tf_op jit(solution)/shard_map/ppermute | solution.py:389
  2.7 2.2 %copy-start = (f32[2048,512]{1,0:T(8,128)S(1)}, f32[2048,512]{1,0:T(8,128)}, u32[]{:S(2)}) copy-start(f32[2048,512]{1,0:T(8,128)} %x_ref.3) | copy-start | bytes 12582916
  4.9 40.9 %copy-start.7 = (s32[2,1]{0,1:T(1,128)S(1)}, s32[2,1]{0,1:T(1,128)}, u32[]{:S(2)}) copy-start(s32[2,1]{0,1:T(1,128)} %param.3) | copy-start | bytes 28
  45.8 13.3 %copy-start.1 = (f32[2048,512]{1,0:T(8,128)S(1)}, f32[2048,512]{1,0:T(8,128)}, u32[]{:S(2)}) copy-start(f32[2048,512]{1,0:T(8,128)} %x_ref.3) | copy-start | bytes 12582916
  56.0 15.1 %collective-permute-start.1 = (f32[1024,256]{1,0:T(8,128)}, f32[1024,256]{1,0:T(8,128)}, u32[]{:S(2)}, u32[]{:S(2)}) collective-permute-start(f32[1024,256]{1,0:T(8,128)} %get-tuple-element.30), channel_id=1, source_target_pairs={{0,1},{1,2},{2,3},{3,4},{4,5},{5,6},{6,7},{7,0},{8,9},{9,10},{10,1... | collective-permute-start | bytes 3145736 | tf_op jit(solution)/shard_map/ppermute | solution.py:389
  59.1 4.5 %copy-start.5 = (f32[2048,512]{1,0:T(8,128)}, f32[2048,512]{1,0:T(8,128)S(1)}, u32[]{:S(2)}) copy-start(f32[2048,512]{1,0:T(8,128)S(1)} %collective-permute-done.x_ref.left_ref) | copy-start | bytes 12582916
  63.6 21.0 %all-to-all-start.2 = ((f32[32,32,128]{2,1,0:T(8,128)}), f32[32,32,128]{2,1,0:T(8,128)S(1)}, u32[]{:S(2)}, u32[]{:S(2)}) async-start(f32[32,32,128]{2,1,0:T(8,128)} %bitcast.5), calls=%async_computation.2 | async-start | bytes 1048576 | tf_op jit(solution)/shard_map/all_to_all | solution.py:393
  71.1 2.2 %copy-start.6 = (f32[2048,512]{1,0:T(8,128)S(1)}, f32[2048,512]{1,0:T(8,128)}, u32[]{:S(2)}) copy-start(f32[2048,512]{1,0:T(8,128)} %copy-done.5) | copy-start | bytes 12582916
  79.0 38.6 %collective-permute-start.2 = (f32[2048,256]{1,0:T(8,128)}, f32[2048,256]{1,0:T(8,128)}, u32[]{:S(2)}, u32[]{:S(2)}) collective-permute-start(f32[2048,256]{1,0:T(8,128)} %get-tuple-element.33.m_ref), channel_id=1, source_target_pairs={{0,1},{1,2},{2,3},{3,4},{4,5},{5,6},{6,7},{7,0},{8,9},{9,10},{10,1... | collective-permute-start | bytes 6291464 | tf_op jit(solution)/shard_map/ppermute | solution.py:389
  102.6 12.1 %copy-start.2 = (f32[2048,256]{1,0:T(8,128)S(1)}, f32[2048,256]{1,0:T(8,128)}, u32[]{:S(2)}) copy-start(f32[2048,256]{1,0:T(8,128)} %get-tuple-element.33.m_ref) | copy-start | bytes 6291460
  111.6 7.9 %collective-permute-start.4 = (f32[256,256]{1,0:T(8,128)S(1)}, f32[256,256]{1,0:T(8,128)S(1)}, u32[]{:S(2)}, u32[]{:S(2)}) collective-permute-start(f32[256,256]{1,0:T(8,128)S(1)} %get-tuple-element.49), channel_id=1, source_target_pairs={{0,1},{1,2},{2,3},{3,4},{4,5},{5,6},{6,7},{7,0},{8,9},{9,10},{10,1... | collective-permute-start | bytes 786440 | tf_op jit(solution)/shard_map/ppermute | solution.py:389
  114.7 6.1 %collective-permute-start.3 = (f32[256,256]{1,0:T(8,128)S(1)}, f32[256,256]{1,0:T(8,128)S(1)}, u32[]{:S(2)}, u32[]{:S(2)}) collective-permute-start(f32[256,256]{1,0:T(8,128)S(1)} %get-tuple-element.46), channel_id=1, source_target_pairs={{0,1},{1,2},{2,3},{3,4},{4,5},{5,6},{6,7},{7,0},{8,9},{9,10},{10,1... | collective-permute-start | bytes 786440 | tf_op jit(solution)/shard_map/ppermute | solution.py:389
  114.7 4.8 %copy-start.3 = (bf16[2048,256]{1,0:T(8,128)(2,1)S(1)}, bf16[2048,256]{1,0:T(8,128)(2,1)}, u32[]{:S(2)}) copy-start(bf16[2048,256]{1,0:T(8,128)(2,1)} %get-tuple-element.47.high_ref) | copy-start | bytes 3145732
  114.7 4.8 %copy-start.4 = (bf16[2048,256]{1,0:T(8,128)(2,1)S(1)}, bf16[2048,256]{1,0:T(8,128)(2,1)}, u32[]{:S(2)}) copy-start(bf16[2048,256]{1,0:T(8,128)(2,1)} %get-tuple-element.48.low_ref) | copy-start | bytes 3145732

commit v7 on v5

--- a/solution.py
+++ b/solution.py
@@ -123,8 +123,8 @@
 
     def put(move_a, move_m, stay_a, stay_m):
         if len(outs) == 2:
-            for i, block in enumerate((move_a, move_m, stay_a, stay_m)):
-                outs[0][HALF * i:HALF * i + HALF, :] = block
+            outs[0][:HALF, :] = move_a
+            outs[0][HALF:, :] = move_m
         else:
             outs[0][...], outs[1][...] = move_a, move_m
         outs[-1][:HALF, :] = stay_a
@@ -183,17 +183,21 @@
     )(in_vmem(x))
 
 
-def meet_kernel(x_ref, q_ref, left_ref, a_ref, norm_ref, packed_ref):
+def meet_kernel(x_ref, q_ref, left_ref, a_ref, norm_ref, packed_ref, held_ref, sems):
     q = split(q_ref[...])
-    norm, total = 0.0, 0.0
-    for rows in row_tiles(x_ref, 512):
+    norm, total, outs = 0.0, 0.0, []
+    for i, rows in enumerate(row_tiles(x_ref, 512)):
         a = dot3(split(x_ref[rows, :]), q, NN)
-        a_ref[rows, :] = a
+        held_ref[rows, :] = a
         norm += squares(a)
+        outs.append(pltpu.make_async_copy(held_ref.at[rows], a_ref.at[rows], sems.at[i]))
+        outs[-1].start()
     norm_ref[...] = norm
     for rows in row_tiles(x_ref, 512):
-        total += dot3(split(a_ref[rows, :]), split(left_ref[rows, :]), TN)
+        total += dot3(split(held_ref[rows, :]), split(left_ref[rows, :]), TN)
     pack(packed_ref, total)
+    for copy in outs:
+        copy.wait()
 
 
 def meet(x, q, left):
@@ -202,13 +206,14 @@
         meet_kernel,
         "meet",
         (
-            jax.ShapeDtypeStruct((rows, HALF), F32),
+            pltpu.HBM((rows, HALF), F32),
             jax.ShapeDtypeStruct((8, HALF), F32),
             jax.ShapeDtypeStruct((HALF * PAIR // 128, 128), F32),
         ),
         12 * rows * PAIR * HALF,
         in_specs=[VMEM] * 3,
-        out_specs=[VMEM] * 3,
+        out_specs=[HBM, VMEM, VMEM],
+        scratch_shapes=[pltpu.VMEM((rows, HALF), F32), pltpu.SemaphoreType.DMA((rows // 512,))],
     )(in_vmem(x), q, in_vmem(left))
 
 
@@ -230,83 +235,89 @@
     fill(out_ref, cross, norm_ref[:8, :], norm_ref[8:, :])
 
 
-def project_kernel(parts_ref, high_ref, low_ref, norm_a_ref, norm_m_ref, out_ref):
+def project_kernel(parts_ref, move_ref, norm_a_ref, norm_m_ref, out_ref, held_ref, sem):
+    copy = pltpu.make_async_copy(move_ref, held_ref, sem)
+    copy.start()
     total = parts_ref[0:32, :]
     for k in range(1, SLABS):
         total = total + parts_ref[32 * k:32 * k + 32, :]
     wide = jnp.concatenate([total[8 * b:8 * b + 8] for b in range(4)], 1)
     wide = jnp.concatenate([wide, wide], 0)
-    cross = dot3(split(wide), (high_ref[...], low_ref[...]), NN)[:8]
+    copy.wait()
+    cross = dot3(split(wide), split(held_ref[...]), NN)[:8]
     fill(out_ref, cross, norm_a_ref[...], norm_m_ref[...])
 
 
-def payload(kernel, *arrays):
+def share(parts, norms):
     out = jax.ShapeDtypeStruct((SLABS * CHUNK, 128), F32)
-    return call(kernel, "payload", out, 10**7, in_specs=[VMEM] * len(arrays), out_specs=VMEM)(*arrays)
-
-
-def turn_kernel(
-    x_ref, q_ref, out_ref, norm_ref, high_ref, low_ref, a_high_ref, a_low_ref, held_ref, turn_ref, part_ref, sems
-):
-    pltpu.sync_copy(q_ref, turn_ref)
-    move, stay = split(turn_ref[:PAIR, :]), split(turn_ref[PAIR:, :])
-    high_ref[...], low_ref[...] = move
-    norm, outs = 0.0, []
-    for i, rows in enumerate(row_tiles(x_ref, 512)):
-        x = split(x_ref[rows, :])
-        out = dot3(x, move, NN)
-        held_ref[rows, :] = out
+    return call(share_kernel, "share", out, 10**7, in_specs=[VMEM] * 2, out_specs=VMEM)(parts, norms)
+
+
+def project(parts, move, norm_a, norm_m):
+    return call(
+        project_kernel,
+        "project",
+        jax.ShapeDtypeStruct((SLABS * CHUNK, 128), F32),
+        10**7,
+        in_specs=[VMEM, HBM, VMEM, VMEM],
+        out_specs=VMEM,
+        scratch_shapes=[pltpu.VMEM((PAIR, HALF), F32), pltpu.SemaphoreType.DMA],
+    )(parts, in_hbm(move), norm_a, norm_m)
+
+
+def turn_kernel(x_ref, q_ref, stay_ref, out_ref, norm_ref, held_ref, sems):
+    rows = x_ref.shape[0]
+    outs = [pltpu.make_async_copy(stay_ref, out_ref.at[pl.ds(rows, PAIR)], sems.at[rows // 512])]
+    outs[0].start()
+    q = split(q_ref[...])
+    norm = 0.0
+    for i, part in enumerate(row_tiles(x_ref, 512)):
+        out = dot3(split(x_ref[part, :]), q, NN)
+        held_ref[part, :] = out
         norm += squares(out)
-        part_ref[0, rows, :], part_ref[1, rows, :] = split(dot3(x, stay, NN))
-        goes = ((held_ref, out_ref), (part_ref.at[0], a_high_ref), (part_ref.at[1], a_low_ref))
-        for j, (here, there) in enumerate(goes):
-            outs.append(pltpu.make_async_copy(here.at[rows], there.at[rows], sems.at[i, j]))
-            outs[-1].start()
+        outs.append(pltpu.make_async_copy(held_ref.at[part], out_ref.at[part], sems.at[i]))
+        outs[-1].start()
     norm_ref[...] = norm
     for copy in outs:
         copy.wait()
 
 
-def turn(x, q):
+def turn(x, q, stay):
     rows = x.shape[0]
-    part = pltpu.HBM((rows, HALF), BF16)
     return call(
         turn_kernel,
         "turn",
         (
-            pltpu.HBM((rows, HALF), F32),
+            pltpu.HBM((rows + PAIR, HALF), F32),
             jax.ShapeDtypeStruct((8, HALF), F32),
-            jax.ShapeDtypeStruct((PAIR, HALF), BF16),
-            jax.ShapeDtypeStruct((PAIR, HALF), BF16),
-            part,
-            part,
         ),
-        30 * 10**9,
-        in_specs=[VMEM, HBM],
-        out_specs=[HBM] + [VMEM] * 3 + [HBM] * 2,
-        scratch_shapes=[
-            pltpu.VMEM((rows, HALF), F32),
-            pltpu.VMEM((2 * PAIR, HALF), F32),
-            pltpu.VMEM((2, rows, HALF), BF16),
-            pltpu.SemaphoreType.DMA((rows // 512, 3)),
-        ],
-    )(in_vmem(x), in_hbm(q))
-
-
-def ready_kernel(m_ref, high_ref, low_ref):
-    high_ref[...], low_ref[...] = split(m_ref[...])
-
-
-def ready(m):
-    out = jax.ShapeDtypeStruct(m.shape, BF16)
-    return call(
+        6 * rows * PAIR * HALF,
+        in_specs=[VMEM] * 3,
+        out_specs=[HBM, VMEM],
+        scratch_shapes=[pltpu.VMEM((rows, HALF), F32), pltpu.SemaphoreType.DMA((rows // 512 + 1,))],
+    )(in_vmem(x), q, in_vmem(stay))
+
+
+def ready_kernel(x_ref, m_ref, a_high_ref, a_low_ref, m_high_ref, m_low_ref):
+    q = split(m_ref[x_ref.shape[0]:, :])
+    for rows in row_tiles(x_ref, 512):
+        m_high_ref[rows, :], m_low_ref[rows, :] = split(m_ref[rows, :])
+        out = dot3(split(x_ref[rows, :]), q, NN)
+        a_high_ref[rows, :], a_low_ref[rows, :] = split(out)
+
+
+def ready(x, m):
+    rows = x.shape[0]
+    out = jax.ShapeDtypeStruct((rows, HALF), BF16)
+    parts = call(
         ready_kernel,
         "ready",
-        (out, out),
+        (out,) * 4,
         10**6,
-        in_specs=[VMEM],
-        out_specs=[VMEM] * 2,
-    )(in_vmem(m))
+        in_specs=[VMEM] * 2,
+        out_specs=[VMEM] * 4,
+    )(in_vmem(x), in_vmem(m))
+    return parts[:2], parts[2:]
 
 
 def right_a_kernel(high_ref, low_ref, q_ref, out_ref):
@@ -373,7 +384,7 @@
         in_specs=[VMEM] * 3,
         out_specs=HBM,
         scratch_shapes=[pltpu.VMEM((rows, HALF), F32), pltpu.SemaphoreType.DMA((rows // 512,))],
-    )(a, in_vmem(m), q)
+    )(in_vmem(a), in_vmem(m), q)
 
 
 def passed_along(value):
@@ -391,20 +402,20 @@
     cross, norms = first_inner(columns)
     movers, cross = lax.optimization_barrier((movers[:, 0], cross))
     parts = exchanged(cross, (16, 128))
-    packed = exchanged(payload(share_kernel, parts, norms), (CHUNK // 2, 2, 128))
-    both, stay = rotation(0, movers, packed, (2 * PAIR, PAIR))
-
-    left_both = passed_along(both)
+    packed = exchanged(share(parts, norms), (CHUNK // 2, 2, 128))
+    move, stay = rotation(0, movers, packed, (PAIR, PAIR))
+
+    left_move = passed_along(move)
     a, norm_a, cross = meet(columns, stay, left_columns)
-    parts = exchanged(cross, (32, 128))
-    m, norm_m, high, low, *left_a = turn(left_columns, left_both)
+    parts = exchanged(cross, (16, 2, 128))
+    m, norm_m = turn(left_columns, left_move, stay)
     left_m = passed_along(m)
-    packed = exchanged(payload(project_kernel, parts, high, low, norm_a, norm_m), (CHUNK // 2, 2, 128))
+    packed = exchanged(project(parts, left_move, norm_a, norm_m), (CHUNK // 2, 2, 128))
     move_a, move_m, stay = rotation(1, movers, packed, (HALF, HALF, PAIR))
 
+    left_move_m = passed_along(move_m)
     left_move_a = passed_along(move_a)
-    left_move_m = passed_along(move_m)
-    left_m = ready(left_m)
+    left_a, left_m = ready(left_columns, left_m)
     out = left(a, m, stay)
     left_a, left_m, out = lax.optimization_barrier((left_a, left_m, out))
     part = right_a(*left_a, left_move_a)

time: 124 us -> 125 us (level)
  waiting for transfers between devices: 6.98 us -> 12 us
  Pallas kernels: 38.8 us -> 36.7 us
  starting transfers between devices: 15.2 us -> 13.7 us
    all_to_all x1, waiting for transfers between devices: 3.08 us -> 12 us  [exchanged(): lax.all_to_all(packed.reshape(SLABS, *shape), 'slab', 0, 0)]
    ppermute x5, waiting for transfers between devices: 3.9 us -> 0.01 us  [passed_along(): lax.ppermute(value, 'blk', [(source, (source + 1) % count) for source in...]
    ppermute x5, starting transfers between devices: 11.4 us -> 9.8 us  [passed_along(): lax.ppermute(value, 'blk', [(source, (source + 1) % count) for source in...]
    pallas_call x5, Pallas kernels: 12.5 us -> 11.2 us  [the longest x1 4.64 us: meet(): call(meet_kernel, 'meet', (pltpu.HBM((rows, HALF), F32), jax.ShapeDtypeSt...]
    unnamed x16 -> x18, local copies, waits for them, and re-layouts: 4.43 us -> 4.43 us
  transfers between devices with their start and end apart: 6 -> 6, of which waited for: 3 -> 1; matrix products, arithmetic and copies ran while one was open for 0% -> 0% of each run, Pallas kernels for 30% -> 28%
where the time goes in v7:
time: 125 us; the launch traced here: 124 us
  blocking collectives  57 us (46%)
  Pallas kernels  36.7 us (29%)
  starting transfers between devices  13.7 us (11%)
  waiting for transfers between devices  12 us (10%)
  local copies, waits for them, and re-layouts  4.43 us (4%)
    all_to_all x3, blocking collectives, exchanged(): lax.all_to_all(packed.reshape(SLABS, *shape), 'slab', 0, 0)  57 us
    pallas_call x2, Pallas kernels, rotation(): call(lambda *refs: rotation_kernel(index, *refs), 'rotation', [jax.ShapeD...  18.5 us
    all_to_all x1, waiting for transfers between devices, exchanged(): lax.all_to_all(packed.reshape(SLABS, *shape), 'slab', 0, 0)  12 us
    ppermute x5, starting transfers between devices, passed_along(): lax.ppermute(value, 'blk', [(source, (source + 1) % count) for source in...  9.8 us
    pallas_call x1, Pallas kernels, meet(): call(meet_kernel, 'meet', (pltpu.HBM((rows, HALF), F32), jax.ShapeDtypeSt...  4.64 us
    unnamed x18, local copies, waits for them, and re-layouts  4.43 us
    all_to_all x1, starting transfers between devices, exchanged(): lax.all_to_all(packed.reshape(SLABS, *shape), 'slab', 0, 0)  3.9 us
    pallas_call x1, Pallas kernels, turn(): call(turn_kernel, 'turn', (pltpu.HBM((rows + PAIR, HALF), F32), jax.Shape...  2.9 us
  transfers between devices with their start and end apart: 6, of which 1 were waited for; matrix products, arithmetic and copies ran while one was open for 0% of the time, Pallas kernels for 28%

profile of v7, /device:TPU:1, one launch (start us, length us, event | category | flops | bytes accessed | tf_op | source)
XLA Modules:
  0.0 124.2 jit_solution(7137712721090476384)
XLA Ops:
  0.0 2.7 %collective-permute-start = (f32[2048,512]{1,0:T(8,128)}, f32[2048,512]{1,0:T(8,128)S(1)}, u32[]{:S(2)}, u32[]{:S(2)}) collective-permute-start(f32[2048,512]{1,0:T(8,128)} %x_ref.3), channel_id=1, source_target_pairs={{0,1},{1,2},{2,3},{3,4},{4,5},{5,6},{6,7},{7,0},{8,9},{9,10},{10,1... | collective-permute-start | bytes 12582920 | tf_op jit(solution)/shard_map/ppermute | solution.py:392
  2.7 0.0 copy-start
  2.7 2.2 %copy-done = f32[2048,512]{1,0:T(8,128)S(1)} copy-done((f32[2048,512]{1,0:T(8,128)S(1)}, f32[2048,512]{1,0:T(8,128)}, u32[]{:S(2)}) %copy-start) | copy-done | bytes 4194328
  4.9 0.0 copy-start.8
  4.9 1.1 first_inner.1
  6.0 23.5 %all_to_all.20 = f32[32,16,128]{2,1,0:T(8,128)S(1)} all-to-all(f32[32,16,128]{2,1,0:T(8,128)S(1)} %bitcast.15), channel_id=1, replica_groups=mesh['slab'=32,'blk'=8] {'slab'}, dimensions={0} | all-to-all | bytes 524288 | tf_op jit(solution)/shard_map/all_to_all | solution.py:396
  29.6 0.1 share.1
  29.6 16.6 %all_to_all.21 = f32[32,10,2,128]{3,2,1,0:T(2,128)S(1)} all-to-all(f32[32,10,2,128]{3,2,1,0:T(2,128)S(1)} %bitcast.10), channel_id=1, replica_groups=mesh['slab'=32,'blk'=8] {'slab'}, dimensions={0} | all-to-all | bytes 655360 | tf_op jit(solution)/shard_map/all_to_all | solution.py:396
  46.2 0.0 copy-done.8
  46.2 0.0 copy-start.1
  46.2 9.2 %rotation.2 = (f32[512,256]{1,0:T(8,128)S(1)}, f32[512,256]{1,0:T(8,128)S(1)}) custom-call(s32[2]{0:T(128)S(1)} %bitcast.16, f32[640,128]{1,0:T(8,128)S(1)} %bitcast.14), custom_call_target="tpu_custom_call" | custom-call | flops 10000000000 | bytes 4194304 | tf_op jit(solution)/shard_map/rotation/pallas_call | solution.py:143
  55.5 3.1 %collective-permute-start.1 = (f32[512,256]{1,0:T(8,128)S(1)}, f32[512,256]{1,0:T(8,128)S(1)}, u32[]{:S(2)}, u32[]{:S(2)}) collective-permute-start(f32[512,256]{1,0:T(8,128)S(1)} %get-tuple-element.32), channel_id=1, source_target_pairs={{0,1},{1,2},{2,3},{3,4},{4,5},{5,6},{6,7},{7,0},{8,9},{9,10},{10,1... | collective-permute-start | bytes 1572872 | tf_op jit(solution)/shard_map/ppermute | solution.py:392
  58.6 0.0 collective-permute-done.x_ref.left_ref
  58.6 0.0 copy-start.2
  58.6 0.0 copy-done.1
  58.6 4.6 %meet.1 = (f32[2048,256]{1,0:T(8,128)}, f32[8,256]{1,0:T(8,128)S(1)}, f32[1024,128]{1,0:T(8,128)}) custom-call(f32[2048,512]{1,0:T(8,128)S(1)} %copy-done.1, f32[512,256]{1,0:T(8,128)S(1)} %get-tuple-element.33.stay_ref.q_ref, f32[2048,512]{1,0:T(8,128)S(1)} %collective-permute-done.x_ref.left_ref), custom_call_target="tpu_custom_call" | custom-call | flops 3221225472 | bytes 4194304 | tf_op jit(solution)/shard_map/meet/pallas_call | solution.py:205
  63.2 0.0 copy-done.2
  63.3 3.9 %all-to-all-start.2 = ((f32[32,16,2,128]{3,2,1,0:T(2,128)}), f32[32,16,2,128]{3,2,1,0:T(2,128)S(1)}, u32[]{:S(2)}, u32[]{:S(2)}) async-start(f32[32,16,2,128]{3,2,1,0:T(2,128)} %bitcast.5), calls=%async_computation.2 | async-start | bytes 1048576 | tf_op jit(solution)/shard_map/all_to_all | solution.py:396
  67.2 0.0 collective-permute-done.1.q_ref.move_ref
  67.2 0.0 copy-start.3
  67.2 2.2 %copy-done.3 = f32[2048,512]{1,0:T(8,128)S(1)} copy-done((f32[2048,512]{1,0:T(8,128)S(1)}, f32[2048,512]{1,0:T(8,128)}, u32[]{:S(2)}) %copy-start.3) | copy-done | bytes 4194328
  69.4 0.0 copy-start.7
  69.4 2.9 %turn.1 = (f32[2560,256]{1,0:T(8,128)}, f32[8,256]{1,0:T(8,128)S(1)}) custom-call(f32[2048,512]{1,0:T(8,128)S(1)} %copy-done.3, f32[512,256]{1,0:T(8,128)S(1)} %collective-permute-done.1.q_ref.move_ref, f32[512,256]{1,0:T(8,128)S(1)} %get-tuple-element.33.stay_ref.q_ref), custom_call_target="tpu_custom_call" | custom-call | flops 1610612736 | bytes 4194304 | tf_op jit(solution)/shard_map/turn/pallas_call | solution.py:287
  72.3 0.0 copy-done.7
  72.3 0.1 collective-permute-start.2
  72.4 12.0 %all-to-all-done.2 = f32[32,16,2,128]{3,2,1,0:T(2,128)S(1)} async-done(((f32[32,16,2,128]{3,2,1,0:T(2,128)}), f32[32,16,2,128]{3,2,1,0:T(2,128)S(1)}, u32[]{:S(2)}, u32[]{:S(2)}) %all-to-all-start.2) | async-done | bytes 524320 | tf_op jit(solution)/shard_map/all_to_all | solution.py:396
  84.4 1.3 %project.1 = f32[640,128]{1,0:T(8,128)S(1)} custom-call(f32[1024,128]{1,0:T(8,128)S(1)} %bitcast.9, f32[512,256]{1,0:T(8,128)} %copy-done.7, f32[8,256]{1,0:T(8,128)S(1)} %get-tuple-element.41.norm_a_ref, f32[8,256]{1,0:T(8,128)S(1)} %get-tuple-element.42.norm_m_ref), custom_call_target="tpu_custom_call" | custom-call | flops 10000000 | bytes 4194304 | tf_op jit(solution)/shard_map/project/pallas_call | solution.py:257
  85.8 16.9 %all_to_all.22 = f32[32,10,2,128]{3,2,1,0:T(2,128)S(1)} all-to-all(f32[32,10,2,128]{3,2,1,0:T(2,128)S(1)} %bitcast.11), channel_id=1, replica_groups=mesh['slab'=32,'blk'=8] {'slab'}, dimensions={0} | all-to-all | bytes 655360 | tf_op jit(solution)/shard_map/all_to_all | solution.py:396
  102.6 0.0 copy-start.5
  102.6 0.0 copy-start.6
  102.6 9.3 %rotation.3 = (f32[256,256]{1,0:T(8,128)S(1)}, f32[256,256]{1,0:T(8,128)S(1)}, f32[512,256]{1,0:T(8,128)S(1)}) custom-call(s32[2]{0:T(128)S(1)} %bitcast.17, f32[640,128]{1,0:T(8,128)S(1)} %bitcast.13), custom_call_target="tpu_custom_call" | custom-call | flops 10000000000 | bytes 4194304 | tf_op jit(solution)/shard_map/rotation/pallas_call | solution.py:143
  111.9 3.8 %collective-permute-start.4 = (f32[256,256]{1,0:T(8,128)S(1)}, f32[256,256]{1,0:T(8,128)S(1)}, u32[]{:S(2)}, u32[]{:S(2)}) collective-permute-start(f32[256,256]{1,0:T(8,128)S(1)} %get-tuple-element.49), channel_id=1, source_target_pairs={{0,1},{1,2},{2,3},{3,4},{4,5},{5,6},{6,7},{7,0},{8,9},{9,10},{10,1... | collective-permute-start | bytes 786440 | tf_op jit(solution)/shard_map/ppermute | solution.py:392
  115.7 0.0 collective-permute-start.3
  115.7 0.0 copy-done.5
  115.7 0.0 copy-done.6
  115.7 0.0 copy-start.4
  115.7 2.9 %left.1.onto_ref = f32[2048,512]{1,0:T(8,128)} custom-call(f32[2048,256]{1,0:T(8,128)S(1)} %copy-done.6, f32[2560,256]{1,0:T(8,128)S(1)} %copy-done.5, f32[512,256]{1,0:T(8,128)S(1)} %get-tuple-element.43.q_ref), custom_call_target="tpu_custom_call" | custom-call | flops 1610612736 | bytes 4194304 | tf_op jit(solution)/shard_map/left/pallas_call | solution.py:379
  118.6 0.0 collective-permute-done.2.m_ref
  118.6 0.0 copy-done.4
  118.6 2.3 %ready.1 = (bf16[2048,256]{1,0:T(8,128)(2,1)S(1)}, bf16[2048,256]{1,0:T(8,128)(2,1)S(1)}, bf16[2048,256]{1,0:T(8,128)(2,1)S(1)}, bf16[2048,256]{1,0:T(8,128)(2,1)S(1)}) custom-call(f32[2048,512]{1,0:T(8,128)S(1)} %copy-done.4, f32[2560,256]{1,0:T(8,128)S(1)} %collective-permute-done.2.m_ref), custom_call_target="tpu_custom_call" | custom-call | flops 1000000 | bytes 4194304 | tf_op jit(solution)/shard_map/ready/pallas_call | solution.py:312
  120.9 0.0 collective-permute-done.4.q_ref
  121.0 1.0 right_a.1.part_ref
  121.9 0.0 collective-permute-done.3.q_ref
  122.0 2.1 %right.1 = f32[2048,512]{1,0:T(8,128)} custom-call(bf16[2048,256]{1,0:T(8,128)(2,1)S(1)} %get-tuple-element.44.high_ref, bf16[2048,256]{1,0:T(8,128)(2,1)S(1)} %get-tuple-element.45.low_ref, f32[256,256]{1,0:T(8,128)S(1)} %collective-permute-done.3.q_ref, f32[2048,256]{1,0:T(8,128)S(1)} %right_a.1.part_ref, ...), custom_call_target="tpu_custom_call", output_to_operand_aliasing={{}: (4, {})} | custom-call | flops 805306368 | bytes 4194304 | tf_op jit(solution)/shard_map/right/pallas_call | solution.py:354
Async XLA Ops:
  0.0 58.6 %collective-permute-start = (f32[2048,512]{1,0:T(8,128)}, f32[2048,512]{1,0:T(8,128)S(1)}, u32[]{:S(2)}, u32[]{:S(2)}) collective-permute-start(f32[2048,512]{1,0:T(8,128)} %x_ref.3), channel_id=1, source_target_pairs={{0,1},{1,2},{2,3},{3,4},{4,5},{5,6},{6,7},{7,0},{8,9},{9,10},{10,1... | collective-permute-start | bytes 12582920 | tf_op jit(solution)/shard_map/ppermute | solution.py:392
  2.7 2.2 %copy-start = (f32[2048,512]{1,0:T(8,128)S(1)}, f32[2048,512]{1,0:T(8,128)}, u32[]{:S(2)}) copy-start(f32[2048,512]{1,0:T(8,128)} %x_ref.3) | copy-start | bytes 12582916
  4.9 41.3 %copy-start.8 = (s32[2,1]{0,1:T(1,128)S(1)}, s32[2,1]{0,1:T(1,128)}, u32[]{:S(2)}) copy-start(s32[2,1]{0,1:T(1,128)} %param.3) | copy-start | bytes 28
  46.2 12.4 %copy-start.1 = (f32[2048,512]{1,0:T(8,128)S(1)}, f32[2048,512]{1,0:T(8,128)}, u32[]{:S(2)}) copy-start(f32[2048,512]{1,0:T(8,128)} %x_ref.3) | copy-start | bytes 12582916
  55.5 11.7 %collective-permute-start.1 = (f32[512,256]{1,0:T(8,128)S(1)}, f32[512,256]{1,0:T(8,128)S(1)}, u32[]{:S(2)}, u32[]{:S(2)}) collective-permute-start(f32[512,256]{1,0:T(8,128)S(1)} %get-tuple-element.32), channel_id=1, source_target_pairs={{0,1},{1,2},{2,3},{3,4},{4,5},{5,6},{6,7},{7,0},{8,9},{9,10},{10,1... | collective-permute-start | bytes 1572872 | tf_op jit(solution)/shard_map/ppermute | solution.py:392
  58.6 4.7 %copy-start.2 = (f32[2048,512]{1,0:T(8,128)}, f32[2048,512]{1,0:T(8,128)S(1)}, u32[]{:S(2)}) copy-start(f32[2048,512]{1,0:T(8,128)S(1)} %collective-permute-done.x_ref.left_ref) | copy-start | bytes 12582916
  63.3 21.2 %all-to-all-start.2 = ((f32[32,16,2,128]{3,2,1,0:T(2,128)}), f32[32,16,2,128]{3,2,1,0:T(2,128)S(1)}, u32[]{:S(2)}, u32[]{:S(2)}) async-start(f32[32,16,2,128]{3,2,1,0:T(2,128)} %bitcast.5), calls=%async_computation.2 | async-start | bytes 1048576 | tf_op jit(solution)/shard_map/all_to_all | solution.py:396
  67.2 2.2 %copy-start.3 = (f32[2048,512]{1,0:T(8,128)S(1)}, f32[2048,512]{1,0:T(8,128)}, u32[]{:S(2)}) copy-start(f32[2048,512]{1,0:T(8,128)} %copy-done.2) | copy-start | bytes 12582916
  69.4 2.9 %copy-start.7 = (f32[512,256]{1,0:T(8,128)}, f32[512,256]{1,0:T(8,128)S(1)}, u32[]{:S(2)}) copy-start(f32[512,256]{1,0:T(8,128)S(1)} %collective-permute-done.1.q_ref.move_ref) | copy-start | bytes 1572868
  72.3 46.3 %collective-permute-start.2 = (f32[2560,256]{1,0:T(8,128)}, f32[2560,256]{1,0:T(8,128)S(1)}, u32[]{:S(2)}, u32[]{:S(2)}) collective-permute-start(f32[2560,256]{1,0:T(8,128)} %get-tuple-element.34.m_ref), channel_id=1, source_target_pairs={{0,1},{1,2},{2,3},{3,4},{4,5},{5,6},{6,7},{7,0},{8,9},{9,10},{10,1... | collective-permute-start | bytes 7864328 | tf_op jit(solution)/shard_map/ppermute | solution.py:392
  102.6 13.1 %copy-start.5 = (f32[2560,256]{1,0:T(8,128)S(1)}, f32[2560,256]{1,0:T(8,128)}, u32[]{:S(2)}) copy-start(f32[2560,256]{1,0:T(8,128)} %get-tuple-element.34.m_ref) | copy-start | bytes 7864324
  102.6 13.1 %copy-start.6 = (f32[2048,256]{1,0:T(8,128)S(1)}, f32[2048,256]{1,0:T(8,128)}, u32[]{:S(2)}) copy-start(f32[2048,256]{1,0:T(8,128)} %get-tuple-element.39.a_ref) | copy-start | bytes 6291460
  111.9 9.1 %collective-permute-start.4 = (f32[256,256]{1,0:T(8,128)S(1)}, f32[256,256]{1,0:T(8,128)S(1)}, u32[]{:S(2)}, u32[]{:S(2)}) collective-permute-start(f32[256,256]{1,0:T(8,128)S(1)} %get-tuple-element.49), channel_id=1, source_target_pairs={{0,1},{1,2},{2,3},{3,4},{4,5},{5,6},{6,7},{7,0},{8,9},{9,10},{10,1... | collective-permute-start | bytes 786440 | tf_op jit(solution)/shard_map/ppermute | solution.py:392
  115.7 6.2 %collective-permute-start.3 = (f32[256,256]{1,0:T(8,128)S(1)}, f32[256,256]{1,0:T(8,128)S(1)}, u32[]{:S(2)}, u32[]{:S(2)}) collective-permute-start(f32[256,256]{1,0:T(8,128)S(1)} %get-tuple-element.46), channel_id=1, source_target_pairs={{0,1},{1,2},{2,3},{3,4},{4,5},{5,6},{6,7},{7,0},{8,9},{9,10},{10,1... | collective-permute-start | bytes 786440 | tf_op jit(solution)/shard_map/ppermute | solution.py:392
  115.7 2.9 %copy-start.4 = (f32[2048,512]{1,0:T(8,128)S(1)}, f32[2048,512]{1,0:T(8,128)}, u32[]{:S(2)}) copy-start(f32[2048,512]{1,0:T(8,128)} %copy-done.2) | copy-start | bytes 12582916

commit v8 on v5

--- a/solution.py
+++ b/solution.py
@@ -330,7 +330,7 @@
 def right_kernel(high_ref, low_ref, q_ref, part_ref, onto_ref, out_ref, held_ref, sems):
     q = split(q_ref[...])
     outs = []
-    for i, rows in enumerate(row_tiles(high_ref, 512)):
+    for i, rows in enumerate(row_tiles(high_ref, 256)):
         held_ref[rows, :] = part_ref[rows, :] + dot3((high_ref[rows, :], low_ref[rows, :]), q, NN)
         outs.append(pltpu.make_async_copy(held_ref.at[rows], out_ref.at[rows, pl.ds(HALF, HALF)], sems.at[i]))
         outs[-1].start()
@@ -347,7 +347,7 @@
         6 * rows * HALF * HALF,
         in_specs=[VMEM] * 4 + [HBM],
         out_specs=HBM,
-        scratch_shapes=[pltpu.VMEM((rows, HALF), F32), pltpu.SemaphoreType.DMA((rows // 512,))],
+        scratch_shapes=[pltpu.VMEM((rows, HALF), F32), pltpu.SemaphoreType.DMA((rows // 256,))],
         input_output_aliases={4: 0},
     )(high, low, q, part, onto)
 

time: 124 us -> 124 us (level)
  no operation moved by 1% of the time
where the time goes in v8:
time: 124 us; the launch traced here: 123 us
  blocking collectives  57.7 us (47%)
  Pallas kernels  38.6 us (31%)
  starting transfers between devices  15.3 us (12%)
  waiting for transfers between devices  7.05 us (6%)
  local copies, waits for them, and re-layouts  4.43 us (4%)
    all_to_all x3, blocking collectives, exchanged(): lax.all_to_all(packed.reshape(SLABS, *shape), 'slab', 0, 0)  57.7 us
    pallas_call x2, Pallas kernels, rotation(): call(lambda *refs: rotation_kernel(index, *refs), 'rotation', [jax.ShapeD...  19.2 us
    ppermute x5, starting transfers between devices, passed_along(): lax.ppermute(value, 'blk', [(source, (source + 1) % count) for source in...  11.4 us
    pallas_call x1, Pallas kernels, turn(): call(turn_kernel, 'turn', (pltpu.HBM((rows, HALF), F32), jax.ShapeDtypeSt...  5.73 us
    pallas_call x1, Pallas kernels, meet(): call(meet_kernel, 'meet', (jax.ShapeDtypeStruct((rows, HALF), F32), jax.S...  4.55 us
    unnamed x16, local copies, waits for them, and re-layouts  4.43 us
    all_to_all x1, starting transfers between devices, exchanged(): lax.all_to_all(packed.reshape(SLABS, *shape), 'slab', 0, 0)  3.89 us
    ppermute x5, waiting for transfers between devices, passed_along(): lax.ppermute(value, 'blk', [(source, (source + 1) % count) for source in...  3.89 us
  transfers between devices with their start and end apart: 6, of which 3 were waited for; matrix products, arithmetic and copies ran while one was open for 0% of the time, Pallas kernels for 30%

profile of v8, /device:TPU:1, one launch (start us, length us, event | category | flops | bytes accessed | tf_op | source)
XLA Modules:
  0.0 123.4 jit_solution(4062819552666468928)
XLA Ops:
  0.0 2.7 %collective-permute-start = (f32[2048,512]{1,0:T(8,128)}, f32[2048,512]{1,0:T(8,128)S(1)}, u32[]{:S(2)}, u32[]{:S(2)}) collective-permute-start(f32[2048,512]{1,0:T(8,128)} %x_ref.3), channel_id=1, source_target_pairs={{0,1},{1,2},{2,3},{3,4},{4,5},{5,6},{6,7},{7,0},{8,9},{9,10},{10,1... | collective-permute-start | bytes 12582920 | tf_op jit(solution)/shard_map/ppermute | solution.py:381
  2.7 0.0 copy-start
  2.7 2.2 %copy-done = f32[2048,512]{1,0:T(8,128)S(1)} copy-done((f32[2048,512]{1,0:T(8,128)S(1)}, f32[2048,512]{1,0:T(8,128)}, u32[]{:S(2)}) %copy-start) | copy-done | bytes 4194328
  4.9 0.0 copy-start.7
  4.9 1.1 first_inner.1
  6.0 23.5 %all_to_all.20 = f32[32,16,128]{2,1,0:T(8,128)S(1)} all-to-all(f32[32,16,128]{2,1,0:T(8,128)S(1)} %bitcast.15), channel_id=1, replica_groups=mesh['slab'=32,'blk'=8] {'slab'}, dimensions={0} | all-to-all | bytes 524288 | tf_op jit(solution)/shard_map/all_to_all | solution.py:385
  29.6 0.1 payload.2
  29.6 16.6 %all_to_all.21 = f32[32,10,2,128]{3,2,1,0:T(2,128)S(1)} all-to-all(f32[32,10,2,128]{3,2,1,0:T(2,128)S(1)} %bitcast.10), channel_id=1, replica_groups=mesh['slab'=32,'blk'=8] {'slab'}, dimensions={0} | all-to-all | bytes 655360 | tf_op jit(solution)/shard_map/all_to_all | solution.py:385
  46.2 0.0 copy-done.7
  46.2 0.0 copy-start.1
  46.2 10.2 %rotation.2 = (f32[1024,256]{1,0:T(8,128)}, f32[512,256]{1,0:T(8,128)S(1)}) custom-call(s32[2]{0:T(128)S(1)} %bitcast.16, f32[640,128]{1,0:T(8,128)S(1)} %bitcast.14), custom_call_target="tpu_custom_call" | custom-call | flops 10000000000 | bytes 4194304 | tf_op jit(solution)/shard_map/rotation/pallas_call | solution.py:143
  56.4 3.1 %collective-permute-start.1 = (f32[1024,256]{1,0:T(8,128)}, f32[1024,256]{1,0:T(8,128)}, u32[]{:S(2)}, u32[]{:S(2)}) collective-permute-start(f32[1024,256]{1,0:T(8,128)} %get-tuple-element.34), channel_id=1, source_target_pairs={{0,1},{1,2},{2,3},{3,4},{4,5},{5,6},{6,7},{7,0},{8,9},{9,10},{10,1... | collective-permute-start | bytes 3145736 | tf_op jit(solution)/shard_map/ppermute | solution.py:381
  59.5 0.0 collective-permute-done.x_ref.left_ref
  59.5 0.0 copy-start.5
  59.5 0.0 copy-done.1
  59.5 4.5 %meet.1 = (f32[2048,256]{1,0:T(8,128)S(1)}, f32[8,256]{1,0:T(8,128)S(1)}, f32[1024,128]{1,0:T(8,128)}) custom-call(f32[2048,512]{1,0:T(8,128)S(1)} %copy-done.1, f32[512,256]{1,0:T(8,128)S(1)} %get-tuple-element.40.q_ref, f32[2048,512]{1,0:T(8,128)S(1)} %collective-permute-done.x_ref.left_ref), custom_call_target="tpu_custom_call" | custom-call | flops 3221225472 | bytes 4194304 | tf_op jit(solution)/shard_map/meet/pallas_call | solution.py:201
  64.1 0.0 copy-done.5
  64.1 3.9 %all-to-all-start.2 = ((f32[32,32,128]{2,1,0:T(8,128)}), f32[32,32,128]{2,1,0:T(8,128)S(1)}, u32[]{:S(2)}, u32[]{:S(2)}) async-start(f32[32,32,128]{2,1,0:T(8,128)} %bitcast.5), calls=%async_computation.2 | async-start | bytes 1048576 | tf_op jit(solution)/shard_map/all_to_all | solution.py:385
  68.0 3.6 %collective-permute-done.1.q_ref = f32[1024,256]{1,0:T(8,128)} collective-permute-done((f32[1024,256]{1,0:T(8,128)}, f32[1024,256]{1,0:T(8,128)}, u32[]{:S(2)}, u32[]{:S(2)}) %collective-permute-start.1) | collective-permute-done | bytes 1048608 | tf_op jit(solution)/shard_map/ppermute | solution.py:381
  71.6 0.0 copy-start.6
  71.6 2.2 %copy-done.6 = f32[2048,512]{1,0:T(8,128)S(1)} copy-done((f32[2048,512]{1,0:T(8,128)S(1)}, f32[2048,512]{1,0:T(8,128)}, u32[]{:S(2)}) %copy-start.6) | copy-done | bytes 4194328
  73.8 5.7 %turn.1 = (f32[2048,256]{1,0:T(8,128)}, f32[8,256]{1,0:T(8,128)S(1)}, bf16[512,256]{1,0:T(8,128)(2,1)S(1)}, bf16[512,256]{1,0:T(8,128)(2,1)S(1)}, bf16[2048,256]{1,0:T(8,128)(2,1)}, /*index=5*/bf16[2048,256]{1,0:T(8,128)(2,1)}) custom-call(f32[2048,512]{1,0:T(8,128)S(1)} %copy-done.6, f32[1024,256]{1,0:T(8,128)} %collective-permute-done.1.q_ref), custom_call_target="tpu_custom_call" | custom-call | flops 30000001024 | bytes 4194304 | tf_op jit(solution)/shard_map/turn/pallas_call | solution.py:273
  79.5 2.5 %collective-permute-start.2 = (f32[2048,256]{1,0:T(8,128)}, f32[2048,256]{1,0:T(8,128)}, u32[]{:S(2)}, u32[]{:S(2)}) collective-permute-start(f32[2048,256]{1,0:T(8,128)} %get-tuple-element.37.m_ref), channel_id=1, source_target_pairs={{0,1},{1,2},{2,3},{3,4},{4,5},{5,6},{6,7},{7,0},{8,9},{9,10},{10,1... | collective-permute-start | bytes 6291464 | tf_op jit(solution)/shard_map/ppermute | solution.py:381
  82.0 3.2 %all-to-all-done.2 = f32[32,32,128]{2,1,0:T(8,128)S(1)} async-done(((f32[32,32,128]{2,1,0:T(8,128)}), f32[32,32,128]{2,1,0:T(8,128)S(1)}, u32[]{:S(2)}, u32[]{:S(2)}) %all-to-all-start.2) | async-done | bytes 524320 | tf_op jit(solution)/shard_map/all_to_all | solution.py:385
  85.2 0.3 payload.3
  85.5 17.6 %all_to_all.22 = f32[32,10,2,128]{3,2,1,0:T(2,128)S(1)} all-to-all(f32[32,10,2,128]{3,2,1,0:T(2,128)S(1)} %bitcast.11), channel_id=1, replica_groups=mesh['slab'=32,'blk'=8] {'slab'}, dimensions={0} | all-to-all | bytes 655360 | tf_op jit(solution)/shard_map/all_to_all | solution.py:385
  103.1 0.0 copy-start.2
  103.1 9.0 %rotation.3 = (f32[256,256]{1,0:T(8,128)S(1)}, f32[256,256]{1,0:T(8,128)S(1)}, f32[512,256]{1,0:T(8,128)S(1)}) custom-call(s32[2]{0:T(128)S(1)} %bitcast.17, f32[640,128]{1,0:T(8,128)S(1)} %bitcast.13), custom_call_target="tpu_custom_call" | custom-call | flops 10000000000 | bytes 4194304 | tf_op jit(solution)/shard_map/rotation/pallas_call | solution.py:143
  112.1 3.1 %collective-permute-start.4 = (f32[256,256]{1,0:T(8,128)S(1)}, f32[256,256]{1,0:T(8,128)S(1)}, u32[]{:S(2)}, u32[]{:S(2)}) collective-permute-start(f32[256,256]{1,0:T(8,128)S(1)} %get-tuple-element.53), channel_id=1, source_target_pairs={{0,1},{1,2},{2,3},{3,4},{4,5},{5,6},{6,7},{7,0},{8,9},{9,10},{10,1... | collective-permute-start | bytes 786440 | tf_op jit(solution)/shard_map/ppermute | solution.py:381
  115.2 0.0 collective-permute-start.3
  115.2 0.0 copy-done.2
  115.2 0.0 copy-start.3
  115.2 0.0 copy-start.4
  115.2 2.9 %left.1.onto_ref = f32[2048,512]{1,0:T(8,128)} custom-call(f32[2048,256]{1,0:T(8,128)S(1)} %get-tuple-element.41.a_ref, f32[2048,256]{1,0:T(8,128)S(1)} %copy-done.2, f32[512,256]{1,0:T(8,128)S(1)} %get-tuple-element.47.q_ref), custom_call_target="tpu_custom_call" | custom-call | flops 1610612736 | bytes 4194304 | tf_op jit(solution)/shard_map/left/pallas_call | solution.py:368
  118.1 0.0 collective-permute-done.2.m_ref
  118.1 1.9 %ready.1 = (bf16[2048,256]{1,0:T(8,128)(2,1)S(1)}, bf16[2048,256]{1,0:T(8,128)(2,1)S(1)}) custom-call(f32[2048,256]{1,0:T(8,128)} %collective-permute-done.2.m_ref), custom_call_target="tpu_custom_call" | custom-call | flops 1000000 | bytes 4194304 | tf_op jit(solution)/shard_map/ready/pallas_call | solution.py:302
  120.0 0.0 collective-permute-done.4.q_ref
  120.0 0.0 copy-done.3
  120.0 0.0 copy-done.4
  120.1 1.0 right_a.1.part_ref
  121.0 0.3 collective-permute-done.3.q_ref
  121.3 1.9 %right.1 = f32[2048,512]{1,0:T(8,128)} custom-call(bf16[2048,256]{1,0:T(8,128)(2,1)S(1)} %get-tuple-element.48.high_ref, bf16[2048,256]{1,0:T(8,128)(2,1)S(1)} %get-tuple-element.49.low_ref, f32[256,256]{1,0:T(8,128)S(1)} %collective-permute-done.3.q_ref, f32[2048,256]{1,0:T(8,128)S(1)} %right_a.1.part_ref, ...), custom_call_target="tpu_custom_call", output_to_operand_aliasing={{}: (4, {})} | custom-call | flops 805306368 | bytes 4194304 | tf_op jit(solution)/shard_map/right/pallas_call | solution.py:343
Async XLA Ops:
  0.0 59.5 %collective-permute-start = (f32[2048,512]{1,0:T(8,128)}, f32[2048,512]{1,0:T(8,128)S(1)}, u32[]{:S(2)}, u32[]{:S(2)}) collective-permute-start(f32[2048,512]{1,0:T(8,128)} %x_ref.3), channel_id=1, source_target_pairs={{0,1},{1,2},{2,3},{3,4},{4,5},{5,6},{6,7},{7,0},{8,9},{9,10},{10,1... | collective-permute-start | bytes 12582920 | tf_op jit(solution)/shard_map/ppermute | solution.py:381
  2.7 2.2 %copy-start = (f32[2048,512]{1,0:T(8,128)S(1)}, f32[2048,512]{1,0:T(8,128)}, u32[]{:S(2)}) copy-start(f32[2048,512]{1,0:T(8,128)} %x_ref.3) | copy-start | bytes 12582916
  4.9 41.3 %copy-start.7 = (s32[2,1]{0,1:T(1,128)S(1)}, s32[2,1]{0,1:T(1,128)}, u32[]{:S(2)}) copy-start(s32[2,1]{0,1:T(1,128)} %param.3) | copy-start | bytes 28
  46.2 13.3 %copy-start.1 = (f32[2048,512]{1,0:T(8,128)S(1)}, f32[2048,512]{1,0:T(8,128)}, u32[]{:S(2)}) copy-start(f32[2048,512]{1,0:T(8,128)} %x_ref.3) | copy-start | bytes 12582916
  56.4 15.2 %collective-permute-start.1 = (f32[1024,256]{1,0:T(8,128)}, f32[1024,256]{1,0:T(8,128)}, u32[]{:S(2)}, u32[]{:S(2)}) collective-permute-start(f32[1024,256]{1,0:T(8,128)} %get-tuple-element.34), channel_id=1, source_target_pairs={{0,1},{1,2},{2,3},{3,4},{4,5},{5,6},{6,7},{7,0},{8,9},{9,10},{10,1... | collective-permute-start | bytes 3145736 | tf_op jit(solution)/shard_map/ppermute | solution.py:381
  59.5 4.6 %copy-start.5 = (f32[2048,512]{1,0:T(8,128)}, f32[2048,512]{1,0:T(8,128)S(1)}, u32[]{:S(2)}) copy-start(f32[2048,512]{1,0:T(8,128)S(1)} %collective-permute-done.x_ref.left_ref) | copy-start | bytes 12582916
  64.1 21.1 %all-to-all-start.2 = ((f32[32,32,128]{2,1,0:T(8,128)}), f32[32,32,128]{2,1,0:T(8,128)S(1)}, u32[]{:S(2)}, u32[]{:S(2)}) async-start(f32[32,32,128]{2,1,0:T(8,128)} %bitcast.5), calls=%async_computation.2 | async-start | bytes 1048576 | tf_op jit(solution)/shard_map/all_to_all | solution.py:385
  71.6 2.2 %copy-start.6 = (f32[2048,512]{1,0:T(8,128)S(1)}, f32[2048,512]{1,0:T(8,128)}, u32[]{:S(2)}) copy-start(f32[2048,512]{1,0:T(8,128)} %copy-done.5) | copy-start | bytes 12582916
  79.5 38.6 %collective-permute-start.2 = (f32[2048,256]{1,0:T(8,128)}, f32[2048,256]{1,0:T(8,128)}, u32[]{:S(2)}, u32[]{:S(2)}) collective-permute-start(f32[2048,256]{1,0:T(8,128)} %get-tuple-element.37.m_ref), channel_id=1, source_target_pairs={{0,1},{1,2},{2,3},{3,4},{4,5},{5,6},{6,7},{7,0},{8,9},{9,10},{10,1... | collective-permute-start | bytes 6291464 | tf_op jit(solution)/shard_map/ppermute | solution.py:381
  103.1 12.2 %copy-start.2 = (f32[2048,256]{1,0:T(8,128)S(1)}, f32[2048,256]{1,0:T(8,128)}, u32[]{:S(2)}) copy-start(f32[2048,256]{1,0:T(8,128)} %get-tuple-element.37.m_ref) | copy-start | bytes 6291460
  112.1 7.9 %collective-permute-start.4 = (f32[256,256]{1,0:T(8,128)S(1)}, f32[256,256]{1,0:T(8,128)S(1)}, u32[]{:S(2)}, u32[]{:S(2)}) collective-permute-start(f32[256,256]{1,0:T(8,128)S(1)} %get-tuple-element.53), channel_id=1, source_target_pairs={{0,1},{1,2},{2,3},{3,4},{4,5},{5,6},{6,7},{7,0},{8,9},{9,10},{10,1... | collective-permute-start | bytes 786440 | tf_op jit(solution)/shard_map/ppermute | solution.py:381
  115.2 6.1 %collective-permute-start.3 = (f32[256,256]{1,0:T(8,128)S(1)}, f32[256,256]{1,0:T(8,128)S(1)}, u32[]{:S(2)}, u32[]{:S(2)}) collective-permute-start(f32[256,256]{1,0:T(8,128)S(1)} %get-tuple-element.50), channel_id=1, source_target_pairs={{0,1},{1,2},{2,3},{3,4},{4,5},{5,6},{6,7},{7,0},{8,9},{9,10},{10,1... | collective-permute-start | bytes 786440 | tf_op jit(solution)/shard_map/ppermute | solution.py:381
  115.2 4.8 %copy-start.3 = (bf16[2048,256]{1,0:T(8,128)(2,1)S(1)}, bf16[2048,256]{1,0:T(8,128)(2,1)}, u32[]{:S(2)}) copy-start(bf16[2048,256]{1,0:T(8,128)(2,1)} %get-tuple-element.51.high_ref) | copy-start | bytes 3145732
  115.2 4.8 %copy-start.4 = (bf16[2048,256]{1,0:T(8,128)(2,1)S(1)}, bf16[2048,256]{1,0:T(8,128)(2,1)}, u32[]{:S(2)}) copy-start(bf16[2048,256]{1,0:T(8,128)(2,1)} %get-tuple-element.52.low_ref) | copy-start | bytes 3145732
